TPU v7x, 512 devices: a whole 4x4x16 slice. The times are simulated.
512 devices in a mesh: gx: 64 (over z_hi, x, y), gy: 8 (over z_lo, core).
Axes of the slice: x: 4, y: 4, z: 16 (z_hi: 4, z_lo: 4; z = z_hi * 4 + z_lo), core: 2. Of those that a mesh axis runs over, the one named last changes fastest.
Arguments:
- velocity: float32 [3, 256, 128, 128], P(None, 'gx', 'gy'), may hold values from -6 to 6
- canopy: int32 [256, 128, 128], P('gx', 'gy'), may hold values 0 or 1
- weight_in: bfloat16 [648, 512], replicated, may hold values from -0.25 to 0.25
- bias_in: float32 [512], replicated, may hold values from -6 to 6
- weight_out: bfloat16 [512, 384], replicated, may hold values from -0.25 to 0.25
- bias_out: float32 [384], replicated, may hold values from -6 to 6
- cotangent: bfloat16 [3, 256, 128, 128], P(None, 'gx', 'gy'), may hold values from -24 to 24
Outputs:
- new_velocity: float32 [3, 256, 128, 128], P(None, 'gx', 'gy')
- velocity_grad: float32 [3, 256, 128, 128], P(None, 'gx', 'gy')
- weight_in_grad: float32 [648, 512], replicated
- bias_in_grad: float32 [512], replicated
- weight_out_grad: float32 [512, 384], replicated
- bias_out_grad: float32 [384], replicated
Inputs may be any that keep to these rules, and one draw needn't show every extreme that they name: canopy holds only 0 and 1.
All inputs are finite; a program needn't handle non-finite values. No bound on the sum of `canopy` on one device may be relied on, other than what follows from the above.
Results may differ from a plain program's by a relative error of at most 0.0056.
Values sent between devices are 32-bit elements; how exact they have to be, the bound alone decides.
No kernel may reach another device: no remote copies, remote signals or barrier semaphores. Data moves between devices by JAX's collectives and lax.ppermute only.
A program may use at most 128 MiB of HBM per device.

v0:
```python
import jax
import jax.numpy as jnp
from jax import lax
from jax.sharding import PartitionSpec as P

time_step = 0.25
viscosity = 0.2
penalty_eta = 0.05


def extended(block, sides, width):
    for axis, dim in sides:
        count = lax.axis_size(axis)
        forward = [(i, i + 1) for i in range(count - 1)]
        forward.append((count - 1, 0))
        backward = [(target, source) for source, target in forward]
        low = lax.ppermute(
            lax.slice_in_dim(block, block.shape[dim] - width, None, axis=dim), axis, forward
        )
        high = lax.ppermute(lax.slice_in_dim(block, 0, width, axis=dim), axis, backward)
        block = jnp.concatenate([low, block, high], axis=dim)
    return block


def pad_depth(field):
    return jnp.pad(field, ((0, 0), (0, 0), (0, 0), (1, 1)))


def centred(padded, axis):
    if axis == 1:
        return (padded[:, 2:, 1:-1, 1:-1] - padded[:, :-2, 1:-1, 1:-1]) * 0.5
    if axis == 2:
        return (padded[:, 1:-1, 2:, 1:-1] - padded[:, 1:-1, :-2, 1:-1]) * 0.5
    return (padded[:, 1:-1, 1:-1, 2:] - padded[:, 1:-1, 1:-1, :-2]) * 0.5


def laplace(padded):
    middle = padded[:, 1:-1, 1:-1, 1:-1]
    total = padded[:, 2:, 1:-1, 1:-1] + padded[:, :-2, 1:-1, 1:-1]
    total = total + padded[:, 1:-1, 2:, 1:-1] + padded[:, 1:-1, :-2, 1:-1]
    total = total + padded[:, 1:-1, 1:-1, 2:] + padded[:, 1:-1, 1:-1, :-2]
    return total - 6.0 * middle


def advect(padded):
    first = centred(padded[0:1] * padded, 1)
    second = centred(padded[1:2] * padded, 2)
    third = centred(padded[2:3] * padded, 3)
    return first + second + third


def divergence(along_x, along_y, along_z):
    part_x = (along_x[:, 2:] - along_x[:, :-2]) * 0.5
    part_y = (along_y[:, :, 2:] - along_y[:, :, :-2]) * 0.5
    part_z = (along_z[:, :, :, 2:] - along_z[:, :, :, :-2]) * 0.5
    return part_x + part_y + part_z


def select(stack_in, indices):
    return jnp.stack([stack_in[entry] for entry in indices])


def to_blocks(padded):
    count_x = (padded.shape[1] - 2) // 4
    count_y = (padded.shape[2] - 2) // 4
    count_z = (padded.shape[3] - 2) // 4
    stacked = jnp.stack(
        [padded[:, offset : offset + 4 * count_x : 4] for offset in range(6)], axis=1
    )
    stacked = jnp.stack(
        [stacked[:, :, :, offset : offset + 4 * count_y : 4] for offset in range(6)], axis=3
    )
    stacked = jnp.stack(
        [stacked[..., offset : offset + 4 * count_z : 4] for offset in range(6)], axis=5
    )
    stacked = stacked.transpose(0, 1, 3, 5, 2, 4, 6)
    return stacked.reshape(stacked.shape[0] * 216, -1)


def from_rows(outputs, count_x, count_y, count_z):
    shaped = outputs.reshape(6, 4, 4, 4, count_x, count_y, count_z).transpose(0, 4, 1, 5, 2, 6, 3)
    return shaped.reshape(6, 4 * count_x, 4 * count_y, 4 * count_z)


def to_rows(stress_grad):
    count_x = stress_grad.shape[1] // 4
    count_y = stress_grad.shape[2] // 4
    count_z = stress_grad.shape[3] // 4
    shaped = stress_grad.reshape(6, count_x, 4, count_y, 4, count_z, 4).transpose(
        0, 2, 4, 6, 1, 3, 5
    )
    return shaped.reshape(384, count_x * count_y * count_z)


def fold_last(stacked):
    count = stacked.shape[-1]
    leading = stacked.shape[:-2]
    main = jnp.stack([stacked[..., offset, :] for offset in range(4)], axis=-1).reshape(
        leading + (4 * count,)
    )
    blank = jnp.zeros_like(stacked[..., 0, :])
    extra = jnp.stack([stacked[..., 4, :], stacked[..., 5, :], blank, blank], axis=-1).reshape(
        leading + (4 * count,)
    )
    main = jnp.concatenate([main, jnp.zeros(leading + (2,), main.dtype)], axis=-1)
    extra = jnp.concatenate(
        [jnp.zeros(leading + (4,), extra.dtype), extra[..., : 4 * count - 2]], axis=-1
    )
    return main + extra


def fold_depth_side(column_grad, count_x, count_y, count_z):
    shaped = column_grad.reshape(3, 6, 6, 6, count_x, count_y, count_z).transpose(
        0, 1, 4, 2, 5, 3, 6
    )
    shaped = fold_last(shaped)
    shaped = jnp.moveaxis(shaped, (3, 4), (4, 5))
    return fold_last(shaped)


def fold_across(shaped):
    moved = jnp.moveaxis(shaped, (1, 2), (3, 4))
    return fold_last(moved).transpose(0, 3, 2, 1)


def closure(columns, stress_rows, weight_in, bias_in, weight_out, bias_out):
    pre_act = (
        lax.dot_general(
            weight_in, columns, (((0,), (0,)), ((), ())), preferred_element_type=jnp.float32
        )
        + bias_in[:, None]
    )
    hidden = jax.nn.silu(pre_act).astype(jnp.bfloat16)
    outputs = (
        lax.dot_general(
            weight_out, hidden, (((0,), (0,)), ((), ())), preferred_element_type=jnp.float32
        )
        + bias_out[:, None]
    )
    bias_out_sum = jnp.sum(stress_rows, axis=1)
    rows_low = stress_rows.astype(jnp.bfloat16)
    weight_out_sum = lax.dot_general(
        hidden, rows_low, (((1,), (1,)), ((), ())), preferred_element_type=jnp.float32
    )
    hidden_grad = lax.dot_general(
        weight_out, rows_low, (((1,), (0,)), ((), ())), preferred_element_type=jnp.float32
    )
    sigmoid_pre = jax.nn.sigmoid(pre_act)
    pre_grad = hidden_grad * (sigmoid_pre * (1.0 + pre_act * (1.0 - sigmoid_pre)))
    bias_in_sum = jnp.sum(pre_grad, axis=1)
    pre_low = pre_grad.astype(jnp.bfloat16)
    weight_in_sum = lax.dot_general(
        columns, pre_low, (((1,), (1,)), ((), ())), preferred_element_type=jnp.float32
    )
    column_grad = lax.dot_general(
        weight_in, pre_low, (((1,), (0,)), ((), ())), preferred_element_type=jnp.float32
    )
    return (outputs, column_grad, weight_in_sum, bias_in_sum, weight_out_sum, bias_out_sum)


def stress_from_slopes(grad_x, grad_y, grad_z):
    return -jnp.stack(
        [
            grad_x[0],
            grad_y[1],
            grad_z[2],
            grad_y[0] + grad_x[1],
            grad_z[0] + grad_x[2],
            grad_z[1] + grad_y[2],
        ]
    )


def on_device(velocity, canopy, weight_in, bias_in, weight_out, bias_out, cotangent):
    count_x = velocity.shape[1] // 4
    count_y = velocity.shape[2] // 4
    count_z = velocity.shape[3] // 4
    rimmed = extended(velocity, (("gx", 1), ("gy", 2)), 1)
    padded = pad_depth(rimmed)
    factor = 1.0 + time_step * canopy.astype(jnp.float32) / penalty_eta
    incoming = cotangent.astype(jnp.float32)
    direct = incoming / factor
    adjoint = time_step * direct
    adj_pad = pad_depth(extended(adjoint, (("gx", 1), ("gy", 2)), 1))
    grad_x = centred(adj_pad, 1)
    grad_y = centred(adj_pad, 2)
    grad_z = centred(adj_pad, 3)
    stress_grad = stress_from_slopes(grad_x, grad_y, grad_z)
    columns = to_blocks(padded).astype(jnp.bfloat16)
    outputs, column_grad, w_in_s, b_in_s, w_out_s, b_out_s = closure(
        columns, to_rows(stress_grad), weight_in, bias_in, weight_out, bias_out
    )
    stress = from_rows(outputs, count_x, count_y, count_z)
    stress_pad = pad_depth(extended(stress, (("gx", 1), ("gy", 2)), 1))
    along_x = select(stress_pad, (0, 3, 4))[:, :, 1:-1, 1:-1]
    along_y = select(stress_pad, (3, 1, 5))[:, 1:-1, :, 1:-1]
    along_z = pad_depth(select(stress, (4, 5, 2)))
    force = divergence(along_x, along_y, along_z)
    rhs = -advect(padded) + viscosity * laplace(padded) + force
    new_velocity = (velocity + time_step * rhs) / factor
    transport_a = jnp.stack(
        [
            jnp.sum(grad_x * velocity, axis=0),
            jnp.sum(grad_y * velocity, axis=0),
            jnp.sum(grad_z * velocity, axis=0),
        ]
    )
    transport_b = grad_x * velocity[0:1] + grad_y * velocity[1:2] + grad_z * velocity[2:3]
    stencil_grad = direct + transport_a + transport_b + viscosity * laplace(adj_pad)
    ghost = fold_across(fold_depth_side(column_grad, count_x, count_y, count_z))[..., 1:-1]
    widened = extended(ghost, (("gx", 1), ("gy", 2)), 1)
    middle = widened[:, 2:-2]
    middle = middle.at[:, 0].add(widened[:, 0]).at[:, -1].add(widened[:, -1])
    folded = middle[:, :, 2:-2]
    folded = folded.at[:, :, 0].add(middle[:, :, 0]).at[:, :, -1].add(middle[:, :, -1])
    velocity_grad = stencil_grad + folded
    totals = lax.psum((w_in_s, b_in_s, w_out_s, b_out_s), ("gx", "gy"))
    blocks_total = columns.shape[1] * lax.axis_size("gx") * lax.axis_size("gy")
    scale = float(blocks_total) ** (-0.5)
    weight_in_grad = totals[0] * scale
    bias_in_grad = totals[1] * scale
    weight_out_grad = totals[2] * scale
    bias_out_grad = totals[3] * scale
    return (
        new_velocity,
        velocity_grad,
        weight_in_grad,
        bias_in_grad,
        weight_out_grad,
        bias_out_grad,
    )


def solution(mesh):
    placed = (
        P(None, "gx", "gy", None),
        P("gx", "gy", None),
        P(),
        P(),
        P(),
        P(),
        P(None, "gx", "gy", None),
    )
    return jax.shard_map(
        on_device,
        mesh=mesh,
        in_specs=placed,
        out_specs=(P(None, "gx", "gy", None), P(None, "gx", "gy", None), P(), P(), P(), P()),
        check_vma=False,
    )
```

profile of v0, /device:TPU:1, one launch (start us, length us, event | category | flops | bytes accessed | tf_op | source)
XLA Modules:
  0.0 782.5 jit_solution(17877821020374605648)
XLA Ops:
  8.9 17.9 %collective-permute-start.8 = (f32[3,1,16,128]{3,2,1,0:T(8,128)S(1)}, f32[3,1,16,128]{3,2,1,0:T(8,128)S(1)}, u32[]{:S(2)}, u32[]{:S(2)}) collective-permute-start(f32[3,1,16,128]{3,2,1,0:T(8,128)S(1)} %get-tuple-element.118), channel_id=1, source_target_pairs={{8,0},{16,8},{24,16},{32,24},{40,32},{48,40},{56,48},{64,56},{72,6... | collective-permute-start | bytes 73736 | tf_op jit(solution)/shard_map/ppermute | solution.py:20
  26.8 1.9 collective-permute-start.9
  29.5 1.9 collective-permute-start
  31.4 11.5 %collective-permute-start.1 = (f32[3,1,16,128]{3,2,1,0:T(8,128)S(1)}, f32[3,1,16,128]{3,2,1,0:T(8,128)S(1)}, u32[]{:S(2)}, u32[]{:S(2)}) collective-permute-start(f32[3,1,16,128]{3,2,1,0:T(8,128)S(1)} %get-tuple-element.119), channel_id=1, source_target_pairs={{8,0},{16,8},{24,16},{32,24},{40,32},{48,40},{56,48},{64,56},{72,6... | collective-permute-start | bytes 73736 | tf_op jit(solution)/shard_map/ppermute | solution.py:20
  42.9 1.4 multiply_bitcast_fusion.2
  44.5 3.4 collective-permute-start.10
  47.9 2.5 collective-permute-start.11
  51.5 1.6 multiply_reduce_fusion.2
  53.8 5.9 collective-permute-start.3
  59.7 1.9 collective-permute-start.2
  63.9 1.8 stack.166
  66.1 1.8 stack.167
  68.5 1.8 stack.168
  71.4 1.8 stack.169
  84.0 4.7 slice.531
  88.7 4.7 slice.532
  93.4 4.7 slice.533
  98.1 4.7 slice.534
  102.8 4.7 slice.535
  107.5 4.7 slice.536
  116.8 4.4 copy.159
  122.0 1.9 fusion.53
  124.2 1.4 fusion.36
  125.6 2.2 fusion.42
  129.5 6.5 reshape.272
  136.7 1.9 collective-permute-start.4
  138.6 11.5 %collective-permute-start.5 = (f32[6,1,16,128]{3,2,1,0:T(8,128)}, f32[6,1,16,128]{3,2,1,0:T(8,128)}, u32[]{:S(2)}, u32[]{:S(2)}) collective-permute-start(f32[6,1,16,128]{3,2,1,0:T(8,128)} %get-tuple-element.98), channel_id=1, source_target_pairs={{8,0},{16,8},{24,16},{32,24},{40,32},{48,40},{56,48},{64,56},{72,6... | collective-permute-start | bytes 147464 | tf_op jit(solution)/shard_map/ppermute | solution.py:20
  151.0 4.9 copy.173
  155.9 4.7 copy.172
  160.7 10.0 %maximum_maximum_fusion = f32[3,6,1,6,4,32,4]{6,5,4,3,1,0,2:T(8,128)} fusion(f32[3,6,1,6,4,32,1]{6,5,4,3,1,0,2:T(8,128)} %copy.173, f32[3,6,1,6,4,32,1]{6,5,4,3,1,0,2:T(8,128)} %copy.172, f32[4]{0:T(128)S(1)} %pad.57.clone), kind=kLoop, calls=%fused_computation | loop fusion | flops 110592 | bytes 331792 | tf_op jit(solution)/shard_map/stack | solution.py:102
  170.6 7.0 reshape.275
  177.9 4.7 copy.171
  182.6 7.0 reshape.274
  191.9 1.9 collective-permute-start.13
  193.8 3.4 collective-permute-start.12
  197.2 104.9 %all-reduce.10 = (f32[512]{0:T(512)S(1)}, f32[384]{0:T(512)S(1)}) all-reduce(f32[512]{0:T(512)S(1)} %copy-done.21, f32[384]{0:T(512)S(1)} %reduce_sum.52), channel_id=1, replica_groups=mesh['gx'=64,'gy'=8] {'gx','gy'}, use_global_device_ids=true, to_apply=%region_5.6 | all-reduce | flops 896 | bytes 7168 | tf_op jit(solution)/shard_map/psum | solution.py:217
  303.3 2.1 broadcast_multiply_fusion.4
  305.5 1.4 copy.162
  308.1 1.4 copy.160
  310.8 2.9 collective-permute-start.15
  313.7 2.6 collective-permute-start.14
  319.3 5.2 collective-permute-start.7
  324.5 1.9 collective-permute-start.6
  326.5 1.7 fusion.27
  328.7 2.5 fusion.11
  331.2 439.9 %all-reduce.14.cloned.1.call-done = (f32[648,512]{1,0:T(8,128)}, f32[512,384]{1,0:T(8,128)}) async-done(((f32[648,512]{1,0:T(8,128)}, f32[512,384]{1,0:T(8,128)}), (f32[648,512]{1,0:T(8,128)}, f32[512,384]{1,0:T(8,128)})) %all-reduce.14.cloned.1.call-update) | async-done | bytes 2113552 | tf_op jit(solution)/shard_map/psum | solution.py:217
  771.1 2.5 broadcast_multiply_fusion
  773.6 2.1 broadcast_multiply_fusion.1
  (172 shorter events, 37.3 us)
Async XLA Ops:
  7.2 106.0 %copy-start = (bf16[648,512]{1,0:T(8,128)(2,1)S(1)}, bf16[648,512]{1,0:T(8,128)(2,1)}, u32[]{:S(2)}) copy-start(bf16[648,512]{1,0:T(8,128)(2,1)} %param.17) | copy-start | bytes 1990660
  7.2 763.9 %all-reduce.14.cloned.1.call-start = ((), (), s32[]{:S(2)}) async-start(), calls=%async_computation | async-start | bytes 4227072 | tf_op jit(solution)/shard_map/psum | solution.py:217
  8.9 35.6 %collective-permute-start.8 = (f32[3,1,16,128]{3,2,1,0:T(8,128)S(1)}, f32[3,1,16,128]{3,2,1,0:T(8,128)S(1)}, u32[]{:S(2)}, u32[]{:S(2)}) collective-permute-start(f32[3,1,16,128]{3,2,1,0:T(8,128)S(1)} %get-tuple-element.118), channel_id=1, source_target_pairs={{8,0},{16,8},{24,16},{32,24},{40,32},{48,40},{56,48},{64,56},{72,6... | collective-permute-start | bytes 73736 | tf_op jit(solution)/shard_map/ppermute | solution.py:20
  26.8 17.6 %collective-permute-start.9 = (f32[3,1,16,128]{3,2,1,0:T(8,128)S(1)}, f32[3,1,16,128]{3,2,1,0:T(8,128)S(1)}, u32[]{:S(2)}, u32[]{:S(2)}) collective-permute-start(f32[3,1,16,128]{3,2,1,0:T(8,128)S(1)} %get-tuple-element.117), channel_id=1, source_target_pairs={{0,8},{8,16},{16,24},{24,32},{32,40},{40,48},{48,56},{56,64},{64,7... | collective-permute-start | bytes 73736 | tf_op jit(solution)/shard_map/ppermute | solution.py:17
  29.5 21.0 %collective-permute-start = (f32[3,1,16,128]{3,2,1,0:T(8,128)S(1)}, f32[3,1,16,128]{3,2,1,0:T(8,128)S(1)}, u32[]{:S(2)}, u32[]{:S(2)}) collective-permute-start(f32[3,1,16,128]{3,2,1,0:T(8,128)S(1)} %get-tuple-element.120), channel_id=1, source_target_pairs={{0,8},{8,16},{16,24},{24,32},{32,40},{40,48},{48,56},{56,64},{64,7... | collective-permute-start | bytes 73736 | tf_op jit(solution)/shard_map/ppermute | solution.py:17
  31.4 21.7 %collective-permute-start.1 = (f32[3,1,16,128]{3,2,1,0:T(8,128)S(1)}, f32[3,1,16,128]{3,2,1,0:T(8,128)S(1)}, u32[]{:S(2)}, u32[]{:S(2)}) collective-permute-start(f32[3,1,16,128]{3,2,1,0:T(8,128)S(1)} %get-tuple-element.119), channel_id=1, source_target_pairs={{8,0},{16,8},{24,16},{32,24},{40,32},{48,40},{56,48},{64,56},{72,6... | collective-permute-start | bytes 73736 | tf_op jit(solution)/shard_map/ppermute | solution.py:20
  44.4 31.0 %copy-start.8 = (f32[3,1,16,128]{3,2,1,0:T(8,128)}, f32[3,1,16,128]{3,2,1,0:T(8,128)S(1)}, u32[]{:S(2)}) copy-start(f32[3,1,16,128]{3,2,1,0:T(8,128)S(1)} %collective-permute-done.8) | copy-start | bytes 73732
  44.5 17.8 %copy-start.10 = (f32[3,1,16,128]{3,2,1,0:T(8,128)}, f32[3,1,16,128]{3,2,1,0:T(8,128)S(1)}, u32[]{:S(2)}) copy-start(f32[3,1,16,128]{3,2,1,0:T(8,128)S(1)} %collective-permute-done.9) | copy-start | bytes 73732
  44.5 6.0 collective-permute-start.10
  47.9 3.3 collective-permute-start.11
  50.5 0.6 copy-start.14
  51.1 2.7 copy-start.19
  51.2 11.0 %copy-start.20 = (f32[3,6,1,128]{3,2,1,0:T(1,128)}, f32[3,6,1,128]{3,2,1,0:T(1,128)S(1)}, u32[]{:S(2)}) copy-start(f32[3,6,1,128]{3,2,1,0:T(1,128)S(1)} %collective-permute-done.11) | copy-start | bytes 27652
  53.1 9.1 %copy-start.15 = (f32[3,1,16,128]{3,2,1,0:T(8,128)}, f32[3,1,16,128]{3,2,1,0:T(8,128)S(1)}, u32[]{:S(2)}) copy-start(f32[3,1,16,128]{3,2,1,0:T(8,128)S(1)} %collective-permute-done.1) | copy-start | bytes 73732
  53.8 27.3 %collective-permute-start.3 = (f32[3,6,1,128]{3,2,1,0:T(1,128)}, f32[3,6,1,128]{3,2,1,0:T(1,128)S(1)}, u32[]{:S(2)}, u32[]{:S(2)}) collective-permute-start(f32[3,6,1,128]{3,2,1,0:T(1,128)} %get-tuple-element.106), channel_id=1, source_target_pairs={{1,0},{2,1},{3,2},{4,3},{5,4},{6,5},{7,6},{0,7},{9,8},{10,9},{11,1... | collective-permute-start | bytes 27656 | tf_op jit(solution)/shard_map/ppermute | solution.py:20
  59.7 21.4 %collective-permute-start.2 = (f32[3,6,1,128]{3,2,1,0:T(1,128)}, f32[3,6,1,128]{3,2,1,0:T(1,128)}, u32[]{:S(2)}, u32[]{:S(2)}) collective-permute-start(f32[3,6,1,128]{3,2,1,0:T(1,128)} %get-tuple-element.105), channel_id=1, source_target_pairs={{0,1},{1,2},{2,3},{3,4},{4,5},{5,6},{6,7},{7,0},{8,9},{9,10},{10,1... | collective-permute-start | bytes 27656 | tf_op jit(solution)/shard_map/ppermute | solution.py:17
  62.3 12.1 %copy-start.13 = (f32[1,4,16,128]{3,2,1,0:T(8,128)S(1)}, f32[1,4,16,128]{3,2,1,0:T(8,128)}, u32[]{:S(2)}) copy-start(f32[1,4,16,128]{3,2,1,0:T(8,128)} %get-tuple-element.110) | copy-start | bytes 98308
  81.1 1.5 copy-start.17
  112.8 9.2 %copy-start.16 = (bf16[384,128]{1,0:T(8,128)(2,1)S(1)}, bf16[384,128]{1,0:T(8,128)(2,1)}, u32[]{:S(2)}) copy-start(bf16[384,128]{1,0:T(8,128)(2,1)} %convert_element_type.38) | copy-start | bytes 294916
  114.2 9.7 %copy-start.12 = (f32[512,128]{0,1:T(8,128)}, f32[512,128]{0,1:T(8,128)S(1)}, u32[]{:S(2)}) copy-start(f32[512,128]{0,1:T(8,128)S(1)} %fusion.1) | copy-start | bytes 786436
  136.0 20.0 %copy-start.2 = (f32[6,4,16,128]{3,2,1,0:T(8,128)}, f32[6,4,16,128]{3,2,1,0:T(8,128)S(1)}, u32[]{:S(2)}) copy-start(f32[6,4,16,128]{3,2,1,0:T(8,128)S(1)} %reshape.272) | copy-start | bytes 589828
  136.7 180.9 %collective-permute-start.4 = (f32[6,1,16,128]{3,2,1,0:T(8,128)}, f32[6,1,16,128]{3,2,1,0:T(8,128)}, u32[]{:S(2)}, u32[]{:S(2)}) collective-permute-start(f32[6,1,16,128]{3,2,1,0:T(8,128)} %get-tuple-element.99), channel_id=1, source_target_pairs={{0,8},{8,16},{16,24},{24,32},{32,40},{40,48},{48,56},{56,64},{64,7... | collective-permute-start | bytes 147464 | tf_op jit(solution)/shard_map/ppermute | solution.py:17
  138.6 179.8 %collective-permute-start.5 = (f32[6,1,16,128]{3,2,1,0:T(8,128)}, f32[6,1,16,128]{3,2,1,0:T(8,128)}, u32[]{:S(2)}, u32[]{:S(2)}) collective-permute-start(f32[6,1,16,128]{3,2,1,0:T(8,128)} %get-tuple-element.98), channel_id=1, source_target_pairs={{8,0},{16,8},{24,16},{32,24},{40,32},{48,40},{56,48},{64,56},{72,6... | collective-permute-start | bytes 147464 | tf_op jit(solution)/shard_map/ppermute | solution.py:20
  182.6 14.5 %copy-start.21 = (f32[512]{0:T(512)S(1)}, f32[512]{0:T(512)}, u32[]{:S(2)}) copy-start(f32[512]{0:T(512)} %get-tuple-element.121) | copy-start | bytes 6148
  189.7 113.6 %copy-start.5 = (f32[6,18,130]{2,1,0:T(8,128)S(1)}, f32[6,18,130]{2,1,0:T(8,128)}, u32[]{:S(2)}) copy-start(f32[6,18,130]{2,1,0:T(8,128)} %get-tuple-element.91) | copy-start | bytes 168484
  189.7 113.6 %copy-start.6 = (f32[6,18,130]{2,1,0:T(8,128)S(1)}, f32[6,18,130]{2,1,0:T(8,128)}, u32[]{:S(2)}) copy-start(f32[6,18,130]{2,1,0:T(8,128)} %get-tuple-element.92) | copy-start | bytes 168484
  189.7 113.6 %copy-start.7 = (f32[6,18,130]{2,1,0:T(8,128)S(1)}, f32[6,18,130]{2,1,0:T(8,128)}, u32[]{:S(2)}) copy-start(f32[6,18,130]{2,1,0:T(8,128)} %get-tuple-element.93) | copy-start | bytes 168484
  189.7 113.6 %copy-start.18 = (f32[3,6,1,128]{3,2,1,0:T(1,128)S(1)}, f32[3,6,1,128]{3,2,1,0:T(1,128)}, u32[]{:S(2)}) copy-start(f32[3,6,1,128]{3,2,1,0:T(1,128)} %copy-done.17) | copy-start | bytes 27652
  190.9 127.5 %copy-start.3 = (f32[6,4,16,128]{3,2,1,0:T(8,128)S(1)}, f32[6,4,16,128]{3,2,1,0:T(8,128)}, u32[]{:S(2)}) copy-start(f32[6,4,16,128]{3,2,1,0:T(8,128)} %copy-done.2) | copy-start | bytes 589828
  191.0 135.5 %copy-start.9 = (f32[3,1,16,128]{3,2,1,0:T(8,128)S(1)}, f32[3,1,16,128]{3,2,1,0:T(8,128)}, u32[]{:S(2)}) copy-start(f32[3,1,16,128]{3,2,1,0:T(8,128)} %copy-done.8) | copy-start | bytes 73732
  191.0 135.5 %copy-start.11 = (f32[3,1,16,128]{3,2,1,0:T(8,128)S(1)}, f32[3,1,16,128]{3,2,1,0:T(8,128)}, u32[]{:S(2)}) copy-start(f32[3,1,16,128]{3,2,1,0:T(8,128)} %copy-done.10) | copy-start | bytes 73732
  191.9 118.9 %collective-permute-start.13 = (f32[3,1,18,128]{3,2,1,0:T(8,128)}, f32[3,1,18,128]{3,2,1,0:T(8,128)S(1)}, u32[]{:S(2)}, u32[]{:S(2)}) collective-permute-start(f32[3,1,18,128]{3,2,1,0:T(8,128)} %get-tuple-element.78), channel_id=1, source_target_pairs={{8,0},{16,8},{24,16},{32,24},{40,32},{48,40},{56,48},{64,56},{72,6... | collective-permute-start | bytes 82952 | tf_op jit(solution)/shard_map/ppermute | solution.py:20
  193.8 117.0 %collective-permute-start.12 = (f32[3,1,18,128]{3,2,1,0:T(8,128)}, f32[3,1,18,128]{3,2,1,0:T(8,128)S(1)}, u32[]{:S(2)}, u32[]{:S(2)}) collective-permute-start(f32[3,1,18,128]{3,2,1,0:T(8,128)} %get-tuple-element.77), channel_id=1, source_target_pairs={{0,8},{8,16},{16,24},{24,32},{32,40},{40,48},{48,56},{56,64},{64,7... | collective-permute-start | bytes 82952 | tf_op jit(solution)/shard_map/ppermute | solution.py:17
  303.3 25.4 %copy-start.4 = (f32[3,4,16,128]{3,2,1,0:T(8,128)S(1)}, f32[3,4,16,128]{3,2,1,0:T(8,128)}, u32[]{:S(2)}) copy-start(f32[3,4,16,128]{3,2,1,0:T(8,128)} %param.15) | copy-start | bytes 294916
  308.1 467.6 %copy-start.1 = (bf16[648,512]{1,0:T(8,128)(2,1)S(1)}, bf16[648,512]{1,0:T(8,128)(2,1)}, u32[]{:S(2)}) copy-start(bf16[648,512]{1,0:T(8,128)(2,1)} %param.17) | copy-start | bytes 1990660
  310.8 6.5 collective-permute-start.15
  313.7 3.6 collective-permute-start.14
  319.3 8.8 %collective-permute-start.7 = (f32[6,6,1,128]{3,2,1,0:T(1,128)S(1)}, f32[6,6,1,128]{3,2,1,0:T(1,128)S(1)}, u32[]{:S(2)}, u32[]{:S(2)}) collective-permute-start(f32[6,6,1,128]{3,2,1,0:T(1,128)S(1)} %get-tuple-element.97), channel_id=1, source_target_pairs={{1,0},{2,1},{3,2},{4,3},{5,4},{6,5},{7,6},{0,7},{9,8},{10,9},{11,1... | collective-permute-start | bytes 55304 | tf_op jit(solution)/shard_map/ppermute | solution.py:20
  324.5 3.6 collective-permute-start.6
Sparse Core Ops, SparseCore 0:
  303.4 467.6 all-reduce.13
where the time goes:
time: 784 us; the launch traced here: 783 us
  waiting for transfers between devices  440 us (56%)
  blocking collectives  105 us (13%)
  local copies, waits for them, and re-layouts  104 us (13%)
  starting transfers between devices  78.4 us (10%)
  other arithmetic  31.5 us (4%)
  between operations  15.1 us (2%)
  matrix products  8.03 us (1%)
    psum x1, waiting for transfers between devices, on_device(): totals = lax.psum((w_in_s, b_in_s, w_out_s, b_out_s), ('gx', 'gy'))  440 us
    psum x1, blocking collectives, on_device(): totals = lax.psum((w_in_s, b_in_s, w_out_s, b_out_s), ('gx', 'gy'))  105 us
    ppermute x8, starting transfers between devices, extended(): lax.ppermute(lax.slice_in_dim(block, 0, width, axis=dim), axis, backward)  60.3 us
    slice x6, local copies, waits for them, and re-layouts, to_blocks(): stacked[..., offset:offset + 4 * count_z:4]  28.1 us
    ppermute x8, starting transfers between devices, extended(): lax.ppermute(lax.slice_in_dim(block, block.shape[dim] - width, None, axis...  18.1 us
  transfers between devices with their start and end apart: 17, of which 2 were waited for; matrix products, arithmetic and copies ran while one was open for 10% of the time, Pallas kernels for 0%

commit v1 on v0

--- a/solution.py
+++ b/solution.py
@@ -1,11 +1,56 @@
 import jax
 import jax.numpy as jnp
 from jax import lax
-from jax.sharding import PartitionSpec as P
+from jax.sharding import Mesh, PartitionSpec as P
 
 time_step = 0.25
 viscosity = 0.2
 penalty_eta = 0.05
+
+
+GX = ("zh", "x", "y")
+GY = ("zl", "core")
+ROWS = 136
+PARTS = 16
+
+
+def flatten(weight_in_sum, bias_in_sum, weight_out_sum, bias_out_sum):
+    pieces = [weight_in_sum[:, start : start + 128] for start in range(0, 512, 128)]
+    pieces += [weight_out_sum[:, start : start + 128] for start in range(0, 384, 128)]
+    pieces += [bias_in_sum.reshape(4, 128), bias_out_sum.reshape(3, 128)]
+    rows = sum(piece.shape[0] for piece in pieces)
+    pieces.append(jnp.zeros((2 * PARTS * ROWS - rows, 128), jnp.float32))
+    return jnp.concatenate(pieces, axis=0)
+
+
+def unflatten(flat):
+    weight_in_sum = jnp.concatenate([flat[648 * i : 648 * i + 648] for i in range(4)], axis=1)
+    base = 4 * 648
+    weight_out_sum = jnp.concatenate(
+        [flat[base + 512 * i : base + 512 * i + 512] for i in range(3)], axis=1
+    )
+    base = base + 3 * 512
+    bias_in_sum = flat[base : base + 4].reshape(512)
+    bias_out_sum = flat[base + 4 : base + 7].reshape(384)
+    return weight_in_sum, bias_in_sum, weight_out_sum, bias_out_sum
+
+
+def sum_everywhere(flat):
+    core = lax.axis_index("core")
+    swap = [(0, 1), (1, 0)]
+    halves = flat.reshape(2, PARTS, ROWS, 128)
+    got = lax.ppermute(halves[1 - core], "core", swap)
+    half = halves[core] + got
+    part = jnp.sum(lax.all_to_all(half, ("x", "y"), 0, 0), axis=0)
+    part = jnp.pad(part, ((0, 144 - ROWS), (0, 0))).reshape(16, 9, 128)
+    piece = jnp.sum(lax.all_to_all(part, ("zh", "zl"), 0, 0), axis=0)
+    part = lax.all_to_all(jnp.broadcast_to(piece, part.shape), ("zh", "zl"), 0, 0)
+    part = part.reshape(144, 128)[:ROWS]
+    half = lax.all_to_all(jnp.broadcast_to(part, half.shape), ("x", "y"), 0, 0)
+    other = lax.ppermute(half, "core", swap)
+    first = jnp.where(core == 0, half, other)
+    second = jnp.where(core == 0, other, half)
+    return jnp.stack([first, second]).reshape(2 * PARTS * ROWS, 128)
 
 
 def extended(block, sides, width):
@@ -175,13 +220,13 @@
     count_x = velocity.shape[1] // 4
     count_y = velocity.shape[2] // 4
     count_z = velocity.shape[3] // 4
-    rimmed = extended(velocity, (("gx", 1), ("gy", 2)), 1)
+    rimmed = extended(velocity, ((GX, 1), (GY, 2)), 1)
     padded = pad_depth(rimmed)
     factor = 1.0 + time_step * canopy.astype(jnp.float32) / penalty_eta
     incoming = cotangent.astype(jnp.float32)
     direct = incoming / factor
     adjoint = time_step * direct
-    adj_pad = pad_depth(extended(adjoint, (("gx", 1), ("gy", 2)), 1))
+    adj_pad = pad_depth(extended(adjoint, ((GX, 1), (GY, 2)), 1))
     grad_x = centred(adj_pad, 1)
     grad_y = centred(adj_pad, 2)
     grad_z = centred(adj_pad, 3)
@@ -191,7 +236,7 @@
         columns, to_rows(stress_grad), weight_in, bias_in, weight_out, bias_out
     )
     stress = from_rows(outputs, count_x, count_y, count_z)
-    stress_pad = pad_depth(extended(stress, (("gx", 1), ("gy", 2)), 1))
+    stress_pad = pad_depth(extended(stress, ((GX, 1), (GY, 2)), 1))
     along_x = select(stress_pad, (0, 3, 4))[:, :, 1:-1, 1:-1]
     along_y = select(stress_pad, (3, 1, 5))[:, 1:-1, :, 1:-1]
     along_z = pad_depth(select(stress, (4, 5, 2)))
@@ -208,14 +253,14 @@
     transport_b = grad_x * velocity[0:1] + grad_y * velocity[1:2] + grad_z * velocity[2:3]
     stencil_grad = direct + transport_a + transport_b + viscosity * laplace(adj_pad)
     ghost = fold_across(fold_depth_side(column_grad, count_x, count_y, count_z))[..., 1:-1]
-    widened = extended(ghost, (("gx", 1), ("gy", 2)), 1)
+    widened = extended(ghost, ((GX, 1), (GY, 2)), 1)
     middle = widened[:, 2:-2]
     middle = middle.at[:, 0].add(widened[:, 0]).at[:, -1].add(widened[:, -1])
     folded = middle[:, :, 2:-2]
     folded = folded.at[:, :, 0].add(middle[:, :, 0]).at[:, :, -1].add(middle[:, :, -1])
     velocity_grad = stencil_grad + folded
-    totals = lax.psum((w_in_s, b_in_s, w_out_s, b_out_s), ("gx", "gy"))
-    blocks_total = columns.shape[1] * lax.axis_size("gx") * lax.axis_size("gy")
+    totals = unflatten(sum_everywhere(flatten(w_in_s, b_in_s, w_out_s, b_out_s)))
+    blocks_total = columns.shape[1] * lax.axis_size(GX) * lax.axis_size(GY)
     scale = float(blocks_total) ** (-0.5)
     weight_in_grad = totals[0] * scale
     bias_in_grad = totals[1] * scale
@@ -232,19 +277,20 @@
 
 
 def solution(mesh):
+    mesh = Mesh(mesh.devices.reshape(4, 4, 4, 4, 2), GX + GY)
     placed = (
-        P(None, "gx", "gy", None),
-        P("gx", "gy", None),
-        P(),
-        P(),
-        P(),
-        P(),
-        P(None, "gx", "gy", None),
+        P(None, GX, GY, None),
+        P(GX, GY, None),
+        P(),
+        P(),
+        P(),
+        P(),
+        P(None, GX, GY, None),
     )
     return jax.shard_map(
         on_device,
         mesh=mesh,
         in_specs=placed,
-        out_specs=(P(None, "gx", "gy", None), P(None, "gx", "gy", None), P(), P(), P(), P()),
+        out_specs=(P(None, GX, GY, None), P(None, GX, GY, None), P(), P(), P(), P()),
         check_vma=False,
     )

time: 784 us -> 305 us (0.39)
  waiting for transfers between devices: 440 us -> 26.8 us
  blocking collectives: 105 us -> 0 us
  starting transfers between devices: 78.4 us -> 118 us
  between operations: 15.1 us -> 1.99 us
  local copies, waits for them, and re-layouts: 104 us -> 116 us
    psum x1 -> x0, waiting for transfers between devices: 440 us -> none  [on_device(): totals = lax.psum((w_in_s, b_in_s, w_out_s, b_out_s), ('gx', 'gy'))]
    psum x1 -> x0, blocking collectives: 105 us -> none  [on_device(): totals = lax.psum((w_in_s, b_in_s, w_out_s, b_out_s), ('gx', 'gy'))]
    all_to_all x0 -> x4, starting transfers between devices: none -> 26.7 us  [the longest x1 9.84 us: sum_everywhere(): half = lax.all_to_all(jnp.broadcast_to(part, half.shape), ('x', 'y'), 0, 0)]
    all_to_all x0 -> x4, waiting for transfers between devices: none -> 26 us  [the longest x1 15.9 us: sum_everywhere(): part = jnp.sum(lax.all_to_all(half, ('x', 'y'), 0, 0), axis=0)]
    ppermute x0 -> x2, starting transfers between devices: none -> 8.44 us  [the longest x1 5.49 us: sum_everywhere(): other = lax.ppermute(half, 'core', swap)]
  transfers between devices with their start and end apart: 17 -> 22, of which waited for: 2 -> 4; matrix products, arithmetic and copies ran while one was open for 10% -> 32% of each run, Pallas kernels for 0% -> 0%
where the time goes in v1:
time: 305 us; the launch traced here: 301 us
  starting transfers between devices  118 us (39%)
  local copies, waits for them, and re-layouts  116 us (38%)
  other arithmetic  35.1 us (12%)
  waiting for transfers between devices  26.8 us (9%)
  matrix products  3.38 us (1%)
    ppermute x8, starting transfers between devices, extended(): lax.ppermute(lax.slice_in_dim(block, 0, width, axis=dim), axis, backward)  63.9 us
    slice x6, local copies, waits for them, and re-layouts, to_blocks(): stacked[..., offset:offset + 4 * count_z:4]  28.1 us
    ppermute x8, starting transfers between devices, extended(): lax.ppermute(lax.slice_in_dim(block, block.shape[dim] - width, None, axis...  19.4 us
    all_to_all x1, waiting for transfers between devices, sum_everywhere(): part = jnp.sum(lax.all_to_all(half, ('x', 'y'), 0, 0), axis=0)  15.9 us
    another operation x2, other arithmetic, fold_last(): jnp.stack([stacked[..., 4, :], stacked[..., 5, :], blank, blank], axis=-1)  10.2 us
    all_to_all x1, waiting for transfers between devices, sum_everywhere(): half = lax.all_to_all(jnp.broadcast_to(part, half.shape), ('x', 'y'), 0, 0)  10.1 us
    all_to_all x1, starting transfers between devices, sum_everywhere(): half = lax.all_to_all(jnp.broadcast_to(part, half.shape), ('x', 'y'), 0, 0)  9.84 us
    another operation x6, local copies, waits for them, and re-layouts, fold_last(): jnp.stack([stacked[..., 4, :], stacked[..., 5, :], blank, blank], axis=-1)  9.58 us
  transfers between devices with their start and end apart: 22, of which 4 were waited for; matrix products, arithmetic and copies ran while one was open for 32% of the time, Pallas kernels for 0%

profile of v1, /device:TPU:1, one launch (start us, length us, event | category | flops | bytes accessed | tf_op | source)
XLA Modules:
  0.0 301.5 jit_solution(4085565387152064541)
XLA Ops:
  2.9 17.9 %collective-permute-start.8 = (f32[3,1,16,128]{3,2,1,0:T(8,128)S(1)}, f32[3,1,16,128]{3,2,1,0:T(8,128)S(1)}, u32[]{:S(2)}, u32[]{:S(2)}) collective-permute-start(f32[3,1,16,128]{3,2,1,0:T(8,128)S(1)} %get-tuple-element.130), channel_id=1, source_target_pairs={{8,0},{16,8},{24,16},{32,24},{40,32},{48,40},{56,48},{64,56},{72,6... | collective-permute-start | bytes 73736 | tf_op jit(solution)/shard_map/ppermute | solution.py:65
  20.9 1.9 collective-permute-start.9
  23.6 1.9 collective-permute-start
  25.5 11.5 %collective-permute-start.1 = (f32[3,1,16,128]{3,2,1,0:T(8,128)S(1)}, f32[3,1,16,128]{3,2,1,0:T(8,128)S(1)}, u32[]{:S(2)}, u32[]{:S(2)}) collective-permute-start(f32[3,1,16,128]{3,2,1,0:T(8,128)S(1)} %get-tuple-element.131), channel_id=1, source_target_pairs={{8,0},{16,8},{24,16},{32,24},{40,32},{48,40},{56,48},{64,56},{72,6... | collective-permute-start | bytes 73736 | tf_op jit(solution)/shard_map/ppermute | solution.py:65
  37.0 1.4 multiply_bitcast_fusion.2
  38.5 3.4 %collective-permute-start.10 = (f32[3,6,1,128]{3,2,1,0:T(1,128)S(1)}, f32[3,6,1,128]{3,2,1,0:T(1,128)S(1)}, u32[]{:S(2)}, u32[]{:S(2)}) collective-permute-start(f32[3,6,1,128]{3,2,1,0:T(1,128)S(1)} %get-tuple-element.116), channel_id=1, source_target_pairs={{1,0},{2,1},{3,2},{4,3},{5,4},{6,5},{7,6},{0,7},{9,8},{10,9},{11,1... | collective-permute-start | bytes 27656 | tf_op jit(solution)/shard_map/ppermute | solution.py:65
  42.0 2.5 collective-permute-start.11
  47.1 5.9 %collective-permute-start.3 = (f32[3,6,1,128]{3,2,1,0:T(1,128)}, f32[3,6,1,128]{3,2,1,0:T(1,128)}, u32[]{:S(2)}, u32[]{:S(2)}) collective-permute-start(f32[3,6,1,128]{3,2,1,0:T(1,128)} %get-tuple-element.118), channel_id=1, source_target_pairs={{1,0},{2,1},{3,2},{4,3},{5,4},{6,5},{7,6},{0,7},{9,8},{10,9},{11,1... | collective-permute-start | bytes 27656 | tf_op jit(solution)/shard_map/ppermute | solution.py:65
  53.0 1.9 collective-permute-start.2
  69.7 4.7 %slice.582 = bf16[3,6,1,6,4,32]{5,4,0,1,3,2:T(4,128)(2,1)S(1)} slice(bf16[3,6,1,6,4,130]{5,4,0,1,3,2:T(4,128)(2,1)S(1)} %bitcast_dynamic-update-slice_fusion.6), slice={[0:3:1], [0:6:1], [0:1:1], [0:6:1], [0:4:1], [0:128:4]} | slice | bytes 55296 | tf_op jit(solution)/shard_map/slice | solution.py:119
  74.3 4.7 %slice.583 = bf16[3,6,1,6,4,32]{5,4,0,1,3,2:T(4,128)(2,1)S(1)} slice(bf16[3,6,1,6,4,130]{5,4,0,1,3,2:T(4,128)(2,1)S(1)} %bitcast_dynamic-update-slice_fusion.6), slice={[0:3:1], [0:6:1], [0:1:1], [0:6:1], [0:4:1], [1:129:4]} | slice | bytes 55296 | tf_op jit(solution)/shard_map/slice | solution.py:119
  79.0 4.7 %slice.584 = bf16[3,6,1,6,4,32]{5,4,0,1,3,2:T(4,128)(2,1)S(1)} slice(bf16[3,6,1,6,4,130]{5,4,0,1,3,2:T(4,128)(2,1)S(1)} %bitcast_dynamic-update-slice_fusion.6), slice={[0:3:1], [0:6:1], [0:1:1], [0:6:1], [0:4:1], [2:130:4]} | slice | bytes 55296 | tf_op jit(solution)/shard_map/slice | solution.py:119
  83.7 4.7 %slice.585 = bf16[3,6,1,6,4,32]{5,4,0,1,3,2:T(4,128)(2,1)S(1)} slice(bf16[3,6,1,6,4,130]{5,4,0,1,3,2:T(4,128)(2,1)S(1)} %bitcast_dynamic-update-slice_fusion.6), slice={[0:3:1], [0:6:1], [0:1:1], [0:6:1], [0:4:1], [3:130:4]} | slice | bytes 55296 | tf_op jit(solution)/shard_map/slice | solution.py:119
  88.4 4.7 %slice.586 = bf16[3,6,1,6,4,32]{5,4,0,1,3,2:T(4,128)(2,1)S(1)} slice(bf16[3,6,1,6,4,130]{5,4,0,1,3,2:T(4,128)(2,1)S(1)} %bitcast_dynamic-update-slice_fusion.6), slice={[0:3:1], [0:6:1], [0:1:1], [0:6:1], [0:4:1], [4:130:4]} | slice | bytes 55296 | tf_op jit(solution)/shard_map/slice | solution.py:119
  93.1 4.7 %slice.587 = bf16[3,6,1,6,4,32]{5,4,0,1,3,2:T(4,128)(2,1)S(1)} slice(bf16[3,6,1,6,4,130]{5,4,0,1,3,2:T(4,128)(2,1)S(1)} %bitcast_dynamic-update-slice_fusion.6), slice={[0:3:1], [0:6:1], [0:1:1], [0:6:1], [0:4:1], [5:130:4]} | slice | bytes 55296 | tf_op jit(solution)/shard_map/slice | solution.py:119
  102.8 4.4 %copy.159 = f32[6,1,4,4,4,32,4]{6,5,4,3,2,0,1:T(8,128)} copy(f32[6,1,4,4,4,32,4]{5,3,6,4,2,0,1:T(4,128)S(1)} %bitcast.208) | data formatting | bytes 393216 | tf_op jit(solution)/shard_map/transpose | solution.py:126
  107.2 6.6 %reshape.297 = f32[6,4,16,128]{3,2,1,0:T(8,128)S(1)} reshape(f32[6,1,4,4,4,32,4]{6,5,4,3,2,0,1:T(8,128)} %copy.159) | data formatting | bytes 393216 | tf_op jit(solution)/shard_map/reshape | solution.py:127
  114.4 1.9 collective-permute-start.4
  116.4 11.7 %collective-permute-start.5 = (f32[6,1,16,128]{3,2,1,0:T(8,128)}, f32[6,1,16,128]{3,2,1,0:T(8,128)}, u32[]{:S(2)}, u32[]{:S(2)}) collective-permute-start(f32[6,1,16,128]{3,2,1,0:T(8,128)} %get-tuple-element.110), channel_id=1, source_target_pairs={{8,0},{16,8},{24,16},{32,24},{40,32},{48,40},{56,48},{64,56},{72,6... | collective-permute-start | bytes 147464 | tf_op jit(solution)/shard_map/ppermute | solution.py:65
  129.8 4.6 %copy.173 = f32[3,6,1,6,4,32,1]{6,5,4,3,1,0,2:T(8,128)} copy(f32[3,6,1,6,4,32,1]{5,4,3,1,0,6,2:T(4,128)S(1)} %get-tuple-element.74) | data formatting | bytes 110592 | tf_op jit(solution)/shard_map/stack;squeeze | solution.py:147
  134.5 4.7 %copy.172 = f32[3,6,1,6,4,32,1]{6,5,4,3,1,0,2:T(8,128)} copy(f32[3,6,1,6,4,32,1]{5,4,3,1,0,6,2:T(4,128)S(1)} %get-tuple-element.75) | data formatting | bytes 110592 | tf_op jit(solution)/shard_map/stack;squeeze | solution.py:147
  142.0 6.0 %concatenate.112 = f32[4352,128]{1,0:T(8,128)S(1)} concatenate(f32[648,128]{1,0:T(8,128)} %get-tuple-element.72, f32[648,128]{1,0:T(8,128)S(1)} %get-tuple-element.71, f32[648,128]{1,0:T(8,128)S(1)} %get-tuple-element.70, f32[648,128]{1,0:T(8,128)S(1)} %get-tuple-element.69, f32[512,128]{1,0:T(8,128)} %get-tuple-element.85, f32[512,128]{1,0:T(8,128)} %get-tuple-element.84, ...), dimensions={0} | concatenate | bytes 4456448 | tf_op jit(solution)/shard_map/concatenate | solution.py:23
  149.0 3.0 collective-permute-start.16
  152.0 10.0 %maximum_maximum_fusion = f32[3,6,1,6,4,32,4]{6,5,4,3,1,0,2:T(8,128)} fusion(f32[3,6,1,6,4,32,1]{6,5,4,3,1,0,2:T(8,128)} %copy.173, f32[3,6,1,6,4,32,1]{6,5,4,3,1,0,2:T(8,128)} %copy.172, f32[4]{0:T(128)S(1)} %pad.71.clone), kind=kLoop, calls=%fused_computation | loop fusion | flops 110592 | bytes 331792 | tf_op jit(solution)/shard_map/stack | solution.py:147
  162.0 7.1 %reshape.300 = f32[3,6,1,6,4,128]{5,4,3,1,0,2:T(4,128)S(1)} reshape(f32[3,6,1,6,4,32,4]{6,5,4,3,1,0,2:T(8,128)} %maximum_maximum_fusion) | data formatting | bytes 442368 | tf_op jit(solution)/shard_map/reshape | solution.py:147
  169.2 2.1 pad_maximum_fusion.1
  171.3 5.6 %copy.171 = f32[3,6,1,6,4,32,4]{6,5,4,3,1,0,2:T(8,128)} copy(f32[3,6,1,6,4,32,4]{5,4,3,1,0,6,2:T(4,128)} %pad_maximum_fusion.1) | data formatting | bytes 442368 | tf_op jit(solution)/shard_map/stack | solution.py:143
  176.9 7.0 %reshape.299 = f32[3,6,1,6,4,128]{5,4,3,1,0,2:T(4,128)S(1)} reshape(f32[3,6,1,6,4,32,4]{6,5,4,3,1,0,2:T(8,128)} %copy.171) | data formatting | bytes 442368 | tf_op jit(solution)/shard_map/reshape | solution.py:143
  185.4 2.4 bitcast_add_fusion
  187.9 3.7 %all-to-all-start = ((f32[16,136,128]{2,1,0:T(8,128)}), f32[16,136,128]{2,1,0:T(8,128)S(1)}, u32[]{:S(2)}, u32[]{:S(2)}) async-start(f32[16,136,128]{2,1,0:T(8,128)} %bitcast_add_fusion), calls=%async_computation | async-start | bytes 2228224 | tf_op jit(solution)/shard_map/all_to_all | solution.py:44
  194.4 15.9 %all-to-all-done = f32[16,136,128]{2,1,0:T(8,128)S(1)} async-done(((f32[16,136,128]{2,1,0:T(8,128)}), f32[16,136,128]{2,1,0:T(8,128)S(1)}, u32[]{:S(2)}, u32[]{:S(2)}) %all-to-all-start) | async-done | bytes 1114144 | tf_op jit(solution)/shard_map/all_to_all | solution.py:44
  211.0 5.5 %all-to-all-start.1 = ((f32[16,9,128]{2,1,0:T(8,128)}), f32[16,9,128]{2,1,0:T(8,128)S(1)}, u32[]{:S(2)}, u32[]{:S(2)}) async-start(f32[16,9,128]{2,1,0:T(8,128)} %reshape.308), calls=%async_computation.1 | async-start | bytes 262144 | tf_op jit(solution)/shard_map/all_to_all | solution.py:46
  217.3 7.2 %collective-permute-start.13 = (f32[3,1,18,128]{3,2,1,0:T(8,128)}, f32[3,1,18,128]{3,2,1,0:T(8,128)S(1)}, u32[]{:S(2)}, u32[]{:S(2)}) collective-permute-start(f32[3,1,18,128]{3,2,1,0:T(8,128)} %get-tuple-element.90), channel_id=1, source_target_pairs={{8,0},{16,8},{24,16},{32,24},{40,32},{48,40},{56,48},{64,56},{72,6... | collective-permute-start | bytes 82952 | tf_op jit(solution)/shard_map/ppermute | solution.py:65
  224.5 2.1 collective-permute-start.12
  226.7 2.1 broadcast_multiply_fusion.2
  229.4 7.6 %all-to-all-start.2 = ((f32[16,9,128]{2,1,0:T(8,128)}), f32[16,9,128]{2,1,0:T(8,128)}, u32[]{:S(2)}, u32[]{:S(2)}) async-start(f32[16,9,128]{2,1,0:T(8,128)} %broadcast_in_dim.7), calls=%async_computation.2 | async-start | bytes 262144 | tf_op jit(solution)/shard_map/all_to_all | solution.py:47
  242.3 4.4 %collective-permute-start.15 = (f32[3,8,1,128]{3,2,1,0:T(1,128)S(1)}, f32[3,8,1,128]{3,2,1,0:T(1,128)S(1)}, u32[]{:S(2)}, u32[]{:S(2)}) collective-permute-start(f32[3,8,1,128]{3,2,1,0:T(1,128)S(1)} %get-tuple-element.107), channel_id=1, source_target_pairs={{1,0},{2,1},{3,2},{4,3},{5,4},{6,5},{7,6},{0,7},{9,8},{10,9},{11,1... | collective-permute-start | bytes 36872 | tf_op jit(solution)/shard_map/ppermute | solution.py:65
  246.7 3.4 %collective-permute-start.14 = (f32[3,8,1,128]{3,2,1,0:T(1,128)S(1)}, f32[3,8,1,128]{3,2,1,0:T(1,128)S(1)}, u32[]{:S(2)}, u32[]{:S(2)}) collective-permute-start(f32[3,8,1,128]{3,2,1,0:T(1,128)S(1)} %get-tuple-element.106), channel_id=1, source_target_pairs={{0,1},{1,2},{2,3},{3,4},{4,5},{5,6},{6,7},{7,0},{8,9},{9,10},{10,1... | collective-permute-start | bytes 36872 | tf_op jit(solution)/shard_map/ppermute | solution.py:62
  252.9 9.8 %all-to-all-start.3 = ((f32[16,136,128]{2,1,0:T(8,128)}), f32[16,136,128]{2,1,0:T(8,128)S(1)}, u32[]{:S(2)}, u32[]{:S(2)}) async-start(f32[16,136,128]{2,1,0:T(8,128)} %broadcast_in_dim.8), calls=%async_computation.3 | async-start | bytes 2228224 | tf_op jit(solution)/shard_map/all_to_all | solution.py:49
  265.7 1.4 constant_dynamic-update-slice_fusion.5
  267.8 10.1 %all-to-all-done.3 = f32[16,136,128]{2,1,0:T(8,128)S(1)} async-done(((f32[16,136,128]{2,1,0:T(8,128)}), f32[16,136,128]{2,1,0:T(8,128)S(1)}, u32[]{:S(2)}, u32[]{:S(2)}) %all-to-all-start.3) | async-done | bytes 1114144 | tf_op jit(solution)/shard_map/all_to_all | solution.py:49
  277.9 5.5 %collective-permute-start.17 = (f32[16,136,128]{2,1,0:T(8,128)S(1)}, f32[16,136,128]{2,1,0:T(8,128)S(1)}, u32[]{:S(2)}, u32[]{:S(2)}) collective-permute-start(f32[16,136,128]{2,1,0:T(8,128)S(1)} %all-to-all-done.3), channel_id=1, source_target_pairs={{0,1},{1,0},{2,3},{3,2},{4,5},{5,4},{6,7},{7,6},{8,9},{9,8},{10,11... | collective-permute-start | bytes 3342344 | tf_op jit(solution)/shard_map/ppermute | solution.py:50
  283.4 1.4 constant_dynamic-update-slice_fusion.3
  285.9 1.9 collective-permute-start.7
  287.8 3.6 %collective-permute-start.6 = (f32[6,6,1,128]{3,2,1,0:T(1,128)S(1)}, f32[6,6,1,128]{3,2,1,0:T(1,128)S(1)}, u32[]{:S(2)}, u32[]{:S(2)}) collective-permute-start(f32[6,6,1,128]{3,2,1,0:T(1,128)S(1)} %get-tuple-element.108), channel_id=1, source_target_pairs={{0,1},{1,2},{2,3},{3,4},{4,5},{5,6},{6,7},{7,0},{8,9},{9,10},{10,1... | collective-permute-start | bytes 55304 | tf_op jit(solution)/shard_map/ppermute | solution.py:62
  291.5 1.9 fusion.27
  294.0 1.4 select_maximum_fusion
  295.6 2.1 fusion.11
  (244 shorter events, 54.7 us)
Async XLA Ops:
  0.6 98.2 %copy-start = (bf16[648,512]{1,0:T(8,128)(2,1)S(1)}, bf16[648,512]{1,0:T(8,128)(2,1)}, u32[]{:S(2)}) copy-start(bf16[648,512]{1,0:T(8,128)(2,1)} %param.17) | copy-start | bytes 1990660
  0.6 44.9 %copy-start.12 = (f32[3,4,16,128]{3,2,1,0:T(8,128)S(1)}, f32[3,4,16,128]{3,2,1,0:T(8,128)}, u32[]{:S(2)}) copy-start(f32[3,4,16,128]{3,2,1,0:T(8,128)} %param.15) | copy-start | bytes 294916
  2.9 35.6 %collective-permute-start.8 = (f32[3,1,16,128]{3,2,1,0:T(8,128)S(1)}, f32[3,1,16,128]{3,2,1,0:T(8,128)S(1)}, u32[]{:S(2)}, u32[]{:S(2)}) collective-permute-start(f32[3,1,16,128]{3,2,1,0:T(8,128)S(1)} %get-tuple-element.130), channel_id=1, source_target_pairs={{8,0},{16,8},{24,16},{32,24},{40,32},{48,40},{56,48},{64,56},{72,6... | collective-permute-start | bytes 73736 | tf_op jit(solution)/shard_map/ppermute | solution.py:65
  20.9 17.6 %collective-permute-start.9 = (f32[3,1,16,128]{3,2,1,0:T(8,128)S(1)}, f32[3,1,16,128]{3,2,1,0:T(8,128)S(1)}, u32[]{:S(2)}, u32[]{:S(2)}) collective-permute-start(f32[3,1,16,128]{3,2,1,0:T(8,128)S(1)} %get-tuple-element.129), channel_id=1, source_target_pairs={{0,8},{8,16},{16,24},{24,32},{32,40},{40,48},{48,56},{56,64},{64,7... | collective-permute-start | bytes 73736 | tf_op jit(solution)/shard_map/ppermute | solution.py:62
  23.6 21.0 %collective-permute-start = (f32[3,1,16,128]{3,2,1,0:T(8,128)S(1)}, f32[3,1,16,128]{3,2,1,0:T(8,128)S(1)}, u32[]{:S(2)}, u32[]{:S(2)}) collective-permute-start(f32[3,1,16,128]{3,2,1,0:T(8,128)S(1)} %get-tuple-element.132), channel_id=1, source_target_pairs={{0,8},{8,16},{16,24},{24,32},{32,40},{40,48},{48,56},{56,64},{64,7... | collective-permute-start | bytes 73736 | tf_op jit(solution)/shard_map/ppermute | solution.py:62
  25.5 20.9 %collective-permute-start.1 = (f32[3,1,16,128]{3,2,1,0:T(8,128)S(1)}, f32[3,1,16,128]{3,2,1,0:T(8,128)S(1)}, u32[]{:S(2)}, u32[]{:S(2)}) collective-permute-start(f32[3,1,16,128]{3,2,1,0:T(8,128)S(1)} %get-tuple-element.131), channel_id=1, source_target_pairs={{8,0},{16,8},{24,16},{32,24},{40,32},{48,40},{56,48},{64,56},{72,6... | collective-permute-start | bytes 73736 | tf_op jit(solution)/shard_map/ppermute | solution.py:65
  38.5 18.2 %copy-start.24 = (f32[3,1,16,128]{3,2,1,0:T(8,128)}, f32[3,1,16,128]{3,2,1,0:T(8,128)S(1)}, u32[]{:S(2)}) copy-start(f32[3,1,16,128]{3,2,1,0:T(8,128)S(1)} %collective-permute-done.8) | copy-start | bytes 73732
  38.5 17.1 %copy-start.26 = (f32[3,1,16,128]{3,2,1,0:T(8,128)}, f32[3,1,16,128]{3,2,1,0:T(8,128)S(1)}, u32[]{:S(2)}) copy-start(f32[3,1,16,128]{3,2,1,0:T(8,128)S(1)} %collective-permute-done.9) | copy-start | bytes 73732
  38.5 6.0 %collective-permute-start.10 = (f32[3,6,1,128]{3,2,1,0:T(1,128)S(1)}, f32[3,6,1,128]{3,2,1,0:T(1,128)S(1)}, u32[]{:S(2)}, u32[]{:S(2)}) collective-permute-start(f32[3,6,1,128]{3,2,1,0:T(1,128)S(1)} %get-tuple-element.116), channel_id=1, source_target_pairs={{1,0},{2,1},{3,2},{4,3},{5,4},{6,5},{7,6},{0,7},{9,8},{10,9},{11,1... | collective-permute-start | bytes 27656 | tf_op jit(solution)/shard_map/ppermute | solution.py:65
  42.0 3.3 %collective-permute-start.11 = (f32[3,6,1,128]{3,2,1,0:T(1,128)S(1)}, f32[3,6,1,128]{3,2,1,0:T(1,128)S(1)}, u32[]{:S(2)}, u32[]{:S(2)}) collective-permute-start(f32[3,6,1,128]{3,2,1,0:T(1,128)S(1)} %get-tuple-element.115), channel_id=1, source_target_pairs={{0,1},{1,2},{2,3},{3,4},{4,5},{5,6},{6,7},{7,0},{8,9},{9,10},{10,1... | collective-permute-start | bytes 27656 | tf_op jit(solution)/shard_map/ppermute | solution.py:62
  45.1 10.4 %copy-start.39 = (f32[3,6,1,128]{3,2,1,0:T(1,128)}, f32[3,6,1,128]{3,2,1,0:T(1,128)S(1)}, u32[]{:S(2)}) copy-start(f32[3,6,1,128]{3,2,1,0:T(1,128)S(1)} %collective-permute-done.10) | copy-start | bytes 27652
  45.3 10.3 %copy-start.40 = (f32[3,6,1,128]{3,2,1,0:T(1,128)}, f32[3,6,1,128]{3,2,1,0:T(1,128)S(1)}, u32[]{:S(2)}) copy-start(f32[3,6,1,128]{3,2,1,0:T(1,128)S(1)} %collective-permute-done.11) | copy-start | bytes 27652
  45.6 11.6 %copy-start.8 = (f32[3,6,18,130]{3,2,1,0:T(8,128)}, f32[3,6,18,130]{3,2,1,0:T(8,128)S(1)}, u32[]{:S(2)}) copy-start(f32[3,6,18,130]{3,2,1,0:T(8,128)S(1)} %select_maximum_fusion.2) | copy-start | bytes 505444
  46.4 9.2 %copy-start.37 = (f32[3,1,16,128]{3,2,1,0:T(8,128)}, f32[3,1,16,128]{3,2,1,0:T(8,128)S(1)}, u32[]{:S(2)}) copy-start(f32[3,1,16,128]{3,2,1,0:T(8,128)S(1)} %collective-permute-done.1) | copy-start | bytes 73732
  46.4 19.7 %copy-start.6 = (f32[3,6,16,128]{3,2,1,0:T(8,128)}, f32[3,6,16,128]{3,2,1,0:T(8,128)S(1)}, u32[]{:S(2)}) copy-start(f32[3,6,16,128]{3,2,1,0:T(8,128)S(1)} %constant_dynamic-update-slice_fusion) | copy-start | bytes 442372
  47.1 19.0 %collective-permute-start.3 = (f32[3,6,1,128]{3,2,1,0:T(1,128)}, f32[3,6,1,128]{3,2,1,0:T(1,128)}, u32[]{:S(2)}, u32[]{:S(2)}) collective-permute-start(f32[3,6,1,128]{3,2,1,0:T(1,128)} %get-tuple-element.118), channel_id=1, source_target_pairs={{1,0},{2,1},{3,2},{4,3},{5,4},{6,5},{7,6},{0,7},{9,8},{10,9},{11,1... | collective-permute-start | bytes 27656 | tf_op jit(solution)/shard_map/ppermute | solution.py:65
  53.0 13.2 %collective-permute-start.2 = (f32[3,6,1,128]{3,2,1,0:T(1,128)}, f32[3,6,1,128]{3,2,1,0:T(1,128)}, u32[]{:S(2)}, u32[]{:S(2)}) collective-permute-start(f32[3,6,1,128]{3,2,1,0:T(1,128)} %get-tuple-element.117), channel_id=1, source_target_pairs={{0,1},{1,2},{2,3},{3,4},{4,5},{5,6},{6,7},{7,0},{8,9},{9,10},{10,1... | collective-permute-start | bytes 27656 | tf_op jit(solution)/shard_map/ppermute | solution.py:62
  102.8 4.4 %copy-start.2 = (f32[6,4,4,4,1,4,32]{6,5,3,2,1,0,4:T(4,128)}, f32[6,4,4,4,1,4,32]{6,5,3,2,1,0,4:T(4,128)S(1)}, u32[]{:S(2)}) copy-start(f32[6,4,4,4,1,4,32]{6,5,3,2,1,0,4:T(4,128)S(1)} %reshape.296) | copy-start | bytes 589828
  107.2 20.9 %copy-start.9 = (f32[648,128]{1,0:T(8,128)S(1)}, f32[648,128]{1,0:T(8,128)}, u32[]{:S(2)}) copy-start(f32[648,128]{1,0:T(8,128)} %convolution_bitcast_fusion) | copy-start | bytes 995332
  113.7 15.1 %copy-start.10 = (f32[6,4,16,128]{3,2,1,0:T(8,128)}, f32[6,4,16,128]{3,2,1,0:T(8,128)S(1)}, u32[]{:S(2)}) copy-start(f32[6,4,16,128]{3,2,1,0:T(8,128)S(1)} %reshape.297) | copy-start | bytes 589828
  114.4 151.3 %collective-permute-start.4 = (f32[6,1,16,128]{3,2,1,0:T(8,128)}, f32[6,1,16,128]{3,2,1,0:T(8,128)}, u32[]{:S(2)}, u32[]{:S(2)}) collective-permute-start(f32[6,1,16,128]{3,2,1,0:T(8,128)} %get-tuple-element.111), channel_id=1, source_target_pairs={{0,8},{8,16},{16,24},{24,32},{32,40},{40,48},{48,56},{56,64},{64,7... | collective-permute-start | bytes 147464 | tf_op jit(solution)/shard_map/ppermute | solution.py:62
  116.4 167.1 %collective-permute-start.5 = (f32[6,1,16,128]{3,2,1,0:T(8,128)}, f32[6,1,16,128]{3,2,1,0:T(8,128)}, u32[]{:S(2)}, u32[]{:S(2)}) collective-permute-start(f32[6,1,16,128]{3,2,1,0:T(8,128)} %get-tuple-element.110), channel_id=1, source_target_pairs={{8,0},{16,8},{24,16},{32,24},{40,32},{48,40},{56,48},{64,56},{72,6... | collective-permute-start | bytes 147464 | tf_op jit(solution)/shard_map/ppermute | solution.py:65
  149.0 36.4 %collective-permute-start.16 = (f32[16,136,128]{2,1,0:T(8,128)}, f32[16,136,128]{2,1,0:T(8,128)}, u32[]{:S(2)}, u32[]{:S(2)}) collective-permute-start(f32[16,136,128]{2,1,0:T(8,128)} %dynamic-slice_bitcast_fusion), channel_id=1, source_target_pairs={{0,1},{1,0},{2,3},{3,2},{4,5},{5,4},{6,7},{7,6},{8,9},{9,8},{10,11... | collective-permute-start | bytes 3342344 | tf_op jit(solution)/shard_map/ppermute | solution.py:42
  162.0 7.1 %copy-start.14 = (f32[3,6,1,6,4,32,1]{5,4,3,1,0,6,2:T(4,128)S(1)}, f32[3,6,1,6,4,32,1]{5,4,3,1,0,6,2:T(4,128)}, u32[]{:S(2)}) copy-start(f32[3,6,1,6,4,32,1]{5,4,3,1,0,6,2:T(4,128)} %get-tuple-element.73) | copy-start | bytes 165892
  162.0 7.1 %copy-start.15 = (f32[3,6,1,6,4,32,1]{5,4,3,1,0,6,2:T(4,128)S(1)}, f32[3,6,1,6,4,32,1]{5,4,3,1,0,6,2:T(4,128)}, u32[]{:S(2)}) copy-start(f32[3,6,1,6,4,32,1]{5,4,3,1,0,6,2:T(4,128)} %get-tuple-element.76) | copy-start | bytes 165892
  162.0 7.1 %copy-start.16 = (f32[3,6,1,6,4,32,1]{5,4,3,1,0,6,2:T(4,128)S(1)}, f32[3,6,1,6,4,32,1]{5,4,3,1,0,6,2:T(4,128)}, u32[]{:S(2)}) copy-start(f32[3,6,1,6,4,32,1]{5,4,3,1,0,6,2:T(4,128)} %get-tuple-element.77) | copy-start | bytes 165892
  187.9 22.4 %all-to-all-start = ((f32[16,136,128]{2,1,0:T(8,128)}), f32[16,136,128]{2,1,0:T(8,128)S(1)}, u32[]{:S(2)}, u32[]{:S(2)}) async-start(f32[16,136,128]{2,1,0:T(8,128)} %bitcast_add_fusion), calls=%async_computation | async-start | bytes 2228224 | tf_op jit(solution)/shard_map/all_to_all | solution.py:44
  193.7 33.0 %copy-start.7 = (f32[3,6,16,128]{3,2,1,0:T(8,128)S(1)}, f32[3,6,16,128]{3,2,1,0:T(8,128)}, u32[]{:S(2)}) copy-start(f32[3,6,16,128]{3,2,1,0:T(8,128)} %copy-done.6) | copy-start | bytes 442372
  211.0 17.7 %all-to-all-start.1 = ((f32[16,9,128]{2,1,0:T(8,128)}), f32[16,9,128]{2,1,0:T(8,128)S(1)}, u32[]{:S(2)}, u32[]{:S(2)}) async-start(f32[16,9,128]{2,1,0:T(8,128)} %reshape.308), calls=%async_computation.1 | async-start | bytes 262144 | tf_op jit(solution)/shard_map/all_to_all | solution.py:46
  216.6 20.5 %copy-start.3 = (f32[6,4,4,4,1,4,32]{6,5,3,2,1,0,4:T(4,128)S(1)}, f32[6,4,4,4,1,4,32]{6,5,3,2,1,0,4:T(4,128)}, u32[]{:S(2)}) copy-start(f32[6,4,4,4,1,4,32]{6,5,3,2,1,0,4:T(4,128)} %copy-done.2) | copy-start | bytes 589828
  217.3 25.0 %collective-permute-start.13 = (f32[3,1,18,128]{3,2,1,0:T(8,128)}, f32[3,1,18,128]{3,2,1,0:T(8,128)S(1)}, u32[]{:S(2)}, u32[]{:S(2)}) collective-permute-start(f32[3,1,18,128]{3,2,1,0:T(8,128)} %get-tuple-element.90), channel_id=1, source_target_pairs={{8,0},{16,8},{24,16},{32,24},{40,32},{48,40},{56,48},{64,56},{72,6... | collective-permute-start | bytes 82952 | tf_op jit(solution)/shard_map/ppermute | solution.py:65
  224.5 17.7 %collective-permute-start.12 = (f32[3,1,18,128]{3,2,1,0:T(8,128)}, f32[3,1,18,128]{3,2,1,0:T(8,128)S(1)}, u32[]{:S(2)}, u32[]{:S(2)}) collective-permute-start(f32[3,1,18,128]{3,2,1,0:T(8,128)} %get-tuple-element.89), channel_id=1, source_target_pairs={{0,8},{8,16},{16,24},{24,32},{32,40},{40,48},{48,56},{56,64},{64,7... | collective-permute-start | bytes 82952 | tf_op jit(solution)/shard_map/ppermute | solution.py:62
  229.4 21.5 %all-to-all-start.2 = ((f32[16,9,128]{2,1,0:T(8,128)}), f32[16,9,128]{2,1,0:T(8,128)}, u32[]{:S(2)}, u32[]{:S(2)}) async-start(f32[16,9,128]{2,1,0:T(8,128)} %broadcast_in_dim.7), calls=%async_computation.2 | async-start | bytes 262144 | tf_op jit(solution)/shard_map/all_to_all | solution.py:47
  242.3 20.5 %collective-permute-start.15 = (f32[3,8,1,128]{3,2,1,0:T(1,128)S(1)}, f32[3,8,1,128]{3,2,1,0:T(1,128)S(1)}, u32[]{:S(2)}, u32[]{:S(2)}) collective-permute-start(f32[3,8,1,128]{3,2,1,0:T(1,128)S(1)} %get-tuple-element.107), channel_id=1, source_target_pairs={{1,0},{2,1},{3,2},{4,3},{5,4},{6,5},{7,6},{0,7},{9,8},{10,9},{11,1... | collective-permute-start | bytes 36872 | tf_op jit(solution)/shard_map/ppermute | solution.py:65
  246.7 16.1 %collective-permute-start.14 = (f32[3,8,1,128]{3,2,1,0:T(1,128)S(1)}, f32[3,8,1,128]{3,2,1,0:T(1,128)S(1)}, u32[]{:S(2)}, u32[]{:S(2)}) collective-permute-start(f32[3,8,1,128]{3,2,1,0:T(1,128)S(1)} %get-tuple-element.106), channel_id=1, source_target_pairs={{0,1},{1,2},{2,3},{3,4},{4,5},{5,6},{6,7},{7,0},{8,9},{9,10},{10,1... | collective-permute-start | bytes 36872 | tf_op jit(solution)/shard_map/ppermute | solution.py:62
  252.9 25.0 %all-to-all-start.3 = ((f32[16,136,128]{2,1,0:T(8,128)}), f32[16,136,128]{2,1,0:T(8,128)S(1)}, u32[]{:S(2)}, u32[]{:S(2)}) async-start(f32[16,136,128]{2,1,0:T(8,128)} %broadcast_in_dim.8), calls=%async_computation.3 | async-start | bytes 2228224 | tf_op jit(solution)/shard_map/all_to_all | solution.py:49
  262.8 4.4 %copy-start.11 = (f32[6,4,16,128]{3,2,1,0:T(8,128)S(1)}, f32[6,4,16,128]{3,2,1,0:T(8,128)}, u32[]{:S(2)}) copy-start(f32[6,4,16,128]{3,2,1,0:T(8,128)} %copy-done.10) | copy-start | bytes 589828
  262.8 28.7 %copy-start.20 = (f32[4,16,128]{2,1,0:T(8,128)S(1)}, f32[4,16,128]{2,1,0:T(8,128)}, u32[]{:S(2)}) copy-start(f32[4,16,128]{2,1,0:T(8,128)} %copy-done.19) | copy-start | bytes 98308
  262.8 28.7 %copy-start.25 = (f32[3,1,16,128]{3,2,1,0:T(8,128)S(1)}, f32[3,1,16,128]{3,2,1,0:T(8,128)}, u32[]{:S(2)}) copy-start(f32[3,1,16,128]{3,2,1,0:T(8,128)} %copy-done.24) | copy-start | bytes 73732
  262.8 28.7 %copy-start.27 = (f32[3,1,16,128]{3,2,1,0:T(8,128)S(1)}, f32[3,1,16,128]{3,2,1,0:T(8,128)}, u32[]{:S(2)}) copy-start(f32[3,1,16,128]{3,2,1,0:T(8,128)} %copy-done.26) | copy-start | bytes 73732
  262.8 28.7 %copy-start.28 = (f32[4,16,128]{2,1,0:T(8,128)S(1)}, f32[4,16,128]{2,1,0:T(8,128)}, u32[]{:S(2)}) copy-start(f32[4,16,128]{2,1,0:T(8,128)} %get-tuple-element.119) | copy-start | bytes 98308
  277.9 19.7 %collective-permute-start.17 = (f32[16,136,128]{2,1,0:T(8,128)S(1)}, f32[16,136,128]{2,1,0:T(8,128)S(1)}, u32[]{:S(2)}, u32[]{:S(2)}) collective-permute-start(f32[16,136,128]{2,1,0:T(8,128)S(1)} %all-to-all-done.3), channel_id=1, source_target_pairs={{0,1},{1,0},{2,3},{3,2},{4,5},{5,4},{6,7},{7,6},{8,9},{9,8},{10,11... | collective-permute-start | bytes 3342344 | tf_op jit(solution)/shard_map/ppermute | solution.py:50
  285.9 7.5 %collective-permute-start.7 = (f32[6,6,1,128]{3,2,1,0:T(1,128)S(1)}, f32[6,6,1,128]{3,2,1,0:T(1,128)S(1)}, u32[]{:S(2)}, u32[]{:S(2)}) collective-permute-start(f32[6,6,1,128]{3,2,1,0:T(1,128)S(1)} %get-tuple-element.109), channel_id=1, source_target_pairs={{1,0},{2,1},{3,2},{4,3},{5,4},{6,5},{7,6},{0,7},{9,8},{10,9},{11,1... | collective-permute-start | bytes 55304 | tf_op jit(solution)/shard_map/ppermute | solution.py:65
  287.8 6.2 %collective-permute-start.6 = (f32[6,6,1,128]{3,2,1,0:T(1,128)S(1)}, f32[6,6,1,128]{3,2,1,0:T(1,128)S(1)}, u32[]{:S(2)}, u32[]{:S(2)}) collective-permute-start(f32[6,6,1,128]{3,2,1,0:T(1,128)S(1)} %get-tuple-element.108), channel_id=1, source_target_pairs={{0,1},{1,2},{2,3},{3,4},{4,5},{5,6},{6,7},{7,0},{8,9},{9,10},{10,1... | collective-permute-start | bytes 55304 | tf_op jit(solution)/shard_map/ppermute | solution.py:62
  293.4 2.2 copy-start.18
  293.4 2.2 copy-start.21
  293.4 2.2 copy-start.36
  293.4 2.2 copy-start.38
  (19 other events, 21.9 us)

commit v2 on v0

v2 whole, which is shorter than its diff:
```python
import jax
import jax.numpy as jnp
import numpy as np
from jax import lax
from jax.experimental import pallas as pl
from jax.experimental.pallas import tpu as pltpu
from jax.sharding import Mesh, PartitionSpec as P

time_step = 0.25
viscosity = 0.2
penalty_eta = 0.05

GX = ("zh", "x", "y")
GY = ("zl", "core")
FLAT = 4352
HALF = FLAT // 2
WIN_ROWS = 648
WOUT_BASE = 4 * WIN_ROWS
BIAS_BASE = WOUT_BASE + 3 * 512
F32 = jnp.float32
BF16 = jnp.bfloat16


def selector():
    table = np.zeros((4, 128, 6, 4, 32), np.float32)
    for offset in range(6):
        for block in range(32):
            z = 4 * block + offset - 1
            if 0 <= z < 128:
                for row in range(4):
                    table[row, z, offset, row, block] = 1.0
    return table.reshape(512, 768).astype(jnp.bfloat16)


def z_next(field):
    lane = lax.broadcasted_iota(jnp.int32, field.shape, field.ndim - 1)
    return jnp.where(lane < 127, pltpu.roll(field, 127, field.ndim - 1), 0.0)


def z_before(field):
    lane = lax.broadcasted_iota(jnp.int32, field.shape, field.ndim - 1)
    return jnp.where(lane > 0, pltpu.roll(field, 1, field.ndim - 1), 0.0)


def split(value):
    high = value.astype(BF16)
    low = (value - high.astype(F32)).astype(BF16)
    return high, low


def dot(left, right, left_dim, right_dim):
    return lax.dot_general(
        left, right, (((left_dim,), (right_dim,)), ((), ())), preferred_element_type=F32
    )


def damping(canopy):
    return 1.0 + time_step * canopy.astype(F32) / penalty_eta


def start_kernel(v_ref, canopy_ref, cot_ref, direct_ref, m1_ref, m2_ref):
    core = lax.axis_index("core")
    factor = damping(canopy_ref[...])
    for i in range(3):
        direct_ref[i] = cot_ref[i].astype(F32) / factor
    for out, row in ((m1_ref, 15 * (1 - core)), (m2_ref, 15 * core)):
        for i in range(3):
            for x in range(4):
                out[pl.ds(i * 4 + x, 1), :] = v_ref[i, x, pl.ds(row, 1), :]
                out[pl.ds(12 + i * 4 + x, 1), :] = (
                    direct_ref[i, x, pl.ds(row, 1), :] * time_step
                )


def layer_kernel(v_ref, direct_ref, r1_ref, r2_ref, m1_ref, m2_ref):
    core = lax.axis_index("core")
    parity = lax.rem(lax.axis_index("y"), 2)
    for out, x in ((m1_ref, 3 * (1 - parity)), (m2_ref, 3 * parity)):
        for k in range(6):
            out[k, 16:24, :] = jnp.zeros((8, 128), F32)
            if k < 3:
                out[k, 1:17, :] = v_ref[k, x]
            else:
                out[k, 1:17, :] = direct_ref[k - 3, x] * time_step
            row1 = r1_ref[pl.ds(k * 4 + x, 1), :]
            row2 = r2_ref[pl.ds(k * 4 + x, 1), :]
            out[k, 0:1, :] = jnp.where(core == 0, row2, row1)
            out[k, 17:18, :] = jnp.where(core == 0, row1, row2)


def main_kernel(
    v_ref, direct_ref, r1_ref, r2_ref, x1_ref, x2_ref,
    win_ref, bin_ref, wout_ref, bout_ref, sel_ref,
    keep_ref, send_ref, nv_ref, vg_ref, m1_ref, m2_ref, ylow_ref, yhigh_ref,
    ext, sgrad, cols, rows, cgrad, cpad, opad, ghost, tau, flat,
):
    core = lax.axis_index("core")
    parity = lax.rem(lax.axis_index("y"), 2)

    for k in range(6):
        ext[k * 6] = jnp.where(parity == 0, x2_ref[k], x1_ref[k])
        ext[k * 6 + 5] = jnp.where(parity == 0, x1_ref[k], x2_ref[k])
        for x in range(4):
            spot = k * 6 + 1 + x
            ext[spot, 16:24, :] = jnp.zeros((8, 128), F32)
            ext[spot, 1:17, :] = v_ref[k, x] if k < 3 else direct_ref[k - 3, x] * time_step
            row1 = r1_ref[k * 4 + x : k * 4 + x + 1, :]
            row2 = r2_ref[k * 4 + x : k * 4 + x + 1, :]
            ext[spot, 0:1, :] = jnp.where(core == 0, row2, row1)
            ext[spot, 17:18, :] = jnp.where(core == 0, row1, row2)

    def at(k, dx, dy):
        return ext[k * 6 + 1 + dx : k * 6 + 5 + dx, 1 + dy : 17 + dy, :]

    def laplace(k):
        middle = at(k, 0, 0)
        total = at(k, 1, 0) + at(k, -1, 0) + at(k, 0, 1) + at(k, 0, -1)
        return total + z_next(middle) + z_before(middle) - 6.0 * middle

    grad_x = [(at(3 + i, 1, 0) - at(3 + i, -1, 0)) * 0.5 for i in range(3)]
    grad_y = [(at(3 + i, 0, 1) - at(3 + i, 0, -1)) * 0.5 for i in range(3)]
    grad_z = [(z_next(at(3 + i, 0, 0)) - z_before(at(3 + i, 0, 0))) * 0.5 for i in range(3)]
    stress_grad = (
        grad_x[0],
        grad_y[1],
        grad_z[2],
        grad_y[0] + grad_x[1],
        grad_z[0] + grad_x[2],
        grad_z[1] + grad_y[2],
    )
    sgrad[:, 16:24, :] = jnp.zeros((24, 8, 128), F32)
    for s in range(6):
        sgrad[s * 4 : s * 4 + 4, 0:16, :] = -stress_grad[s]
    for j in range(3):
        velocity = [at(i, 0, 0) for i in range(3)]
        slope = (grad_x, grad_y, grad_z)[j]
        total = direct_ref[j] + viscosity * laplace(3 + j)
        total = total + slope[0] * velocity[0] + slope[1] * velocity[1] + slope[2] * velocity[2]
        total = total + grad_x[j] * velocity[0] + grad_y[j] * velocity[1] + grad_z[j] * velocity[2]
        vg_ref[j] = total

    selection = sel_ref[...]
    inner = sel_ref[:, 128:640]

    parts = [sgrad[:, 4 * b : 4 * b + 8, :].reshape(192, 128) for b in range(4)]
    high, low = split(jnp.concatenate(parts, axis=1))
    picked = dot(high, inner, 1, 0) + dot(low, inner, 1, 0)
    for sa in range(24):
        for c in range(4):
            rows[pl.ds(sa * 16 + c, 4, stride=4), :] = picked[
                sa * 8 : sa * 8 + 4, c * 128 : c * 128 + 128
            ]
    rows_t = rows[...].T
    rows_low = rows_t.astype(BF16)
    bias_out_sum = jnp.sum(rows_t, axis=0, keepdims=True)

    parts = [
        ext[0:18, 4 * b : 4 * b + 8, :].reshape(144, 128).astype(BF16) for b in range(4)
    ]
    picked = dot(jnp.concatenate(parts, axis=1), selection, 1, 0)
    for g in range(18):
        for z in range(6):
            cols[pl.ds(g * 36 + z, 6, stride=6), :] = picked[
                g * 8 : g * 8 + 6, z * 128 : z * 128 + 128
            ]
    columns = cols[...].astype(BF16)

    pre_act = dot(columns, win_ref[...], 0, 0) + bin_ref[...]
    sigmoid_pre = jax.nn.sigmoid(pre_act)
    hidden = (pre_act * sigmoid_pre).astype(BF16)
    hidden_grad = dot(rows_low, wout_ref[...], 1, 1)
    pre_grad = hidden_grad * (sigmoid_pre * (1.0 + pre_act * (1.0 - sigmoid_pre)))
    pre_low = pre_grad.astype(BF16)
    bias_in_sum = jnp.sum(pre_grad, axis=0, keepdims=True)

    weight_in_sum = dot(columns, pre_low, 1, 0)
    for q in range(4):
        flat[q * WIN_ROWS : (q + 1) * WIN_ROWS, :] = weight_in_sum[:, q * 128 : q * 128 + 128]
    weight_out_sum = dot(hidden, rows_low, 0, 0)
    for q in range(3):
        flat[WOUT_BASE + q * 512 : WOUT_BASE + q * 512 + 512, :] = weight_out_sum[
            :, q * 128 : q * 128 + 128
        ]
    flat[BIAS_BASE:FLAT, :] = jnp.zeros((FLAT - BIAS_BASE, 128), F32)
    for q in range(4):
        flat[BIAS_BASE + q : BIAS_BASE + q + 1, :] = bias_in_sum[:, q * 128 : q * 128 + 128]
    for q in range(3):
        flat[BIAS_BASE + 4 + q : BIAS_BASE + 5 + q, :] = bias_out_sum[:, q * 128 : q * 128 + 128]
    keep_ref[...] = flat[pl.ds(pl.multiple_of(core * HALF, 8), HALF), :]
    send_ref[...] = flat[pl.ds(pl.multiple_of((1 - core) * HALF, 8), HALF), :]

    cgrad[...] = dot(win_ref[...], pre_low, 1, 1)
    for g in range(18):
        for z in range(6):
            cpad[g * 8 : g * 8 + 6, z * 128 : z * 128 + 128] = cgrad[
                pl.ds(g * 36 + z, 6, stride=6), :
            ]
            cpad[g * 8 + 6 : g * 8 + 8, z * 128 : z * 128 + 128] = jnp.zeros((2, 128), F32)
    high, low = split(cpad[...])
    spread = dot(high, selection, 1, 1) + dot(low, selection, 1, 1)
    spread = spread.reshape(18, 8, 512)
    ghost[...] = jnp.zeros((18, 24, 128), F32)
    for b in range(4):
        ghost[:, 4 * b : 4 * b + 8, :] += spread[:, :, b * 128 : b * 128 + 128]
    for j in range(3):
        vg_ref[j] += ghost[j * 6 + 1 : j * 6 + 5, 1:17, :]

    outputs = dot(hidden, wout_ref[...], 1, 0) + bout_ref[...]
    rows[...] = outputs.T
    for sa in range(24):
        for c in range(4):
            opad[sa * 8 : sa * 8 + 4, c * 128 : c * 128 + 128] = rows[
                pl.ds(sa * 16 + c, 4, stride=4), :
            ]
            opad[sa * 8 + 4 : sa * 8 + 8, c * 128 : c * 128 + 128] = jnp.zeros((4, 128), F32)
    high, low = split(opad[...])
    spread = dot(high, inner, 1, 1) + dot(low, inner, 1, 1)
    spread = spread.reshape(24, 8, 512)
    tau[:, 0:8, :] = jnp.zeros((24, 8, 128), F32)
    tau[:, 24:32, :] = jnp.zeros((24, 8, 128), F32)
    for b in range(4):
        tau[:, 8 + 4 * b : 12 + 4 * b, :] = spread[:, 0:4, b * 128 : b * 128 + 128]

    blank = jnp.zeros((1, 16, 128), F32)
    for i, (along_x, along_y, along_z) in enumerate(((0, 3, 4), (3, 1, 5), (4, 5, 2))):
        inside = tau[along_x * 4 : along_x * 4 + 4, 8:24, :]
        force = jnp.concatenate([inside[1:4], blank]) - jnp.concatenate([blank, inside[0:3]])
        force = force + tau[along_y * 4 : along_y * 4 + 4, 9:25, :]
        force = force - tau[along_y * 4 : along_y * 4 + 4, 7:23, :]
        inside = tau[along_z * 4 : along_z * 4 + 4, 8:24, :]
        force = (force + z_next(inside) - z_before(inside)) * 0.5
        product = at(2, 0, 0) * at(i, 0, 0)
        flow = at(0, 1, 0) * at(i, 1, 0) - at(0, -1, 0) * at(i, -1, 0)
        flow = flow + at(1, 0, 1) * at(i, 0, 1) - at(1, 0, -1) * at(i, 0, -1)
        flow = (flow + z_next(product) - z_before(product)) * 0.5
        nv_ref[i] = at(i, 0, 0) + time_step * (viscosity * laplace(i) - flow + force)

    for out, side in ((m1_ref, 1 - parity), (m2_ref, parity)):
        for j, s in enumerate((0, 3, 4)):
            out[j, 0:16, :] = tau[s * 4 + 3 * side, 8:24, :]
            out[j, 16:24, :] = jnp.zeros((8, 128), F32)
            out[3 + j] = ghost[j * 6 + 5 * side]
    for j, s in enumerate((3, 1, 5)):
        for x in range(4):
            spot = j * 4 + x
            ylow_ref[spot : spot + 1, :] = tau[s * 4 + x, 8:9, :]
            yhigh_ref[spot : spot + 1, :] = tau[s * 4 + x, 23:24, :]
            ylow_ref[12 + spot : 13 + spot, :] = ghost[j * 6 + 1 + x, 0:1, :]
            yhigh_ref[12 + spot : 13 + spot, :] = ghost[j * 6 + 1 + x, 17:18, :]


def side_kernel(x1_ref, x2_ref, ylow_ref, yhigh_ref, m1_ref, m2_ref, low, high):
    core = lax.axis_index("core")
    parity = lax.rem(lax.axis_index("y"), 2)
    low[...] = ylow_ref[...]
    high[...] = yhigh_ref[...]
    for j in range(3):
        from_low = jnp.where(parity == 0, x2_ref[3 + j], x1_ref[3 + j])
        from_high = jnp.where(parity == 0, x1_ref[3 + j], x2_ref[3 + j])
        first, last = 12 + j * 4, 15 + j * 4
        low[first : first + 1, :] += from_low[0:1]
        low[last : last + 1, :] += from_high[0:1]
        high[first : first + 1, :] += from_low[17:18]
        high[last : last + 1, :] += from_high[17:18]
    m1_ref[...] = jnp.where(core == 0, high[...], low[...])
    m2_ref[...] = jnp.where(core == 0, low[...], high[...])


def end_kernel(
    nv_ref, vg_ref, canopy_ref, x1_ref, x2_ref, y1_ref, y2_ref, new_ref, grad_ref, part
):
    core = lax.axis_index("core")
    parity = lax.rem(lax.axis_index("y"), 2)
    factor = damping(canopy_ref[...])
    y_low = jnp.where(core == 0, y2_ref[...], y1_ref[...])
    y_high = jnp.where(core == 0, y1_ref[...], y2_ref[...])
    step = time_step * 0.5
    for i in range(3):
        part[...] = nv_ref[i]
        part[0] -= step * jnp.where(parity == 0, x2_ref[i, 0:16, :], x1_ref[i, 0:16, :])
        part[3] += step * jnp.where(parity == 0, x1_ref[i, 0:16, :], x2_ref[i, 0:16, :])
        for x in range(4):
            spot = i * 4 + x
            part[x, 0:1, :] -= step * y_low[spot : spot + 1]
            part[x, 15:16, :] += step * y_high[spot : spot + 1]
        new_ref[i] = part[...] / factor
        part[...] = vg_ref[i]
        part[0] += jnp.where(parity == 0, x2_ref[3 + i, 1:17, :], x1_ref[3 + i, 1:17, :])
        part[3] += jnp.where(parity == 0, x1_ref[3 + i, 1:17, :], x2_ref[3 + i, 1:17, :])
        for x in range(4):
            spot = 12 + i * 4 + x
            part[x, 0:1, :] += y_low[spot : spot + 1]
            part[x, 15:16, :] += y_high[spot : spot + 1]
        grad_ref[i] = part[...]


def weights_kernel(scale, mine_ref, other_ref, win_ref, bin_ref, wout_ref, bout_ref):
    core = lax.axis_index("core")

    def put(out, lanes, start, count, first, second):
        done = 0
        while done < count:
            spot = start + done
            source, spot, room = (
                (first, spot, HALF - spot) if spot < HALF else (second, spot - HALF, count)
            )
            size = min(count - done, room)
            out[done : done + size, lanes * 128 : lanes * 128 + 128] = (
                source[spot : spot + size, :] * scale
            )
            done += size

    def write(first, second):
        for q in range(4):
            put(win_ref, q, q * WIN_ROWS, WIN_ROWS, first, second)
            put(bin_ref, q, BIAS_BASE + q, 1, first, second)
        for q in range(3):
            put(wout_ref, q, WOUT_BASE + q * 512, 512, first, second)
            put(bout_ref, q, BIAS_BASE + 4 + q, 1, first, second)

    @pl.when(core == 0)
    def _():
        write(mine_ref, other_ref)

    @pl.when(core == 1)
    def _():
        write(other_ref, mine_ref)


def call(kernel, outs, scratch=()):
    return pl.pallas_call(
        kernel,
        out_shape=[jax.ShapeDtypeStruct(shape, F32) for shape in outs],
        scratch_shapes=[pltpu.VMEM(shape, F32) for shape in scratch],
        compiler_params=pltpu.CompilerParams(vmem_limit_bytes=48 * 1024 * 1024),
    )


def pairs(axes):
    count = lax.axis_size(axes)
    inner = [(i, i ^ 1) for i in range(count)]
    outer = [(i, (i + 1) % count if i % 2 else (i - 1) % count) for i in range(count)]
    return inner, outer


def exchange(first, second, axes):
    inner, outer = pairs(axes)
    return lax.ppermute(first, axes, inner), lax.ppermute(second, axes, outer)


def sum_everywhere(keep, send):
    across, along = ("x", "y"), ("zh", "zl")
    swap = [(0, 1), (1, 0)]
    parts = lax.axis_size(across)
    depth = lax.axis_size(along)
    count = HALF // parts
    short = -(-count // depth)
    half = (keep + lax.ppermute(send, "core", swap)).reshape(parts, count, 128)
    part = jnp.sum(lax.all_to_all(half, across, 0, 0), axis=0)
    part = jnp.pad(part, ((0, short * depth - count), (0, 0))).reshape(depth, short, 128)
    piece = jnp.sum(lax.all_to_all(part, along, 0, 0), axis=0)
    part = lax.all_to_all(jnp.broadcast_to(piece, part.shape), along, 0, 0)
    part = part.reshape(short * depth, 128)[:count]
    half = lax.all_to_all(jnp.broadcast_to(part, half.shape), across, 0, 0)
    half = half.reshape(HALF, 128)
    return half, lax.ppermute(half, "core", swap)


def on_device(velocity, canopy, weight_in, bias_in, weight_out, bias_out, cotangent):
    field = (3, 4, 16, 128)
    rows = (24, 128)
    layers = (6, 24, 128)
    direct, m1, m2 = call(start_kernel, (field, rows, rows))(velocity, canopy, cotangent)
    y1, y2 = exchange(m1, m2, GY)
    m1, m2 = call(layer_kernel, (layers, layers))(velocity, direct, y1, y2)
    x1, x2 = exchange(m1, m2, GX)
    keep, send, nv, vg, m1, m2, ylow, yhigh = call(
        main_kernel,
        ((HALF, 128), (HALF, 128), field, field, layers, layers, rows, rows),
        (
            (36, 24, 128),
            (24, 24, 128),
            (648, 128),
            (384, 128),
            (648, 128),
            (144, 768),
            (192, 512),
            (18, 24, 128),
            (24, 32, 128),
            (FLAT, 128),
        ),
    )(
        velocity, direct, y1, y2, x1, x2,
        weight_in, bias_in[None], weight_out, bias_out[None], jnp.asarray(selector()),
    )
    x1, x2 = exchange(m1, m2, GX)
    m1, m2 = call(side_kernel, (rows, rows), (rows, rows))(x1, x2, ylow, yhigh)
    y1, y2 = exchange(m1, m2, GY)
    new_velocity, velocity_grad = call(end_kernel, (field, field), ((4, 16, 128),))(
        nv, vg, canopy, x1, x2, y1, y2
    )
    mine, other = sum_everywhere(keep, send)
    blocks = 128 * lax.axis_size(GX) * lax.axis_size(GY)
    scale = float(blocks) ** -0.5
    weight_in_grad, bias_in_grad, weight_out_grad, bias_out_grad = call(
        lambda *refs: weights_kernel(scale, *refs), ((648, 512), (1, 512), (512, 384), (1, 384))
    )(mine, other)
    return (
        new_velocity,
        velocity_grad,
        weight_in_grad,
        bias_in_grad[0],
        weight_out_grad,
        bias_out_grad[0],
    )


def solution(mesh):
    if mesh.devices.size == 512:
        mesh = Mesh(mesh.devices.reshape(4, 4, 4, 4, 2), GX + GY)
    placed = (
        P(None, GX, GY, None),
        P(GX, GY, None),
        P(),
        P(),
        P(),
        P(),
        P(None, GX, GY, None),
    )
    return jax.shard_map(
        on_device,
        mesh=mesh,
        in_specs=placed,
        out_specs=(P(None, GX, GY, None), P(None, GX, GY, None), P(), P(), P(), P()),
        check_vma=False,
    )
```

time: 784 us -> 167 us (0.21)
  waiting for transfers between devices: 440 us -> 16.8 us
  local copies, waits for them, and re-layouts: 104 us -> 7.15 us
  other arithmetic: 31.5 us -> 0.79 us
  blocking collectives: 105 us -> 78.7 us
  starting transfers between devices: 78.4 us -> 54.4 us
  between operations: 15.1 us -> 0.82 us
  matrix products: 8.03 us -> 0 us
    psum x1 -> x0, waiting for transfers between devices: 440 us -> none  [on_device(): totals = lax.psum((w_in_s, b_in_s, w_out_s, b_out_s), ('gx', 'gy'))]
    psum x1 -> x0, blocking collectives: 105 us -> none  [on_device(): totals = lax.psum((w_in_s, b_in_s, w_out_s, b_out_s), ('gx', 'gy'))]
    all_to_all x0 -> x4, blocking collectives: none -> 78.7 us  [the longest x1 25.2 us: sum_everywhere(): piece = jnp.sum(lax.all_to_all(part, along, 0, 0), axis=0)]
    slice x32 -> x1, local copies, waits for them, and re-layouts: 40.7 us -> 0.01 us  [sum_everywhere(): part = part.reshape(short * depth, 128)[:count]]
    another operation x26 -> x0, local copies, waits for them, and re-layouts: 30 us -> none  [the longest x13 15.1 us: stress_from_slopes(): jnp.stack([grad_x[0], grad_y[1], grad_z[2], grad_y[0] + grad_x[1], grad_z...]
    ppermute x16 -> x10, starting transfers between devices: 78.4 us -> 54.4 us  [the longest x8 40.2 us: exchange(): return (lax.ppermute(first, axes, inner), lax.ppermute(second, axes, outer))]
    reshape x8 -> x2, local copies, waits for them, and re-layouts: 21.9 us -> 0.02 us  [the longest x1 0.01 us: sum_everywhere(): jnp.pad(part, ((0, short * depth - count), (0, 0)))]
    ppermute x16 -> x10, waiting for transfers between devices: 0.19 us -> 16.8 us  [the longest x8 14.4 us: exchange(): return (lax.ppermute(first, axes, inner), lax.ppermute(second, axes, outer))]
  transfers between devices with their start and end apart: 17 -> 10, of which waited for: 2 -> 5; matrix products, arithmetic and copies ran while one was open for 10% -> 0% of each run, Pallas kernels for 0% -> 0%
where the time goes in v2:
time: 167 us; the launch traced here: 164 us
  blocking collectives  78.7 us (47%)
  starting transfers between devices  54.4 us (33%)
  waiting for transfers between devices  16.8 us (10%)
  local copies, waits for them, and re-layouts  7.15 us (4%)
  Pallas kernels  5.79 us (3%)
    ppermute x8, starting transfers between devices, exchange(): return (lax.ppermute(first, axes, inner), lax.ppermute(second, axes, outer))  40.2 us
    all_to_all x1, blocking collectives, sum_everywhere(): piece = jnp.sum(lax.all_to_all(part, along, 0, 0), axis=0)  25.2 us
    all_to_all x1, blocking collectives, sum_everywhere(): part = jnp.sum(lax.all_to_all(half, across, 0, 0), axis=0)  20 us
    all_to_all x1, blocking collectives, sum_everywhere(): part = lax.all_to_all(jnp.broadcast_to(piece, part.shape), along, 0, 0)  16.9 us
    all_to_all x1, blocking collectives, sum_everywhere(): half = lax.all_to_all(jnp.broadcast_to(part, half.shape), across, 0, 0)  16.5 us
    ppermute x8, waiting for transfers between devices, exchange(): return (lax.ppermute(first, axes, inner), lax.ppermute(second, axes, outer))  14.4 us
    ppermute x1, starting transfers between devices, sum_everywhere(): return (half, lax.ppermute(half, 'core', swap))  7.26 us
    ppermute x1, starting transfers between devices, sum_everywhere(): half = (keep + lax.ppermute(send, 'core', swap)).reshape(parts, count, 128)  6.94 us
  transfers between devices with their start and end apart: 10, of which 5 were waited for; matrix products, arithmetic and copies ran while one was open for 0% of the time, Pallas kernels for 0%

profile of v2, /device:TPU:1, one launch (start us, length us, event | category | flops | bytes accessed | tf_op | source)
XLA Modules:
  0.0 164.4 jit_solution(10258641830706821022)
XLA Ops:
  0.6 0.0 copy-start
  0.6 0.9 copy-done
  1.5 0.0 copy-start.4
  1.5 0.8 copy-done.4
  2.3 0.0 copy-start.6
  2.3 0.8 copy-done.6
  3.1 8.8 %collective-permute-start = (f32[24,128]{1,0:T(8,128)S(1)}, f32[24,128]{1,0:T(8,128)S(1)}, u32[]{:S(2)}, u32[]{:S(2)}) collective-permute-start(f32[24,128]{1,0:T(8,128)S(1)} %get-tuple-element.28), channel_id=1, source_target_pairs={{0,1},{1,0},{2,3},{3,2},{4,5},{5,4},{6,7},{7,6},{8,9},{9,8},{10,11... | collective-permute-start | bytes 36872 | tf_op jit(solution)/shard_map/ppermute | solution.py:348
  11.9 1.9 %collective-permute-start.1 = (f32[24,128]{1,0:T(8,128)S(1)}, f32[24,128]{1,0:T(8,128)S(1)}, u32[]{:S(2)}, u32[]{:S(2)}) collective-permute-start(f32[24,128]{1,0:T(8,128)S(1)} %get-tuple-element.29), channel_id=1, source_target_pairs={{0,7},{1,2},{2,1},{3,4},{4,3},{5,6},{6,5},{7,0},{8,15},{9,10},{10,... | collective-permute-start | bytes 36872 | tf_op jit(solution)/shard_map/ppermute | solution.py:348
  13.8 0.0 collective-permute-done.r1_ref
  13.9 3.1 %collective-permute-done.1.r2_ref = f32[24,128]{1,0:T(8,128)S(1)} collective-permute-done((f32[24,128]{1,0:T(8,128)S(1)}, f32[24,128]{1,0:T(8,128)S(1)}, u32[]{:S(2)}, u32[]{:S(2)}) %collective-permute-start.1) | collective-permute-done | bytes 12320 | tf_op jit(solution)/shard_map/ppermute | solution.py:348
  17.0 1.9 %collective-permute-start.2 = (f32[6,24,128]{2,1,0:T(8,128)S(1)}, f32[6,24,128]{2,1,0:T(8,128)S(1)}, u32[]{:S(2)}, u32[]{:S(2)}) collective-permute-start(f32[6,24,128]{2,1,0:T(8,128)S(1)} %get-tuple-element.30), channel_id=1, source_target_pairs={{0,8},{8,0},{16,24},{24,16},{32,40},{40,32},{48,56},{56,48},{64,72... | collective-permute-start | bytes 221192 | tf_op jit(solution)/shard_map/ppermute | solution.py:348
  18.9 12.2 %collective-permute-start.3 = (f32[6,24,128]{2,1,0:T(8,128)S(1)}, f32[6,24,128]{2,1,0:T(8,128)S(1)}, u32[]{:S(2)}, u32[]{:S(2)}) collective-permute-start(f32[6,24,128]{2,1,0:T(8,128)S(1)} %get-tuple-element.31), channel_id=1, source_target_pairs={{0,504},{8,16},{16,8},{24,32},{32,24},{40,48},{48,40},{56,64},{64,... | collective-permute-start | bytes 221192 | tf_op jit(solution)/shard_map/ppermute | solution.py:348
  31.1 0.7 broadcast_in_dim.13.bout_ref
  31.8 0.0 collective-permute-done.2.x1_ref
  31.8 1.5 collective-permute-done.3.x2_ref
  33.3 0.0 copy-start.1
  33.3 1.1 copy-done.1
  34.4 0.0 copy-start.2
  34.4 1.1 copy-done.2
  35.5 0.0 copy-start.3
  35.5 1.0 copy-done.3
  36.5 0.0 copy-start.7
  36.5 0.7 copy-done.7
  37.2 3.4 %shard_map.129 = (f32[2176,128]{1,0:T(8,128)S(1)}, f32[2176,128]{1,0:T(8,128)S(1)}, f32[3,4,16,128]{3,2,1,0:T(8,128)S(1)}, f32[3,4,16,128]{3,2,1,0:T(8,128)S(1)}...) custom-call(f32[3,4,16,128]{3,2,1,0:T(8,128)S(1)} %copy-done, ...), custom_call_target="tpu_custom_call" | custom-call | tf_op jit(solution)/shard_map/pallas_call | solution.py:377
  40.6 6.9 %collective-permute-start.8 = (f32[2176,128]{1,0:T(8,128)S(1)}, f32[2176,128]{1,0:T(8,128)S(1)}, u32[]{:S(2)}, u32[]{:S(2)}) collective-permute-start(f32[2176,128]{1,0:T(8,128)S(1)} %get-tuple-element.43), channel_id=1, source_target_pairs={{0,1},{1,0},{2,3},{3,2},{4,5},{5,4},{6,7},{7,6},{8,9},{9,8},{10,11... | collective-permute-start | bytes 3342344 | tf_op jit(solution)/shard_map/ppermute | solution.py:358
  47.5 2.4 %collective-permute-done.8 = f32[2176,128]{1,0:T(8,128)S(1)} collective-permute-done((f32[2176,128]{1,0:T(8,128)S(1)}, f32[2176,128]{1,0:T(8,128)S(1)}, u32[]{:S(2)}, u32[]{:S(2)}) %collective-permute-start.8) | collective-permute-done | bytes 1114144 | tf_op jit(solution)/shard_map/ppermute | solution.py:358
  49.9 0.1 add.5
  50.0 20.0 %all_to_all.20 = f32[16,136,128]{2,1,0:T(8,128)S(1)} all-to-all(f32[16,136,128]{2,1,0:T(8,128)S(1)} %bitcast.7), channel_id=1, replica_groups=mesh['zh'=4,'x'=4,'y'=4,'zl'=4,'core'=2] {'x','y'}, dimensions={0} | all-to-all | bytes 2228224 | tf_op jit(solution)/shard_map/all_to_all | solution.py:359
  69.9 0.1 reduce_sum.18
  70.0 25.2 %all_to_all.21 = f32[16,9,128]{2,1,0:T(8,128)S(1)} all-to-all(f32[16,9,128]{2,1,0:T(8,128)S(1)} %reshape.25), channel_id=1, replica_groups=mesh['zh'=4,'x'=4,'y'=4,'zl'=4,'core'=2] {'zh','zl'}, dimensions={0} | all-to-all | bytes 147456 | tf_op jit(solution)/shard_map/all_to_all | solution.py:361
  95.3 16.9 %all_to_all.22 = f32[16,9,128]{2,1,0:T(8,128)S(1)} all-to-all(f32[16,9,128]{2,1,0:T(8,128)S(1)} %broadcast_in_dim.14), channel_id=1, replica_groups=mesh['zh'=4,'x'=4,'y'=4,'zl'=4,'core'=2] {'zh','zl'}, dimensions={0} | all-to-all | bytes 147456 | tf_op jit(solution)/shard_map/all_to_all | solution.py:362
  112.3 0.1 broadcast_in_dim.15
  112.4 0.0 copy-start.5
  112.4 16.5 %all_to_all.23 = f32[16,136,128]{2,1,0:T(8,128)S(1)} all-to-all(f32[16,136,128]{2,1,0:T(8,128)S(1)} %broadcast_in_dim.15), channel_id=1, replica_groups=mesh['zh'=4,'x'=4,'y'=4,'zl'=4,'core'=2] {'x','y'}, dimensions={0} | all-to-all | bytes 2228224 | tf_op jit(solution)/shard_map/all_to_all | solution.py:364
  128.9 7.3 %collective-permute-start.9 = (f32[2176,128]{1,0:T(8,128)S(1)}, f32[2176,128]{1,0:T(8,128)S(1)}, u32[]{:S(2)}, u32[]{:S(2)}) collective-permute-start(f32[2176,128]{1,0:T(8,128)S(1)} %bitcast.4), channel_id=1, source_target_pairs={{0,1},{1,0},{2,3},{3,2},{4,5},{5,4},{6,7},{7,6},{8,9},{9,8},{10,11... | collective-permute-start | bytes 3342344 | tf_op jit(solution)/shard_map/ppermute | solution.py:366
  136.2 2.2 %collective-permute-start.4 = (f32[6,24,128]{2,1,0:T(8,128)S(1)}, f32[6,24,128]{2,1,0:T(8,128)S(1)}, u32[]{:S(2)}, u32[]{:S(2)}) collective-permute-start(f32[6,24,128]{2,1,0:T(8,128)S(1)} %get-tuple-element.34), channel_id=1, source_target_pairs={{0,8},{8,0},{16,24},{24,16},{32,40},{40,32},{48,56},{56,48},{64,72... | collective-permute-start | bytes 221192 | tf_op jit(solution)/shard_map/ppermute | solution.py:348
  138.4 5.1 %collective-permute-start.5 = (f32[6,24,128]{2,1,0:T(8,128)S(1)}, f32[6,24,128]{2,1,0:T(8,128)S(1)}, u32[]{:S(2)}, u32[]{:S(2)}) collective-permute-start(f32[6,24,128]{2,1,0:T(8,128)S(1)} %get-tuple-element.35), channel_id=1, source_target_pairs={{0,504},{8,16},{16,8},{24,32},{32,24},{40,48},{48,40},{56,64},{64,... | collective-permute-start | bytes 221192 | tf_op jit(solution)/shard_map/ppermute | solution.py:348
  143.5 0.0 collective-permute-done.4.x1_ref
  143.5 8.5 %collective-permute-done.5.x2_ref = f32[6,24,128]{2,1,0:T(8,128)S(1)} collective-permute-done((f32[6,24,128]{2,1,0:T(8,128)S(1)}, f32[6,24,128]{2,1,0:T(8,128)S(1)}, u32[]{:S(2)}, u32[]{:S(2)}) %collective-permute-start.5) | collective-permute-done | bytes 73760 | tf_op jit(solution)/shard_map/ppermute | solution.py:348
  152.0 3.6 %collective-permute-start.6 = (f32[24,128]{1,0:T(8,128)S(1)}, f32[24,128]{1,0:T(8,128)S(1)}, u32[]{:S(2)}, u32[]{:S(2)}) collective-permute-start(f32[24,128]{1,0:T(8,128)S(1)} %get-tuple-element.38), channel_id=1, source_target_pairs={{0,1},{1,0},{2,3},{3,2},{4,5},{5,4},{6,7},{7,6},{8,9},{9,8},{10,11... | collective-permute-start | bytes 36872 | tf_op jit(solution)/shard_map/ppermute | solution.py:348
  155.7 4.4 %collective-permute-start.7 = (f32[24,128]{1,0:T(8,128)S(1)}, f32[24,128]{1,0:T(8,128)S(1)}, u32[]{:S(2)}, u32[]{:S(2)}) collective-permute-start(f32[24,128]{1,0:T(8,128)S(1)} %get-tuple-element.39), channel_id=1, source_target_pairs={{0,7},{1,2},{2,1},{3,4},{4,3},{5,6},{6,5},{7,0},{8,15},{9,10},{10,... | collective-permute-start | bytes 36872 | tf_op jit(solution)/shard_map/ppermute | solution.py:348
  160.1 0.0 collective-permute-done.6.y1_ref
  160.1 1.4 collective-permute-done.7.y2_ref
  161.4 0.0 copy-done.5
  161.4 0.8 shard_map.131
  162.2 0.0 collective-permute-done.9.refs_1_
  162.2 1.6 shard_map.132
  163.8 0.6 reduce
  (9 shorter events, 0.2 us)
Async XLA Ops:
  0.6 0.9 copy-start
  1.5 0.8 copy-start.4
  2.3 0.8 copy-start.6
  3.1 10.7 %collective-permute-start = (f32[24,128]{1,0:T(8,128)S(1)}, f32[24,128]{1,0:T(8,128)S(1)}, u32[]{:S(2)}, u32[]{:S(2)}) collective-permute-start(f32[24,128]{1,0:T(8,128)S(1)} %get-tuple-element.28), channel_id=1, source_target_pairs={{0,1},{1,0},{2,3},{3,2},{4,5},{5,4},{6,7},{7,6},{8,9},{9,8},{10,11... | collective-permute-start | bytes 36872 | tf_op jit(solution)/shard_map/ppermute | solution.py:348
  11.9 5.0 %collective-permute-start.1 = (f32[24,128]{1,0:T(8,128)S(1)}, f32[24,128]{1,0:T(8,128)S(1)}, u32[]{:S(2)}, u32[]{:S(2)}) collective-permute-start(f32[24,128]{1,0:T(8,128)S(1)} %get-tuple-element.29), channel_id=1, source_target_pairs={{0,7},{1,2},{2,1},{3,4},{4,3},{5,6},{6,5},{7,0},{8,15},{9,10},{10,... | collective-permute-start | bytes 36872 | tf_op jit(solution)/shard_map/ppermute | solution.py:348
  17.0 14.8 %collective-permute-start.2 = (f32[6,24,128]{2,1,0:T(8,128)S(1)}, f32[6,24,128]{2,1,0:T(8,128)S(1)}, u32[]{:S(2)}, u32[]{:S(2)}) collective-permute-start(f32[6,24,128]{2,1,0:T(8,128)S(1)} %get-tuple-element.30), channel_id=1, source_target_pairs={{0,8},{8,0},{16,24},{24,16},{32,40},{40,32},{48,56},{56,48},{64,72... | collective-permute-start | bytes 221192 | tf_op jit(solution)/shard_map/ppermute | solution.py:348
  18.9 14.4 %collective-permute-start.3 = (f32[6,24,128]{2,1,0:T(8,128)S(1)}, f32[6,24,128]{2,1,0:T(8,128)S(1)}, u32[]{:S(2)}, u32[]{:S(2)}) collective-permute-start(f32[6,24,128]{2,1,0:T(8,128)S(1)} %get-tuple-element.31), channel_id=1, source_target_pairs={{0,504},{8,16},{16,8},{24,32},{32,24},{40,48},{48,40},{56,64},{64,... | collective-permute-start | bytes 221192 | tf_op jit(solution)/shard_map/ppermute | solution.py:348
  33.3 1.1 copy-start.1
  34.4 1.1 copy-start.2
  35.5 1.0 copy-start.3
  36.5 0.7 copy-start.7
  40.6 9.3 %collective-permute-start.8 = (f32[2176,128]{1,0:T(8,128)S(1)}, f32[2176,128]{1,0:T(8,128)S(1)}, u32[]{:S(2)}, u32[]{:S(2)}) collective-permute-start(f32[2176,128]{1,0:T(8,128)S(1)} %get-tuple-element.43), channel_id=1, source_target_pairs={{0,1},{1,0},{2,3},{3,2},{4,5},{5,4},{6,7},{7,6},{8,9},{9,8},{10,11... | collective-permute-start | bytes 3342344 | tf_op jit(solution)/shard_map/ppermute | solution.py:358
  112.4 49.1 %copy-start.5 = (s32[4,16,128]{2,1,0:T(8,128)S(1)}, s32[4,16,128]{2,1,0:T(8,128)}, u32[]{:S(2)}) copy-start(s32[4,16,128]{2,1,0:T(8,128)} %canopy_ref.3) | copy-start | bytes 98308
  128.9 33.3 %collective-permute-start.9 = (f32[2176,128]{1,0:T(8,128)S(1)}, f32[2176,128]{1,0:T(8,128)S(1)}, u32[]{:S(2)}, u32[]{:S(2)}) collective-permute-start(f32[2176,128]{1,0:T(8,128)S(1)} %bitcast.4), channel_id=1, source_target_pairs={{0,1},{1,0},{2,3},{3,2},{4,5},{5,4},{6,7},{7,6},{8,9},{9,8},{10,11... | collective-permute-start | bytes 3342344 | tf_op jit(solution)/shard_map/ppermute | solution.py:366
  136.2 7.3 %collective-permute-start.4 = (f32[6,24,128]{2,1,0:T(8,128)S(1)}, f32[6,24,128]{2,1,0:T(8,128)S(1)}, u32[]{:S(2)}, u32[]{:S(2)}) collective-permute-start(f32[6,24,128]{2,1,0:T(8,128)S(1)} %get-tuple-element.34), channel_id=1, source_target_pairs={{0,8},{8,0},{16,24},{24,16},{32,40},{40,32},{48,56},{56,48},{64,72... | collective-permute-start | bytes 221192 | tf_op jit(solution)/shard_map/ppermute | solution.py:348
  138.4 13.6 %collective-permute-start.5 = (f32[6,24,128]{2,1,0:T(8,128)S(1)}, f32[6,24,128]{2,1,0:T(8,128)S(1)}, u32[]{:S(2)}, u32[]{:S(2)}) collective-permute-start(f32[6,24,128]{2,1,0:T(8,128)S(1)} %get-tuple-element.35), channel_id=1, source_target_pairs={{0,504},{8,16},{16,8},{24,32},{32,24},{40,48},{48,40},{56,64},{64,... | collective-permute-start | bytes 221192 | tf_op jit(solution)/shard_map/ppermute | solution.py:348
  152.0 8.1 %collective-permute-start.6 = (f32[24,128]{1,0:T(8,128)S(1)}, f32[24,128]{1,0:T(8,128)S(1)}, u32[]{:S(2)}, u32[]{:S(2)}) collective-permute-start(f32[24,128]{1,0:T(8,128)S(1)} %get-tuple-element.38), channel_id=1, source_target_pairs={{0,1},{1,0},{2,3},{3,2},{4,5},{5,4},{6,7},{7,6},{8,9},{9,8},{10,11... | collective-permute-start | bytes 36872 | tf_op jit(solution)/shard_map/ppermute | solution.py:348
  155.7 5.8 %collective-permute-start.7 = (f32[24,128]{1,0:T(8,128)S(1)}, f32[24,128]{1,0:T(8,128)S(1)}, u32[]{:S(2)}, u32[]{:S(2)}) collective-permute-start(f32[24,128]{1,0:T(8,128)S(1)} %get-tuple-element.39), channel_id=1, source_target_pairs={{0,7},{1,2},{2,1},{3,4},{4,3},{5,6},{6,5},{7,0},{8,15},{9,10},{10,... | collective-permute-start | bytes 36872 | tf_op jit(solution)/shard_map/ppermute | solution.py:348

commit v3 on v2

--- a/solution.py
+++ b/solution.py
@@ -58,9 +58,10 @@
     return 1.0 + time_step * canopy.astype(F32) / penalty_eta
 
 
-def start_kernel(v_ref, canopy_ref, cot_ref, direct_ref, m1_ref, m2_ref):
+def start_kernel(v_ref, canopy_ref, cot_ref, direct_ref, factor_ref, m1_ref, m2_ref):
     core = lax.axis_index("core")
     factor = damping(canopy_ref[...])
+    factor_ref[...] = factor
     for i in range(3):
         direct_ref[i] = cot_ref[i].astype(F32) / factor
     for out, row in ((m1_ref, 15 * (1 - core)), (m2_ref, 15 * core)):
@@ -70,6 +71,19 @@
                 out[pl.ds(12 + i * 4 + x, 1), :] = (
                     direct_ref[i, x, pl.ds(row, 1), :] * time_step
                 )
+
+
+def weights_in_kernel(after, win_hbm, wout_hbm, sel_hbm, win_ref, wout_ref, sel_ref, sems):
+    copies = [
+        pltpu.make_async_copy(source, target, sems.at[i])
+        for i, (source, target) in enumerate(
+            ((win_hbm, win_ref), (wout_hbm, wout_ref), (sel_hbm, sel_ref))
+        )
+    ]
+    for copy in copies:
+        copy.start()
+    for copy in copies:
+        copy.wait()
 
 
 def layer_kernel(v_ref, direct_ref, r1_ref, r2_ref, m1_ref, m2_ref):
@@ -267,11 +281,11 @@
 
 
 def end_kernel(
-    nv_ref, vg_ref, canopy_ref, x1_ref, x2_ref, y1_ref, y2_ref, new_ref, grad_ref, part
+    nv_ref, vg_ref, factor_ref, x1_ref, x2_ref, y1_ref, y2_ref, new_ref, grad_ref, done_ref, part
 ):
     core = lax.axis_index("core")
     parity = lax.rem(lax.axis_index("y"), 2)
-    factor = damping(canopy_ref[...])
+    factor = factor_ref[...]
     y_low = jnp.where(core == 0, y2_ref[...], y1_ref[...])
     y_high = jnp.where(core == 0, y1_ref[...], y2_ref[...])
     step = time_step * 0.5
@@ -292,6 +306,7 @@
             part[x, 0:1, :] += y_low[spot : spot + 1]
             part[x, 15:16, :] += y_high[spot : spot + 1]
         grad_ref[i] = part[...]
+    done_ref[...] = y_low[0:8]
 
 
 def weights_kernel(scale, mine_ref, other_ref, win_ref, bin_ref, wout_ref, bout_ref):
@@ -327,12 +342,51 @@
         write(other_ref, mine_ref)
 
 
-def call(kernel, outs, scratch=()):
+def across_kernel(got_ref, *rest):
+    out_ref, part = rest[-2:]
+    count = got_ref.shape[1]
+    depth, _, width = out_ref.shape
+    short = width // 128
+    part[...] = jnp.zeros(part.shape, F32)
+    part[0:count, :] = jnp.sum(got_ref[...], axis=0)
+    for i in range(depth):
+        for j in range(short):
+            out_ref[i, 0:1, j * 128 : j * 128 + 128] = part[i * short + j : i * short + j + 1, :]
+
+
+def along_kernel(got_ref, *rest):
+    out_ref = rest[-1]
+    total = jnp.sum(got_ref[...], axis=0, keepdims=True)
+    out_ref[...] = jnp.broadcast_to(total, out_ref.shape)
+
+
+def spread_kernel(got_ref, *rest):
+    out_ref, part = rest[-2:]
+    depth, _, width = got_ref.shape
+    short = width // 128
+    count = out_ref.shape[1]
+    for i in range(depth):
+        for j in range(short):
+            part[i * short + j : i * short + j + 1, :] = got_ref[i, 0:1, j * 128 : j * 128 + 128]
+    for i in range(out_ref.shape[0]):
+        out_ref[i] = part[0:count, :]
+
+
+def call(kernel, outs, scratch=(), places=None):
+    spaces = {"v": pltpu.VMEM, "h": pltpu.HBM, "a": pl.ANY}
+    specs = {}
+    if places is not None:
+        specs["in_specs"] = [pl.BlockSpec(memory_space=spaces[place]) for place in places]
     return pl.pallas_call(
         kernel,
-        out_shape=[jax.ShapeDtypeStruct(shape, F32) for shape in outs],
-        scratch_shapes=[pltpu.VMEM(shape, F32) for shape in scratch],
+        out_shape=[
+            out if hasattr(out, "dtype") else jax.ShapeDtypeStruct(out, F32) for out in outs
+        ],
+        scratch_shapes=[
+            pltpu.VMEM(shape, F32) if isinstance(shape, tuple) else shape for shape in scratch
+        ],
         compiler_params=pltpu.CompilerParams(vmem_limit_bytes=48 * 1024 * 1024),
+        **specs,
     )
 
 
@@ -348,32 +402,30 @@
     return lax.ppermute(first, axes, inner), lax.ppermute(second, axes, outer)
 
 
-def sum_everywhere(keep, send):
+def on_device(velocity, canopy, weight_in, bias_in, weight_out, bias_out, cotangent):
+    field = (3, 4, 16, 128)
+    rows = (24, 128)
+    layers = (6, 24, 128)
     across, along = ("x", "y"), ("zh", "zl")
     swap = [(0, 1), (1, 0)]
     parts = lax.axis_size(across)
     depth = lax.axis_size(along)
     count = HALF // parts
     short = -(-count // depth)
-    half = (keep + lax.ppermute(send, "core", swap)).reshape(parts, count, 128)
-    part = jnp.sum(lax.all_to_all(half, across, 0, 0), axis=0)
-    part = jnp.pad(part, ((0, short * depth - count), (0, 0))).reshape(depth, short, 128)
-    piece = jnp.sum(lax.all_to_all(part, along, 0, 0), axis=0)
-    part = lax.all_to_all(jnp.broadcast_to(piece, part.shape), along, 0, 0)
-    part = part.reshape(short * depth, 128)[:count]
-    half = lax.all_to_all(jnp.broadcast_to(part, half.shape), across, 0, 0)
-    half = half.reshape(HALF, 128)
-    return half, lax.ppermute(half, "core", swap)
-
-
-def on_device(velocity, canopy, weight_in, bias_in, weight_out, bias_out, cotangent):
-    field = (3, 4, 16, 128)
-    rows = (24, 128)
-    layers = (6, 24, 128)
-    direct, m1, m2 = call(start_kernel, (field, rows, rows))(velocity, canopy, cotangent)
+
+    direct, factor, m1, m2 = call(start_kernel, (field, field[1:], rows, rows))(
+        velocity, canopy, cotangent
+    )
     y1, y2 = exchange(m1, m2, GY)
     m1, m2 = call(layer_kernel, (layers, layers))(velocity, direct, y1, y2)
     x1, x2 = exchange(m1, m2, GX)
+    selection = jnp.asarray(selector())
+    weight_in, weight_out, selection = call(
+        weights_in_kernel,
+        (weight_in, weight_out, selection),
+        (pltpu.SemaphoreType.DMA((3,)),),
+        "ahhh",
+    )(m1, weight_in, weight_out, selection)
     keep, send, nv, vg, m1, m2, ylow, yhigh = call(
         main_kernel,
         ((HALF, 128), (HALF, 128), field, field, layers, layers, rows, rows),
@@ -391,15 +443,27 @@
         ),
     )(
         velocity, direct, y1, y2, x1, x2,
-        weight_in, bias_in[None], weight_out, bias_out[None], jnp.asarray(selector()),
-    )
+        weight_in, bias_in[None], weight_out, bias_out[None], selection,
+    )
+
+    half = (keep + lax.ppermute(send, "core", swap)).reshape(parts, count, 128)
+    got = lax.all_to_all(half, across, 0, 0)
     x1, x2 = exchange(m1, m2, GX)
     m1, m2 = call(side_kernel, (rows, rows), (rows, rows))(x1, x2, ylow, yhigh)
+    cut = (depth, 1, short * 128)
+    (part,) = call(across_kernel, (cut,), ((short * depth, 128),), "vaa")(got, x1, x2)
+    got = lax.all_to_all(part, along, 0, 0)
     y1, y2 = exchange(m1, m2, GY)
-    new_velocity, velocity_grad = call(end_kernel, (field, field), ((4, 16, 128),))(
-        nv, vg, canopy, x1, x2, y1, y2
-    )
-    mine, other = sum_everywhere(keep, send)
+    (part,) = call(along_kernel, (cut,), (), "vaa")(got, y1, y2)
+    got = lax.all_to_all(part, along, 0, 0)
+    new_velocity, velocity_grad, done = call(
+        end_kernel, (field, field, (8, 128)), ((4, 16, 128),)
+    )(
+        nv, vg, factor, x1, x2, y1, y2
+    )
+    (half,) = call(spread_kernel, (half.shape,), ((short * depth, 128),), "va")(got, done)
+    mine = lax.all_to_all(half, across, 0, 0).reshape(HALF, 128)
+    other = lax.ppermute(mine, "core", swap)
     blocks = 128 * lax.axis_size(GX) * lax.axis_size(GY)
     scale = float(blocks) ** -0.5
     weight_in_grad, bias_in_grad, weight_out_grad, bias_out_grad = call(

time: 167 us -> 145 us (0.87); the launches traced: 164 us -> 144 us
  blocking collectives: 78.7 us -> 20.4 us
  starting transfers between devices: 54.4 us -> 82.7 us
  waiting for transfers between devices: 16.8 us -> 24.7 us
  Pallas kernels: 5.79 us -> 7.69 us
    all_to_all x4 -> x1, blocking collectives: 78.7 us -> 20.4 us  [on_device(): mine = lax.all_to_all(half, across, 0, 0).reshape(HALF, 128)]
    all_to_all x0 -> x3, starting transfers between devices: none -> 23.8 us  [the longest x2 20.1 us: on_device(): got = lax.all_to_all(part, along, 0, 0)]
    all_to_all x0 -> x3, waiting for transfers between devices: none -> 12.7 us  [the longest x2 12.7 us: on_device(): got = lax.all_to_all(part, along, 0, 0)]
    ppermute x8, starting transfers between devices: 40.2 us -> 48.4 us  [exchange(): return (lax.ppermute(first, axes, inner), lax.ppermute(second, axes, outer))]
    ppermute x8, waiting for transfers between devices: 14.4 us -> 7.21 us  [exchange(): return (lax.ppermute(first, axes, inner), lax.ppermute(second, axes, outer))]
    ppermute x2, starting transfers between devices: 14.2 us -> 10.6 us  [the longest x1 6.56 us: on_device(): other = lax.ppermute(mine, 'core', swap)]
    ppermute x2, waiting for transfers between devices: 2.36 us -> 4.72 us  [the longest x1 2.36 us: on_device(): half = (keep + lax.ppermute(send, 'core', swap)).reshape(parts, count, 128)]
    pallas_call x2 -> x6, Pallas kernels: 0.81 us -> 2.79 us  [the longest x1 0.77 us: on_device(): call(end_kernel, (field, field, (8, 128)), ((4, 16, 128),))]
  transfers between devices with their start and end apart: 10 -> 13, of which waited for: 5 -> 7; matrix products, arithmetic and copies ran while one was open for 0% -> 0% of each run, Pallas kernels for 0% -> 1%
where the time goes in v3:
time: 145 us; the launch traced here: 144 us
  starting transfers between devices  82.7 us (57%)
  waiting for transfers between devices  24.7 us (17%)
  blocking collectives  20.4 us (14%)
  Pallas kernels  7.69 us (5%)
  local copies, waits for them, and re-layouts  6.36 us (4%)
  other arithmetic  1.7 us (1%)
    ppermute x8, starting transfers between devices, exchange(): return (lax.ppermute(first, axes, inner), lax.ppermute(second, axes, outer))  48.4 us
    all_to_all x1, blocking collectives, on_device(): mine = lax.all_to_all(half, across, 0, 0).reshape(HALF, 128)  20.4 us
    all_to_all x2, starting transfers between devices, on_device(): got = lax.all_to_all(part, along, 0, 0)  20.1 us
    all_to_all x2, waiting for transfers between devices, on_device(): got = lax.all_to_all(part, along, 0, 0)  12.7 us
    ppermute x8, waiting for transfers between devices, exchange(): return (lax.ppermute(first, axes, inner), lax.ppermute(second, axes, outer))  7.21 us
    ppermute x1, starting transfers between devices, on_device(): other = lax.ppermute(mine, 'core', swap)  6.56 us
    unnamed x16, local copies, waits for them, and re-layouts  5.67 us
    ppermute x1, starting transfers between devices, on_device(): half = (keep + lax.ppermute(send, 'core', swap)).reshape(parts, count, 128)  4 us
  transfers between devices with their start and end apart: 13, of which 7 were waited for; matrix products, arithmetic and copies ran while one was open for 0% of the time, Pallas kernels for 1%

profile of v3, /device:TPU:1, one launch (start us, length us, event | category | flops | bytes accessed | tf_op | source)
XLA Modules:
  0.0 144.4 jit_solution(10052566911128698777)
XLA Ops:
  0.6 0.0 copy-start
  0.6 0.9 copy-done
  1.5 0.8 copy-done.5
  2.3 0.8 copy-done.6
  3.1 0.0 copy-start.1
  3.1 0.0 copy-start.7
  3.1 8.9 %collective-permute-start = (f32[24,128]{1,0:T(8,128)S(1)}, f32[24,128]{1,0:T(8,128)S(1)}, u32[]{:S(2)}, u32[]{:S(2)}) collective-permute-start(f32[24,128]{1,0:T(8,128)S(1)} %get-tuple-element.33), channel_id=1, source_target_pairs={{0,1},{1,0},{2,3},{3,2},{4,5},{5,4},{6,7},{7,6},{8,9},{9,8},{10,11... | collective-permute-start | bytes 36872 | tf_op jit(solution)/shard_map/ppermute | solution.py:402
  12.1 1.9 %collective-permute-start.1 = (f32[24,128]{1,0:T(8,128)S(1)}, f32[24,128]{1,0:T(8,128)S(1)}, u32[]{:S(2)}, u32[]{:S(2)}) collective-permute-start(f32[24,128]{1,0:T(8,128)S(1)} %get-tuple-element.34), channel_id=1, source_target_pairs={{0,7},{1,2},{2,1},{3,4},{4,3},{5,6},{6,5},{7,0},{8,15},{9,10},{10,... | collective-permute-start | bytes 36872 | tf_op jit(solution)/shard_map/ppermute | solution.py:402
  14.0 0.0 collective-permute-done.r1_ref
  14.0 3.1 %collective-permute-done.1.r2_ref = f32[24,128]{1,0:T(8,128)S(1)} collective-permute-done((f32[24,128]{1,0:T(8,128)S(1)}, f32[24,128]{1,0:T(8,128)S(1)}, u32[]{:S(2)}, u32[]{:S(2)}) %collective-permute-start.1) | collective-permute-done | bytes 12320 | tf_op jit(solution)/shard_map/ppermute | solution.py:402
  17.1 11.7 %collective-permute-start.3 = (f32[6,24,128]{2,1,0:T(8,128)S(1)}, f32[6,24,128]{2,1,0:T(8,128)S(1)}, u32[]{:S(2)}, u32[]{:S(2)}) collective-permute-start(f32[6,24,128]{2,1,0:T(8,128)S(1)} %get-tuple-element.36), channel_id=1, source_target_pairs={{0,504},{8,16},{16,8},{24,32},{32,24},{40,48},{48,40},{56,64},{64,... | collective-permute-start | bytes 221192 | tf_op jit(solution)/shard_map/ppermute | solution.py:402
  28.8 1.9 %collective-permute-start.2 = (f32[6,24,128]{2,1,0:T(8,128)S(1)}, f32[6,24,128]{2,1,0:T(8,128)S(1)}, u32[]{:S(2)}, u32[]{:S(2)}) collective-permute-start(f32[6,24,128]{2,1,0:T(8,128)S(1)} %get-tuple-element.35.after), channel_id=1, source_target_pairs={{0,8},{8,0},{16,24},{24,16},{32,40},{40,32},{48,56},{56,48},{64,72... | collective-permute-start | bytes 221192 | tf_op jit(solution)/shard_map/ppermute | solution.py:402
  30.8 0.7 broadcast_in_dim.7.bout_ref
  31.5 1.1 copy-done.2
  32.6 1.1 copy-done.3
  33.7 1.0 copy-done.4
  34.7 0.5 shard_map.129
  35.2 0.0 collective-permute-done.3.x2_ref
  35.2 0.0 collective-permute-done.2.x1_ref
  35.2 0.0 copy-done.1
  35.2 0.0 copy-done.7
  35.2 3.3 %shard_map.130 = (f32[2176,128]{1,0:T(8,128)S(1)}, f32[2176,128]{1,0:T(8,128)S(1)}, f32[3,4,16,128]{3,2,1,0:T(8,128)S(1)}, f32[3,4,16,128]{3,2,1,0:T(8,128)S(1)}...) custom-call(f32[3,4,16,128]{3,2,1,0:T(8,128)S(1)} %copy-done.1, ...), custom_call_target="tpu_custom_call" | custom-call | tf_op jit(solution)/shard_map/pallas_call | solution.py:429
  38.5 4.0 %collective-permute-start.8 = (f32[2176,128]{1,0:T(8,128)S(1)}, f32[2176,128]{1,0:T(8,128)S(1)}, u32[]{:S(2)}, u32[]{:S(2)}) collective-permute-start(f32[2176,128]{1,0:T(8,128)S(1)} %get-tuple-element.52), channel_id=1, source_target_pairs={{0,1},{1,0},{2,3},{3,2},{4,5},{5,4},{6,7},{7,6},{8,9},{9,8},{10,11... | collective-permute-start | bytes 3342344 | tf_op jit(solution)/shard_map/ppermute | solution.py:449
  42.5 2.4 %collective-permute-done.8 = f32[2176,128]{1,0:T(8,128)S(1)} collective-permute-done((f32[2176,128]{1,0:T(8,128)S(1)}, f32[2176,128]{1,0:T(8,128)S(1)}, u32[]{:S(2)}, u32[]{:S(2)}) %collective-permute-start.8) | collective-permute-done | bytes 1114144 | tf_op jit(solution)/shard_map/ppermute | solution.py:449
  44.9 1.1 add.3
  46.0 3.7 %all-to-all-start = ((f32[16,136,128]{2,1,0:T(8,128)}), f32[16,136,128]{2,1,0:T(8,128)S(1)}, u32[]{:S(2)}, u32[]{:S(2)}) async-start(f32[16,136,128]{2,1,0:T(8,128)} %bitcast.1), calls=%async_computation | async-start | bytes 2228224 | tf_op jit(solution)/shard_map/all_to_all | solution.py:450
  49.7 3.5 %collective-permute-start.4 = (f32[6,24,128]{2,1,0:T(8,128)S(1)}, f32[6,24,128]{2,1,0:T(8,128)S(1)}, u32[]{:S(2)}, u32[]{:S(2)}) collective-permute-start(f32[6,24,128]{2,1,0:T(8,128)S(1)} %get-tuple-element.43), channel_id=1, source_target_pairs={{0,8},{8,0},{16,24},{24,16},{32,40},{40,32},{48,56},{56,48},{64,72... | collective-permute-start | bytes 221192 | tf_op jit(solution)/shard_map/ppermute | solution.py:402
  53.2 12.4 %collective-permute-start.5 = (f32[6,24,128]{2,1,0:T(8,128)S(1)}, f32[6,24,128]{2,1,0:T(8,128)S(1)}, u32[]{:S(2)}, u32[]{:S(2)}) collective-permute-start(f32[6,24,128]{2,1,0:T(8,128)S(1)} %get-tuple-element.44), channel_id=1, source_target_pairs={{0,504},{8,16},{16,8},{24,32},{32,24},{40,48},{48,40},{56,64},{64,... | collective-permute-start | bytes 221192 | tf_op jit(solution)/shard_map/ppermute | solution.py:402
  65.6 0.0 collective-permute-done.4.x1_ref.rest_0_
  65.6 2.3 %collective-permute-done.5.x2_ref.rest_1_ = f32[6,24,128]{2,1,0:T(8,128)S(1)} collective-permute-done((f32[6,24,128]{2,1,0:T(8,128)S(1)}, f32[6,24,128]{2,1,0:T(8,128)S(1)}, u32[]{:S(2)}, u32[]{:S(2)}) %collective-permute-start.5) | collective-permute-done | bytes 73760 | tf_op jit(solution)/shard_map/ppermute | solution.py:402
  67.9 0.0 all-to-all-done.got_ref
  67.9 0.7 shard_map.133
  68.6 10.4 %all-to-all-start.1 = ((f32[16,1,1152]{2,1,0:T(1,128)}), f32[16,1,1152]{2,1,0:T(1,128)S(1)}, u32[]{:S(2)}, u32[]{:S(2)}) async-start(f32[16,1,1152]{2,1,0:T(1,128)} %shard_map.133), calls=%async_computation.1 | async-start | bytes 147456 | tf_op jit(solution)/shard_map/all_to_all | solution.py:455
  79.1 4.6 %collective-permute-start.6 = (f32[24,128]{1,0:T(8,128)S(1)}, f32[24,128]{1,0:T(8,128)S(1)}, u32[]{:S(2)}, u32[]{:S(2)}) collective-permute-start(f32[24,128]{1,0:T(8,128)S(1)} %get-tuple-element.47), channel_id=1, source_target_pairs={{0,1},{1,0},{2,3},{3,2},{4,5},{5,4},{6,7},{7,6},{8,9},{9,8},{10,11... | collective-permute-start | bytes 36872 | tf_op jit(solution)/shard_map/ppermute | solution.py:402
  83.7 3.4 %collective-permute-start.7 = (f32[24,128]{1,0:T(8,128)S(1)}, f32[24,128]{1,0:T(8,128)S(1)}, u32[]{:S(2)}, u32[]{:S(2)}) collective-permute-start(f32[24,128]{1,0:T(8,128)S(1)} %get-tuple-element.48), channel_id=1, source_target_pairs={{0,7},{1,2},{2,1},{3,4},{4,3},{5,6},{6,5},{7,0},{8,15},{9,10},{10,... | collective-permute-start | bytes 36872 | tf_op jit(solution)/shard_map/ppermute | solution.py:402
  87.1 0.0 collective-permute-done.6.y1_ref.rest_0_
  87.1 1.9 %collective-permute-done.7.y2_ref.rest_1_ = f32[24,128]{1,0:T(8,128)S(1)} collective-permute-done((f32[24,128]{1,0:T(8,128)S(1)}, f32[24,128]{1,0:T(8,128)S(1)}, u32[]{:S(2)}, u32[]{:S(2)}) %collective-permute-start.7) | collective-permute-done | bytes 12320 | tf_op jit(solution)/shard_map/ppermute | solution.py:402
  89.0 1.8 %all-to-all-done.1.got_ref = f32[16,1,1152]{2,1,0:T(1,128)S(1)} async-done(((f32[16,1,1152]{2,1,0:T(1,128)}), f32[16,1,1152]{2,1,0:T(1,128)S(1)}, u32[]{:S(2)}, u32[]{:S(2)}) %all-to-all-start.1) | async-done | bytes 73760 | tf_op jit(solution)/shard_map/all_to_all | solution.py:455
  90.8 0.7 shard_map.134
  91.5 9.6 %all-to-all-start.2 = ((f32[16,1,1152]{2,1,0:T(1,128)}), f32[16,1,1152]{2,1,0:T(1,128)S(1)}, u32[]{:S(2)}, u32[]{:S(2)}) async-start(f32[16,1,1152]{2,1,0:T(1,128)} %shard_map.134), calls=%async_computation.2 | async-start | bytes 147456 | tf_op jit(solution)/shard_map/all_to_all | solution.py:458
  101.1 0.8 shard_map.132
  101.9 10.9 %all-to-all-done.2.got_ref = f32[16,1,1152]{2,1,0:T(1,128)S(1)} async-done(((f32[16,1,1152]{2,1,0:T(1,128)}), f32[16,1,1152]{2,1,0:T(1,128)S(1)}, u32[]{:S(2)}, u32[]{:S(2)}) %all-to-all-start.2) | async-done | bytes 73760 | tf_op jit(solution)/shard_map/all_to_all | solution.py:458
  112.8 0.1 shard_map.135
  112.9 20.4 %all_to_all.20 = f32[16,136,128]{2,1,0:T(8,128)S(1)} all-to-all(f32[16,136,128]{2,1,0:T(8,128)S(1)} %shard_map.135), channel_id=1, replica_groups=mesh['zh'=4,'x'=4,'y'=4,'zl'=4,'core'=2] {'x','y'}, dimensions={0} | all-to-all | bytes 2228224 | tf_op jit(solution)/shard_map/all_to_all | solution.py:465
  133.3 6.6 %collective-permute-start.9 = (f32[2176,128]{1,0:T(8,128)S(1)}, f32[2176,128]{1,0:T(8,128)S(1)}, u32[]{:S(2)}, u32[]{:S(2)}) collective-permute-start(f32[2176,128]{1,0:T(8,128)S(1)} %bitcast.4), channel_id=1, source_target_pairs={{0,1},{1,0},{2,3},{3,2},{4,5},{5,4},{6,7},{7,6},{8,9},{9,8},{10,11... | collective-permute-start | bytes 3342344 | tf_op jit(solution)/shard_map/ppermute | solution.py:466
  139.9 2.4 %collective-permute-done.9.refs_1_ = f32[2176,128]{1,0:T(8,128)S(1)} collective-permute-done((f32[2176,128]{1,0:T(8,128)S(1)}, f32[2176,128]{1,0:T(8,128)S(1)}, u32[]{:S(2)}, u32[]{:S(2)}) %collective-permute-start.9) | collective-permute-done | bytes 1114144 | tf_op jit(solution)/shard_map/ppermute | solution.py:466
  142.2 1.6 %shard_map.136 = (f32[648,512]{1,0:T(8,128)}, f32[1,512]{1,0:T(1,128)}, f32[512,384]{1,0:T(8,128)}, f32[1,384]{1,0:T(1,128)S(1)}) custom-call(f32[2176,128]{1,0:T(8,128)S(1)} %bitcast.5, f32[2176,128]{1,0:T(8,128)S(1)} %collective-permute-done.9.refs_1_), custom_call_target="tpu_custom_call" | custom-call | tf_op jit(solution)/shard_map/pallas_call | solution.py:469
  143.8 0.6 reduce
  (8 shorter events, 0.1 us)
Async XLA Ops:
  0.6 0.9 copy-start
  1.5 0.8 copy-start.5
  2.3 0.8 copy-start.6
  3.1 32.1 %copy-start.1 = (f32[3,4,16,128]{3,2,1,0:T(8,128)S(1)}, f32[3,4,16,128]{3,2,1,0:T(8,128)}, u32[]{:S(2)}) copy-start(f32[3,4,16,128]{3,2,1,0:T(8,128)} %v_ref.5) | copy-start | bytes 294916
  3.1 32.1 %copy-start.7 = (f32[512]{0:T(512)S(1)}, f32[512]{0:T(512)}, u32[]{:S(2)}) copy-start(f32[512]{0:T(512)} %param.11) | copy-start | bytes 6148
  3.1 10.9 %collective-permute-start = (f32[24,128]{1,0:T(8,128)S(1)}, f32[24,128]{1,0:T(8,128)S(1)}, u32[]{:S(2)}, u32[]{:S(2)}) collective-permute-start(f32[24,128]{1,0:T(8,128)S(1)} %get-tuple-element.33), channel_id=1, source_target_pairs={{0,1},{1,0},{2,3},{3,2},{4,5},{5,4},{6,7},{7,6},{8,9},{9,8},{10,11... | collective-permute-start | bytes 36872 | tf_op jit(solution)/shard_map/ppermute | solution.py:402
  12.1 5.0 %collective-permute-start.1 = (f32[24,128]{1,0:T(8,128)S(1)}, f32[24,128]{1,0:T(8,128)S(1)}, u32[]{:S(2)}, u32[]{:S(2)}) collective-permute-start(f32[24,128]{1,0:T(8,128)S(1)} %get-tuple-element.34), channel_id=1, source_target_pairs={{0,7},{1,2},{2,1},{3,4},{4,3},{5,6},{6,5},{7,0},{8,15},{9,10},{10,... | collective-permute-start | bytes 36872 | tf_op jit(solution)/shard_map/ppermute | solution.py:402
  17.1 18.1 %collective-permute-start.3 = (f32[6,24,128]{2,1,0:T(8,128)S(1)}, f32[6,24,128]{2,1,0:T(8,128)S(1)}, u32[]{:S(2)}, u32[]{:S(2)}) collective-permute-start(f32[6,24,128]{2,1,0:T(8,128)S(1)} %get-tuple-element.36), channel_id=1, source_target_pairs={{0,504},{8,16},{16,8},{24,32},{32,24},{40,48},{48,40},{56,64},{64,... | collective-permute-start | bytes 221192 | tf_op jit(solution)/shard_map/ppermute | solution.py:402
  28.8 6.3 %collective-permute-start.2 = (f32[6,24,128]{2,1,0:T(8,128)S(1)}, f32[6,24,128]{2,1,0:T(8,128)S(1)}, u32[]{:S(2)}, u32[]{:S(2)}) collective-permute-start(f32[6,24,128]{2,1,0:T(8,128)S(1)} %get-tuple-element.35.after), channel_id=1, source_target_pairs={{0,8},{8,0},{16,24},{24,16},{32,40},{40,32},{48,56},{56,48},{64,72... | collective-permute-start | bytes 221192 | tf_op jit(solution)/shard_map/ppermute | solution.py:402
  31.5 1.1 copy-start.2
  32.6 1.1 copy-start.3
  33.7 1.0 copy-start.4
  38.5 6.4 %collective-permute-start.8 = (f32[2176,128]{1,0:T(8,128)S(1)}, f32[2176,128]{1,0:T(8,128)S(1)}, u32[]{:S(2)}, u32[]{:S(2)}) collective-permute-start(f32[2176,128]{1,0:T(8,128)S(1)} %get-tuple-element.52), channel_id=1, source_target_pairs={{0,1},{1,0},{2,3},{3,2},{4,5},{5,4},{6,7},{7,6},{8,9},{9,8},{10,11... | collective-permute-start | bytes 3342344 | tf_op jit(solution)/shard_map/ppermute | solution.py:449
  46.0 21.9 %all-to-all-start = ((f32[16,136,128]{2,1,0:T(8,128)}), f32[16,136,128]{2,1,0:T(8,128)S(1)}, u32[]{:S(2)}, u32[]{:S(2)}) async-start(f32[16,136,128]{2,1,0:T(8,128)} %bitcast.1), calls=%async_computation | async-start | bytes 2228224 | tf_op jit(solution)/shard_map/all_to_all | solution.py:450
  49.7 15.9 %collective-permute-start.4 = (f32[6,24,128]{2,1,0:T(8,128)S(1)}, f32[6,24,128]{2,1,0:T(8,128)S(1)}, u32[]{:S(2)}, u32[]{:S(2)}) collective-permute-start(f32[6,24,128]{2,1,0:T(8,128)S(1)} %get-tuple-element.43), channel_id=1, source_target_pairs={{0,8},{8,0},{16,24},{24,16},{32,40},{40,32},{48,56},{56,48},{64,72... | collective-permute-start | bytes 221192 | tf_op jit(solution)/shard_map/ppermute | solution.py:402
  53.2 14.7 %collective-permute-start.5 = (f32[6,24,128]{2,1,0:T(8,128)S(1)}, f32[6,24,128]{2,1,0:T(8,128)S(1)}, u32[]{:S(2)}, u32[]{:S(2)}) collective-permute-start(f32[6,24,128]{2,1,0:T(8,128)S(1)} %get-tuple-element.44), channel_id=1, source_target_pairs={{0,504},{8,16},{16,8},{24,32},{32,24},{40,48},{48,40},{56,64},{64,... | collective-permute-start | bytes 221192 | tf_op jit(solution)/shard_map/ppermute | solution.py:402
  68.6 22.1 %all-to-all-start.1 = ((f32[16,1,1152]{2,1,0:T(1,128)}), f32[16,1,1152]{2,1,0:T(1,128)S(1)}, u32[]{:S(2)}, u32[]{:S(2)}) async-start(f32[16,1,1152]{2,1,0:T(1,128)} %shard_map.133), calls=%async_computation.1 | async-start | bytes 147456 | tf_op jit(solution)/shard_map/all_to_all | solution.py:455
  79.1 8.0 %collective-permute-start.6 = (f32[24,128]{1,0:T(8,128)S(1)}, f32[24,128]{1,0:T(8,128)S(1)}, u32[]{:S(2)}, u32[]{:S(2)}) collective-permute-start(f32[24,128]{1,0:T(8,128)S(1)} %get-tuple-element.47), channel_id=1, source_target_pairs={{0,1},{1,0},{2,3},{3,2},{4,5},{5,4},{6,7},{7,6},{8,9},{9,8},{10,11... | collective-permute-start | bytes 36872 | tf_op jit(solution)/shard_map/ppermute | solution.py:402
  83.7 5.3 %collective-permute-start.7 = (f32[24,128]{1,0:T(8,128)S(1)}, f32[24,128]{1,0:T(8,128)S(1)}, u32[]{:S(2)}, u32[]{:S(2)}) collective-permute-start(f32[24,128]{1,0:T(8,128)S(1)} %get-tuple-element.48), channel_id=1, source_target_pairs={{0,7},{1,2},{2,1},{3,4},{4,3},{5,6},{6,5},{7,0},{8,15},{9,10},{10,... | collective-permute-start | bytes 36872 | tf_op jit(solution)/shard_map/ppermute | solution.py:402
  91.5 21.4 %all-to-all-start.2 = ((f32[16,1,1152]{2,1,0:T(1,128)}), f32[16,1,1152]{2,1,0:T(1,128)S(1)}, u32[]{:S(2)}, u32[]{:S(2)}) async-start(f32[16,1,1152]{2,1,0:T(1,128)} %shard_map.134), calls=%async_computation.2 | async-start | bytes 147456 | tf_op jit(solution)/shard_map/all_to_all | solution.py:458
  133.3 8.9 %collective-permute-start.9 = (f32[2176,128]{1,0:T(8,128)S(1)}, f32[2176,128]{1,0:T(8,128)S(1)}, u32[]{:S(2)}, u32[]{:S(2)}) collective-permute-start(f32[2176,128]{1,0:T(8,128)S(1)} %bitcast.4), channel_id=1, source_target_pairs={{0,1},{1,0},{2,3},{3,2},{4,5},{5,4},{6,7},{7,6},{8,9},{9,8},{10,11... | collective-permute-start | bytes 3342344 | tf_op jit(solution)/shard_map/ppermute | solution.py:466

commit v4 on v3

--- a/solution.py
+++ b/solution.py
@@ -372,7 +372,7 @@
         out_ref[i] = part[0:count, :]
 
 
-def call(kernel, outs, scratch=(), places=None):
+def call(kernel, outs, scratch=(), places=None, room=48):
     spaces = {"v": pltpu.VMEM, "h": pltpu.HBM, "a": pl.ANY}
     specs = {}
     if places is not None:
@@ -385,9 +385,17 @@
         scratch_shapes=[
             pltpu.VMEM(shape, F32) if isinstance(shape, tuple) else shape for shape in scratch
         ],
-        compiler_params=pltpu.CompilerParams(vmem_limit_bytes=48 * 1024 * 1024),
+        compiler_params=pltpu.CompilerParams(vmem_limit_bytes=room * 1024 * 1024),
         **specs,
     )
+
+
+def in_order(array, first):
+    def kernel(array_ref, first_ref, out_ref):
+        out_ref[...] = array_ref[...]
+
+    (array,) = call(kernel, (array.shape,), (), "va", 12)(array, first)
+    return array
 
 
 def pairs(axes):
@@ -451,18 +459,17 @@
     x1, x2 = exchange(m1, m2, GX)
     m1, m2 = call(side_kernel, (rows, rows), (rows, rows))(x1, x2, ylow, yhigh)
     cut = (depth, 1, short * 128)
-    (part,) = call(across_kernel, (cut,), ((short * depth, 128),), "vaa")(got, x1, x2)
+    (part,) = call(across_kernel, (cut,), ((short * depth, 128),), "va", 12)(got, x2)
     got = lax.all_to_all(part, along, 0, 0)
+    (part,) = call(along_kernel, (cut,), (), "v", 12)(got)
+    got = lax.all_to_all(part, along, 0, 0)
+    (half,) = call(spread_kernel, (half.shape,), ((short * depth, 128),), "v", 12)(got)
+    mine = lax.all_to_all(half, across, 0, 0).reshape(HALF, 128)
     y1, y2 = exchange(m1, m2, GY)
-    (part,) = call(along_kernel, (cut,), (), "vaa")(got, y1, y2)
-    got = lax.all_to_all(part, along, 0, 0)
     new_velocity, velocity_grad, done = call(
-        end_kernel, (field, field, (8, 128)), ((4, 16, 128),)
-    )(
-        nv, vg, factor, x1, x2, y1, y2
-    )
-    (half,) = call(spread_kernel, (half.shape,), ((short * depth, 128),), "va")(got, done)
-    mine = lax.all_to_all(half, across, 0, 0).reshape(HALF, 128)
+        end_kernel, (field, field, (8, 128)), ((4, 16, 128),), None, 12
+    )(nv, vg, factor, x1, x2, y1, y2)
+    mine = in_order(mine, done)
     other = lax.ppermute(mine, "core", swap)
     blocks = 128 * lax.axis_size(GX) * lax.axis_size(GY)
     scale = float(blocks) ** -0.5

time: 145 us -> 147 us (1.014)
  blocking collectives: 20.4 us -> 35.4 us
  starting transfers between devices: 82.7 us -> 69 us
    all_to_all x1 -> x2, blocking collectives: 20.4 us -> 35.4 us  [on_device(): got = lax.all_to_all(part, along, 0, 0)]
    all_to_all x2 -> x1, starting transfers between devices: 20.1 us -> 6.56 us  [on_device(): mine = lax.all_to_all(half, across, 0, 0).reshape(HALF, 128)]
    ppermute x8, waiting for transfers between devices: 7.21 us -> 20.4 us  [exchange(): return (lax.ppermute(first, axes, inner), lax.ppermute(second, axes, outer))]
    all_to_all x2 -> x1, waiting for transfers between devices: 12.7 us -> 0.01 us  [on_device(): mine = lax.all_to_all(half, across, 0, 0).reshape(HALF, 128)]
    ppermute x1, starting transfers between devices: 6.56 us -> 3.72 us  [on_device(): other = lax.ppermute(mine, 'core', swap)]
    ppermute x8, starting transfers between devices: 48.4 us -> 51 us  [exchange(): return (lax.ppermute(first, axes, inner), lax.ppermute(second, axes, outer))]
  transfers between devices with their start and end apart: 13 -> 12, of which waited for: 7 -> 6; matrix products, arithmetic and copies ran while one was open for 0% -> 0% of each run, Pallas kernels for 1% -> 1%
where the time goes in v4:
time: 147 us; the launch traced here: 146 us
  starting transfers between devices  69 us (47%)
  blocking collectives  35.4 us (24%)
  waiting for transfers between devices  25.1 us (17%)
  Pallas kernels  7.48 us (5%)
  local copies, waits for them, and re-layouts  6.36 us (4%)
  other arithmetic  1.7 us (1%)
    ppermute x8, starting transfers between devices, exchange(): return (lax.ppermute(first, axes, inner), lax.ppermute(second, axes, outer))  51 us
    all_to_all x2, blocking collectives, on_device(): got = lax.all_to_all(part, along, 0, 0)  35.4 us
    ppermute x8, waiting for transfers between devices, exchange(): return (lax.ppermute(first, axes, inner), lax.ppermute(second, axes, outer))  20.4 us
    all_to_all x1, starting transfers between devices, on_device(): mine = lax.all_to_all(half, across, 0, 0).reshape(HALF, 128)  6.56 us
    unnamed x16, local copies, waits for them, and re-layouts  5.67 us
    ppermute x1, starting transfers between devices, on_device(): half = (keep + lax.ppermute(send, 'core', swap)).reshape(parts, count, 128)  4 us
    ppermute x1, starting transfers between devices, on_device(): other = lax.ppermute(mine, 'core', swap)  3.72 us
    all_to_all x1, starting transfers between devices, on_device(): got = lax.all_to_all(half, across, 0, 0)  3.7 us
  transfers between devices with their start and end apart: 12, of which 6 were waited for; matrix products, arithmetic and copies ran while one was open for 0% of the time, Pallas kernels for 1%

profile of v4, /device:TPU:1, one launch (start us, length us, event | category | flops | bytes accessed | tf_op | source)
XLA Modules:
  0.0 145.8 jit_solution(1169952688414582555)
XLA Ops:
  0.6 0.0 copy-start
  0.6 0.9 copy-done
  1.5 0.8 copy-done.5
  2.3 0.8 copy-done.6
  3.1 0.0 copy-start.1
  3.1 0.0 copy-start.7
  3.1 8.9 %collective-permute-start = (f32[24,128]{1,0:T(8,128)S(1)}, f32[24,128]{1,0:T(8,128)S(1)}, u32[]{:S(2)}, u32[]{:S(2)}) collective-permute-start(f32[24,128]{1,0:T(8,128)S(1)} %get-tuple-element.33), channel_id=1, source_target_pairs={{0,1},{1,0},{2,3},{3,2},{4,5},{5,4},{6,7},{7,6},{8,9},{9,8},{10,11... | collective-permute-start | bytes 36872 | tf_op jit(solution)/shard_map/ppermute | solution.py:410
  12.1 1.9 %collective-permute-start.1 = (f32[24,128]{1,0:T(8,128)S(1)}, f32[24,128]{1,0:T(8,128)S(1)}, u32[]{:S(2)}, u32[]{:S(2)}) collective-permute-start(f32[24,128]{1,0:T(8,128)S(1)} %get-tuple-element.34), channel_id=1, source_target_pairs={{0,7},{1,2},{2,1},{3,4},{4,3},{5,6},{6,5},{7,0},{8,15},{9,10},{10,... | collective-permute-start | bytes 36872 | tf_op jit(solution)/shard_map/ppermute | solution.py:410
  14.0 0.0 collective-permute-done.r1_ref
  14.0 3.1 %collective-permute-done.1.r2_ref = f32[24,128]{1,0:T(8,128)S(1)} collective-permute-done((f32[24,128]{1,0:T(8,128)S(1)}, f32[24,128]{1,0:T(8,128)S(1)}, u32[]{:S(2)}, u32[]{:S(2)}) %collective-permute-start.1) | collective-permute-done | bytes 12320 | tf_op jit(solution)/shard_map/ppermute | solution.py:410
  17.1 11.7 %collective-permute-start.3 = (f32[6,24,128]{2,1,0:T(8,128)S(1)}, f32[6,24,128]{2,1,0:T(8,128)S(1)}, u32[]{:S(2)}, u32[]{:S(2)}) collective-permute-start(f32[6,24,128]{2,1,0:T(8,128)S(1)} %get-tuple-element.36), channel_id=1, source_target_pairs={{0,504},{8,16},{16,8},{24,32},{32,24},{40,48},{48,40},{56,64},{64,... | collective-permute-start | bytes 221192 | tf_op jit(solution)/shard_map/ppermute | solution.py:410
  28.8 1.9 %collective-permute-start.2 = (f32[6,24,128]{2,1,0:T(8,128)S(1)}, f32[6,24,128]{2,1,0:T(8,128)S(1)}, u32[]{:S(2)}, u32[]{:S(2)}) collective-permute-start(f32[6,24,128]{2,1,0:T(8,128)S(1)} %get-tuple-element.35.after), channel_id=1, source_target_pairs={{0,8},{8,0},{16,24},{24,16},{32,40},{40,32},{48,56},{56,48},{64,72... | collective-permute-start | bytes 221192 | tf_op jit(solution)/shard_map/ppermute | solution.py:410
  30.8 0.7 broadcast_in_dim.7.bout_ref
  31.5 1.1 copy-done.2
  32.6 1.1 copy-done.3
  33.7 1.0 copy-done.4
  34.7 0.5 shard_map.129
  35.2 0.0 collective-permute-done.3.x2_ref
  35.2 0.0 collective-permute-done.2.x1_ref
  35.2 0.0 copy-done.1
  35.2 0.0 copy-done.7
  35.2 3.3 %shard_map.130 = (f32[2176,128]{1,0:T(8,128)S(1)}, f32[2176,128]{1,0:T(8,128)S(1)}, f32[3,4,16,128]{3,2,1,0:T(8,128)S(1)}, f32[3,4,16,128]{3,2,1,0:T(8,128)S(1)}...) custom-call(f32[3,4,16,128]{3,2,1,0:T(8,128)S(1)} %copy-done.1, ...), custom_call_target="tpu_custom_call" | custom-call | tf_op jit(solution)/shard_map/pallas_call | solution.py:437
  38.5 4.0 %collective-permute-start.8 = (f32[2176,128]{1,0:T(8,128)S(1)}, f32[2176,128]{1,0:T(8,128)S(1)}, u32[]{:S(2)}, u32[]{:S(2)}) collective-permute-start(f32[2176,128]{1,0:T(8,128)S(1)} %get-tuple-element.52), channel_id=1, source_target_pairs={{0,1},{1,0},{2,3},{3,2},{4,5},{5,4},{6,7},{7,6},{8,9},{9,8},{10,11... | collective-permute-start | bytes 3342344 | tf_op jit(solution)/shard_map/ppermute | solution.py:457
  42.5 2.4 %collective-permute-done.8 = f32[2176,128]{1,0:T(8,128)S(1)} collective-permute-done((f32[2176,128]{1,0:T(8,128)S(1)}, f32[2176,128]{1,0:T(8,128)S(1)}, u32[]{:S(2)}, u32[]{:S(2)}) %collective-permute-start.8) | collective-permute-done | bytes 1114144 | tf_op jit(solution)/shard_map/ppermute | solution.py:457
  44.9 1.1 add.3
  46.0 3.7 %all-to-all-start = ((f32[16,136,128]{2,1,0:T(8,128)}), f32[16,136,128]{2,1,0:T(8,128)S(1)}, u32[]{:S(2)}, u32[]{:S(2)}) async-start(f32[16,136,128]{2,1,0:T(8,128)} %bitcast.1), calls=%async_computation | async-start | bytes 2228224 | tf_op jit(solution)/shard_map/all_to_all | solution.py:458
  49.7 13.4 %collective-permute-start.5 = (f32[6,24,128]{2,1,0:T(8,128)S(1)}, f32[6,24,128]{2,1,0:T(8,128)S(1)}, u32[]{:S(2)}, u32[]{:S(2)}) collective-permute-start(f32[6,24,128]{2,1,0:T(8,128)S(1)} %get-tuple-element.44), channel_id=1, source_target_pairs={{0,504},{8,16},{16,8},{24,32},{32,24},{40,48},{48,40},{56,64},{64,... | collective-permute-start | bytes 221192 | tf_op jit(solution)/shard_map/ppermute | solution.py:410
  63.1 6.2 %collective-permute-done.5.x2_ref.rest_0_ = f32[6,24,128]{2,1,0:T(8,128)S(1)} collective-permute-done((f32[6,24,128]{2,1,0:T(8,128)S(1)}, f32[6,24,128]{2,1,0:T(8,128)S(1)}, u32[]{:S(2)}, u32[]{:S(2)}) %collective-permute-start.5) | collective-permute-done | bytes 73760 | tf_op jit(solution)/shard_map/ppermute | solution.py:410
  69.3 0.0 all-to-all-done.got_ref
  69.3 0.1 shard_map.133
  69.4 20.9 %all_to_all.20.got_ref = f32[16,1,1152]{2,1,0:T(1,128)S(1)} all-to-all(f32[16,1,1152]{2,1,0:T(1,128)S(1)} %shard_map.133), channel_id=1, replica_groups=mesh['zh'=4,'x'=4,'y'=4,'zl'=4,'core'=2] {'zh','zl'}, dimensions={0} | all-to-all | bytes 147456 | tf_op jit(solution)/shard_map/all_to_all | solution.py:463
  90.3 0.1 shard_map.134
  90.4 14.5 %all_to_all.21.got_ref = f32[16,1,1152]{2,1,0:T(1,128)S(1)} all-to-all(f32[16,1,1152]{2,1,0:T(1,128)S(1)} %shard_map.134), channel_id=1, replica_groups=mesh['zh'=4,'x'=4,'y'=4,'zl'=4,'core'=2] {'zh','zl'}, dimensions={0} | all-to-all | bytes 147456 | tf_op jit(solution)/shard_map/all_to_all | solution.py:465
  104.9 1.1 shard_map.135
  105.9 6.6 %all-to-all-start.3 = ((f32[16,136,128]{2,1,0:T(8,128)}), f32[16,136,128]{2,1,0:T(8,128)S(1)}, u32[]{:S(2)}, u32[]{:S(2)}) async-start(f32[16,136,128]{2,1,0:T(8,128)} %shard_map.135), calls=%async_computation.3 | async-start | bytes 2228224 | tf_op jit(solution)/shard_map/all_to_all | solution.py:467
  112.5 3.3 %collective-permute-start.4 = (f32[6,24,128]{2,1,0:T(8,128)S(1)}, f32[6,24,128]{2,1,0:T(8,128)S(1)}, u32[]{:S(2)}, u32[]{:S(2)}) collective-permute-start(f32[6,24,128]{2,1,0:T(8,128)S(1)} %get-tuple-element.43), channel_id=1, source_target_pairs={{0,8},{8,0},{16,24},{24,16},{32,40},{40,32},{48,56},{56,48},{64,72... | collective-permute-start | bytes 221192 | tf_op jit(solution)/shard_map/ppermute | solution.py:410
  115.8 8.6 %collective-permute-done.4.x1_ref = f32[6,24,128]{2,1,0:T(8,128)S(1)} collective-permute-done((f32[6,24,128]{2,1,0:T(8,128)S(1)}, f32[6,24,128]{2,1,0:T(8,128)S(1)}, u32[]{:S(2)}, u32[]{:S(2)}) %collective-permute-start.4) | collective-permute-done | bytes 73760 | tf_op jit(solution)/shard_map/ppermute | solution.py:410
  124.4 7.3 %collective-permute-start.6 = (f32[24,128]{1,0:T(8,128)S(1)}, f32[24,128]{1,0:T(8,128)S(1)}, u32[]{:S(2)}, u32[]{:S(2)}) collective-permute-start(f32[24,128]{1,0:T(8,128)S(1)} %get-tuple-element.47), channel_id=1, source_target_pairs={{0,1},{1,0},{2,3},{3,2},{4,5},{5,4},{6,7},{7,6},{8,9},{9,8},{10,11... | collective-permute-start | bytes 36872 | tf_op jit(solution)/shard_map/ppermute | solution.py:410
  131.7 2.5 %collective-permute-start.7 = (f32[24,128]{1,0:T(8,128)S(1)}, f32[24,128]{1,0:T(8,128)S(1)}, u32[]{:S(2)}, u32[]{:S(2)}) collective-permute-start(f32[24,128]{1,0:T(8,128)S(1)} %get-tuple-element.48), channel_id=1, source_target_pairs={{0,7},{1,2},{2,1},{3,4},{4,3},{5,6},{6,5},{7,0},{8,15},{9,10},{10,... | collective-permute-start | bytes 36872 | tf_op jit(solution)/shard_map/ppermute | solution.py:410
  134.2 0.0 collective-permute-done.6.y1_ref
  134.2 2.5 %collective-permute-done.7.y2_ref = f32[24,128]{1,0:T(8,128)S(1)} collective-permute-done((f32[24,128]{1,0:T(8,128)S(1)}, f32[24,128]{1,0:T(8,128)S(1)}, u32[]{:S(2)}, u32[]{:S(2)}) %collective-permute-start.7) | collective-permute-done | bytes 12320 | tf_op jit(solution)/shard_map/ppermute | solution.py:410
  136.8 0.8 shard_map.132
  137.5 0.0 all-to-all-done.3
  137.5 0.1 shard_map.136.refs_0_
  137.6 3.7 %collective-permute-start.9 = (f32[2176,128]{1,0:T(8,128)S(1)}, f32[2176,128]{1,0:T(8,128)S(1)}, u32[]{:S(2)}, u32[]{:S(2)}) collective-permute-start(f32[2176,128]{1,0:T(8,128)S(1)} %shard_map.136.refs_0_), channel_id=1, source_target_pairs={{0,1},{1,0},{2,3},{3,2},{4,5},{5,4},{6,7},{7,6},{8,9},{9,8},{10,11... | collective-permute-start | bytes 3342344 | tf_op jit(solution)/shard_map/ppermute | solution.py:473
  141.3 2.4 %collective-permute-done.9.refs_1_ = f32[2176,128]{1,0:T(8,128)S(1)} collective-permute-done((f32[2176,128]{1,0:T(8,128)S(1)}, f32[2176,128]{1,0:T(8,128)S(1)}, u32[]{:S(2)}, u32[]{:S(2)}) %collective-permute-start.9) | collective-permute-done | bytes 1114144 | tf_op jit(solution)/shard_map/ppermute | solution.py:473
  143.7 1.6 %shard_map.137 = (f32[648,512]{1,0:T(8,128)}, f32[1,512]{1,0:T(1,128)}, f32[512,384]{1,0:T(8,128)}, f32[1,384]{1,0:T(1,128)S(1)}) custom-call(f32[2176,128]{1,0:T(8,128)S(1)} %shard_map.136.refs_0_, f32[2176,128]{1,0:T(8,128)S(1)} %collective-permute-done.9.refs_1_), custom_call_target="tpu_custom_call" | custom-call | tf_op jit(solution)/shard_map/pallas_call | solution.py:476
  145.3 0.6 reduce
  (8 shorter events, 0.1 us)
Async XLA Ops:
  0.6 0.9 copy-start
  1.5 0.8 copy-start.5
  2.3 0.8 copy-start.6
  3.1 32.1 %copy-start.1 = (f32[3,4,16,128]{3,2,1,0:T(8,128)S(1)}, f32[3,4,16,128]{3,2,1,0:T(8,128)}, u32[]{:S(2)}) copy-start(f32[3,4,16,128]{3,2,1,0:T(8,128)} %v_ref.5) | copy-start | bytes 294916
  3.1 32.1 %copy-start.7 = (f32[512]{0:T(512)S(1)}, f32[512]{0:T(512)}, u32[]{:S(2)}) copy-start(f32[512]{0:T(512)} %param.11) | copy-start | bytes 6148
  3.1 10.9 %collective-permute-start = (f32[24,128]{1,0:T(8,128)S(1)}, f32[24,128]{1,0:T(8,128)S(1)}, u32[]{:S(2)}, u32[]{:S(2)}) collective-permute-start(f32[24,128]{1,0:T(8,128)S(1)} %get-tuple-element.33), channel_id=1, source_target_pairs={{0,1},{1,0},{2,3},{3,2},{4,5},{5,4},{6,7},{7,6},{8,9},{9,8},{10,11... | collective-permute-start | bytes 36872 | tf_op jit(solution)/shard_map/ppermute | solution.py:410
  12.1 5.0 %collective-permute-start.1 = (f32[24,128]{1,0:T(8,128)S(1)}, f32[24,128]{1,0:T(8,128)S(1)}, u32[]{:S(2)}, u32[]{:S(2)}) collective-permute-start(f32[24,128]{1,0:T(8,128)S(1)} %get-tuple-element.34), channel_id=1, source_target_pairs={{0,7},{1,2},{2,1},{3,4},{4,3},{5,6},{6,5},{7,0},{8,15},{9,10},{10,... | collective-permute-start | bytes 36872 | tf_op jit(solution)/shard_map/ppermute | solution.py:410
  17.1 18.1 %collective-permute-start.3 = (f32[6,24,128]{2,1,0:T(8,128)S(1)}, f32[6,24,128]{2,1,0:T(8,128)S(1)}, u32[]{:S(2)}, u32[]{:S(2)}) collective-permute-start(f32[6,24,128]{2,1,0:T(8,128)S(1)} %get-tuple-element.36), channel_id=1, source_target_pairs={{0,504},{8,16},{16,8},{24,32},{32,24},{40,48},{48,40},{56,64},{64,... | collective-permute-start | bytes 221192 | tf_op jit(solution)/shard_map/ppermute | solution.py:410
  28.8 6.3 %collective-permute-start.2 = (f32[6,24,128]{2,1,0:T(8,128)S(1)}, f32[6,24,128]{2,1,0:T(8,128)S(1)}, u32[]{:S(2)}, u32[]{:S(2)}) collective-permute-start(f32[6,24,128]{2,1,0:T(8,128)S(1)} %get-tuple-element.35.after), channel_id=1, source_target_pairs={{0,8},{8,0},{16,24},{24,16},{32,40},{40,32},{48,56},{56,48},{64,72... | collective-permute-start | bytes 221192 | tf_op jit(solution)/shard_map/ppermute | solution.py:410
  31.5 1.1 copy-start.2
  32.6 1.1 copy-start.3
  33.7 1.0 copy-start.4
  38.5 6.4 %collective-permute-start.8 = (f32[2176,128]{1,0:T(8,128)S(1)}, f32[2176,128]{1,0:T(8,128)S(1)}, u32[]{:S(2)}, u32[]{:S(2)}) collective-permute-start(f32[2176,128]{1,0:T(8,128)S(1)} %get-tuple-element.52), channel_id=1, source_target_pairs={{0,1},{1,0},{2,3},{3,2},{4,5},{5,4},{6,7},{7,6},{8,9},{9,8},{10,11... | collective-permute-start | bytes 3342344 | tf_op jit(solution)/shard_map/ppermute | solution.py:457
  46.0 23.3 %all-to-all-start = ((f32[16,136,128]{2,1,0:T(8,128)}), f32[16,136,128]{2,1,0:T(8,128)S(1)}, u32[]{:S(2)}, u32[]{:S(2)}) async-start(f32[16,136,128]{2,1,0:T(8,128)} %bitcast.1), calls=%async_computation | async-start | bytes 2228224 | tf_op jit(solution)/shard_map/all_to_all | solution.py:458
  49.7 19.6 %collective-permute-start.5 = (f32[6,24,128]{2,1,0:T(8,128)S(1)}, f32[6,24,128]{2,1,0:T(8,128)S(1)}, u32[]{:S(2)}, u32[]{:S(2)}) collective-permute-start(f32[6,24,128]{2,1,0:T(8,128)S(1)} %get-tuple-element.44), channel_id=1, source_target_pairs={{0,504},{8,16},{16,8},{24,32},{32,24},{40,48},{48,40},{56,64},{64,... | collective-permute-start | bytes 221192 | tf_op jit(solution)/shard_map/ppermute | solution.py:410
  105.9 31.6 %all-to-all-start.3 = ((f32[16,136,128]{2,1,0:T(8,128)}), f32[16,136,128]{2,1,0:T(8,128)S(1)}, u32[]{:S(2)}, u32[]{:S(2)}) async-start(f32[16,136,128]{2,1,0:T(8,128)} %shard_map.135), calls=%async_computation.3 | async-start | bytes 2228224 | tf_op jit(solution)/shard_map/all_to_all | solution.py:467
  112.5 11.9 %collective-permute-start.4 = (f32[6,24,128]{2,1,0:T(8,128)S(1)}, f32[6,24,128]{2,1,0:T(8,128)S(1)}, u32[]{:S(2)}, u32[]{:S(2)}) collective-permute-start(f32[6,24,128]{2,1,0:T(8,128)S(1)} %get-tuple-element.43), channel_id=1, source_target_pairs={{0,8},{8,0},{16,24},{24,16},{32,40},{40,32},{48,56},{56,48},{64,72... | collective-permute-start | bytes 221192 | tf_op jit(solution)/shard_map/ppermute | solution.py:410
  124.4 9.8 %collective-permute-start.6 = (f32[24,128]{1,0:T(8,128)S(1)}, f32[24,128]{1,0:T(8,128)S(1)}, u32[]{:S(2)}, u32[]{:S(2)}) collective-permute-start(f32[24,128]{1,0:T(8,128)S(1)} %get-tuple-element.47), channel_id=1, source_target_pairs={{0,1},{1,0},{2,3},{3,2},{4,5},{5,4},{6,7},{7,6},{8,9},{9,8},{10,11... | collective-permute-start | bytes 36872 | tf_op jit(solution)/shard_map/ppermute | solution.py:410
  131.7 5.0 %collective-permute-start.7 = (f32[24,128]{1,0:T(8,128)S(1)}, f32[24,128]{1,0:T(8,128)S(1)}, u32[]{:S(2)}, u32[]{:S(2)}) collective-permute-start(f32[24,128]{1,0:T(8,128)S(1)} %get-tuple-element.48), channel_id=1, source_target_pairs={{0,7},{1,2},{2,1},{3,4},{4,3},{5,6},{6,5},{7,0},{8,15},{9,10},{10,... | collective-permute-start | bytes 36872 | tf_op jit(solution)/shard_map/ppermute | solution.py:410
  137.6 6.1 %collective-permute-start.9 = (f32[2176,128]{1,0:T(8,128)S(1)}, f32[2176,128]{1,0:T(8,128)S(1)}, u32[]{:S(2)}, u32[]{:S(2)}) collective-permute-start(f32[2176,128]{1,0:T(8,128)S(1)} %shard_map.136.refs_0_), channel_id=1, source_target_pairs={{0,1},{1,0},{2,3},{3,2},{4,5},{5,4},{6,7},{7,6},{8,9},{9,8},{10,11... | collective-permute-start | bytes 3342344 | tf_op jit(solution)/shard_map/ppermute | solution.py:473

commit v5 on v4

--- a/solution.py
+++ b/solution.py
@@ -102,11 +102,24 @@
             out[k, 17:18, :] = jnp.where(core == 0, row1, row2)
 
 
+def shifted(ext):
+    def at(k, dx, dy):
+        return ext[k * 6 + 1 + dx : k * 6 + 5 + dx, 1 + dy : 17 + dy, :]
+
+    return at
+
+
+def slopes(at):
+    grad_x = [(at(3 + i, 1, 0) - at(3 + i, -1, 0)) * 0.5 for i in range(3)]
+    grad_y = [(at(3 + i, 0, 1) - at(3 + i, 0, -1)) * 0.5 for i in range(3)]
+    grad_z = [(z_next(at(3 + i, 0, 0)) - z_before(at(3 + i, 0, 0))) * 0.5 for i in range(3)]
+    return grad_x, grad_y, grad_z
+
+
 def main_kernel(
     v_ref, direct_ref, r1_ref, r2_ref, x1_ref, x2_ref,
-    win_ref, bin_ref, wout_ref, bout_ref, sel_ref,
-    keep_ref, send_ref, nv_ref, vg_ref, m1_ref, m2_ref, ylow_ref, yhigh_ref,
-    ext, sgrad, cols, rows, cgrad, cpad, opad, ghost, tau, flat,
+    win_ref, bin_ref, wout_ref, sel_ref,
+    keep_ref, send_ref, ext, hidden_ref, pre_low_ref, sgrad, cols, rows, flat,
 ):
     core = lax.axis_index("core")
     parity = lax.rem(lax.axis_index("y"), 2)
@@ -123,17 +136,7 @@
             ext[spot, 0:1, :] = jnp.where(core == 0, row2, row1)
             ext[spot, 17:18, :] = jnp.where(core == 0, row1, row2)
 
-    def at(k, dx, dy):
-        return ext[k * 6 + 1 + dx : k * 6 + 5 + dx, 1 + dy : 17 + dy, :]
-
-    def laplace(k):
-        middle = at(k, 0, 0)
-        total = at(k, 1, 0) + at(k, -1, 0) + at(k, 0, 1) + at(k, 0, -1)
-        return total + z_next(middle) + z_before(middle) - 6.0 * middle
-
-    grad_x = [(at(3 + i, 1, 0) - at(3 + i, -1, 0)) * 0.5 for i in range(3)]
-    grad_y = [(at(3 + i, 0, 1) - at(3 + i, 0, -1)) * 0.5 for i in range(3)]
-    grad_z = [(z_next(at(3 + i, 0, 0)) - z_before(at(3 + i, 0, 0))) * 0.5 for i in range(3)]
+    grad_x, grad_y, grad_z = slopes(shifted(ext))
     stress_grad = (
         grad_x[0],
         grad_y[1],
@@ -145,14 +148,6 @@
     sgrad[:, 16:24, :] = jnp.zeros((24, 8, 128), F32)
     for s in range(6):
         sgrad[s * 4 : s * 4 + 4, 0:16, :] = -stress_grad[s]
-    for j in range(3):
-        velocity = [at(i, 0, 0) for i in range(3)]
-        slope = (grad_x, grad_y, grad_z)[j]
-        total = direct_ref[j] + viscosity * laplace(3 + j)
-        total = total + slope[0] * velocity[0] + slope[1] * velocity[1] + slope[2] * velocity[2]
-        total = total + grad_x[j] * velocity[0] + grad_y[j] * velocity[1] + grad_z[j] * velocity[2]
-        vg_ref[j] = total
-
     selection = sel_ref[...]
     inner = sel_ref[:, 128:640]
 
@@ -185,6 +180,8 @@
     hidden_grad = dot(rows_low, wout_ref[...], 1, 1)
     pre_grad = hidden_grad * (sigmoid_pre * (1.0 + pre_act * (1.0 - sigmoid_pre)))
     pre_low = pre_grad.astype(BF16)
+    hidden_ref[...] = hidden
+    pre_low_ref[...] = pre_low
     bias_in_sum = jnp.sum(pre_grad, axis=0, keepdims=True)
 
     weight_in_sum = dot(columns, pre_low, 1, 0)
@@ -203,7 +200,32 @@
     keep_ref[...] = flat[pl.ds(pl.multiple_of(core * HALF, 8), HALF), :]
     send_ref[...] = flat[pl.ds(pl.multiple_of((1 - core) * HALF, 8), HALF), :]
 
-    cgrad[...] = dot(win_ref[...], pre_low, 1, 1)
+
+def cells_kernel(
+    direct_ref, ext, hidden_ref, pre_low_ref, win_ref, wout_ref, bout_ref, sel_ref,
+    nv_ref, vg_ref, m1_ref, m2_ref, ylow_ref, yhigh_ref,
+    cgrad, rows, cpad, opad, ghost, tau,
+):
+    parity = lax.rem(lax.axis_index("y"), 2)
+    at = shifted(ext)
+    grad_x, grad_y, grad_z = slopes(at)
+    selection = sel_ref[...]
+    inner = sel_ref[:, 128:640]
+
+    def laplace(k):
+        middle = at(k, 0, 0)
+        total = at(k, 1, 0) + at(k, -1, 0) + at(k, 0, 1) + at(k, 0, -1)
+        return total + z_next(middle) + z_before(middle) - 6.0 * middle
+
+    for j in range(3):
+        velocity = [at(i, 0, 0) for i in range(3)]
+        slope = (grad_x, grad_y, grad_z)[j]
+        total = direct_ref[j] + viscosity * laplace(3 + j)
+        total = total + slope[0] * velocity[0] + slope[1] * velocity[1] + slope[2] * velocity[2]
+        total = total + grad_x[j] * velocity[0] + grad_y[j] * velocity[1] + grad_z[j] * velocity[2]
+        vg_ref[j] = total
+
+    cgrad[...] = dot(win_ref[...], pre_low_ref[...], 1, 1)
     for g in range(18):
         for z in range(6):
             cpad[g * 8 : g * 8 + 6, z * 128 : z * 128 + 128] = cgrad[
@@ -219,7 +241,7 @@
     for j in range(3):
         vg_ref[j] += ghost[j * 6 + 1 : j * 6 + 5, 1:17, :]
 
-    outputs = dot(hidden, wout_ref[...], 1, 0) + bout_ref[...]
+    outputs = dot(hidden_ref[...], wout_ref[...], 1, 0) + bout_ref[...]
     rows[...] = outputs.T
     for sa in range(24):
         for c in range(4):
@@ -281,7 +303,7 @@
 
 
 def end_kernel(
-    nv_ref, vg_ref, factor_ref, x1_ref, x2_ref, y1_ref, y2_ref, new_ref, grad_ref, done_ref, part
+    nv_ref, vg_ref, factor_ref, x1_ref, x2_ref, y1_ref, y2_ref, new_ref, grad_ref, part
 ):
     core = lax.axis_index("core")
     parity = lax.rem(lax.axis_index("y"), 2)
@@ -306,7 +328,6 @@
             part[x, 0:1, :] += y_low[spot : spot + 1]
             part[x, 15:16, :] += y_high[spot : spot + 1]
         grad_ref[i] = part[...]
-    done_ref[...] = y_low[0:8]
 
 
 def weights_kernel(scale, mine_ref, other_ref, win_ref, bin_ref, wout_ref, bout_ref):
@@ -328,10 +349,12 @@
     def write(first, second):
         for q in range(4):
             put(win_ref, q, q * WIN_ROWS, WIN_ROWS, first, second)
-            put(bin_ref, q, BIAS_BASE + q, 1, first, second)
+            row = second[BIAS_BASE + q - HALF, :]
+            bin_ref[q * 128 : q * 128 + 128] = row * scale
         for q in range(3):
             put(wout_ref, q, WOUT_BASE + q * 512, 512, first, second)
-            put(bout_ref, q, BIAS_BASE + 4 + q, 1, first, second)
+            row = second[BIAS_BASE + 4 + q - HALF, :]
+            bout_ref[q * 128 : q * 128 + 128] = row * scale
 
     @pl.when(core == 0)
     def _():
@@ -340,6 +363,10 @@
     @pl.when(core == 1)
     def _():
         write(other_ref, mine_ref)
+
+
+def add_kernel(first_ref, second_ref, after, out_ref):
+    out_ref[...] = first_ref[...] + second_ref[...]
 
 
 def across_kernel(got_ref, *rest):
@@ -372,7 +399,7 @@
         out_ref[i] = part[0:count, :]
 
 
-def call(kernel, outs, scratch=(), places=None, room=48):
+def call(kernel, outs, scratch=(), places=None, room=12):
     spaces = {"v": pltpu.VMEM, "h": pltpu.HBM, "a": pl.ANY}
     specs = {}
     if places is not None:
@@ -390,14 +417,6 @@
     )
 
 
-def in_order(array, first):
-    def kernel(array_ref, first_ref, out_ref):
-        out_ref[...] = array_ref[...]
-
-    (array,) = call(kernel, (array.shape,), (), "va", 12)(array, first)
-    return array
-
-
 def pairs(axes):
     count = lax.axis_size(axes)
     inner = [(i, i ^ 1) for i in range(count)]
@@ -434,55 +453,62 @@
         (pltpu.SemaphoreType.DMA((3,)),),
         "ahhh",
     )(m1, weight_in, weight_out, selection)
-    keep, send, nv, vg, m1, m2, ylow, yhigh = call(
+    hidden_type = jax.ShapeDtypeStruct((128, 512), BF16)
+    keep, send, ext, hidden, pre_low = call(
         main_kernel,
-        ((HALF, 128), (HALF, 128), field, field, layers, layers, rows, rows),
+        ((HALF, 128), (HALF, 128), (36, 24, 128), hidden_type, hidden_type),
+        ((24, 24, 128), (648, 128), (384, 128), (FLAT, 128)),
+        None,
+        24,
+    )(
+        velocity, direct, y1, y2, x1, x2,
+        weight_in, bias_in[None], weight_out, selection,
+    )
+    got = lax.ppermute(send, "core", swap)
+    nv, vg, m1, m2, ylow, yhigh = call(
+        cells_kernel,
+        (field, field, layers, layers, rows, rows),
         (
-            (36, 24, 128),
-            (24, 24, 128),
             (648, 128),
             (384, 128),
-            (648, 128),
             (144, 768),
             (192, 512),
             (18, 24, 128),
             (24, 32, 128),
-            (FLAT, 128),
         ),
-    )(
-        velocity, direct, y1, y2, x1, x2,
-        weight_in, bias_in[None], weight_out, bias_out[None], selection,
-    )
-
-    half = (keep + lax.ppermute(send, "core", swap)).reshape(parts, count, 128)
+        None,
+        16,
+    )(direct, ext, hidden, pre_low, weight_in, weight_out, bias_out[None], selection)
+
+    (half,) = call(add_kernel, (keep.shape,), (), "vva", 16)(keep, got, ylow)
+    half = half.reshape(parts, count, 128)
     got = lax.all_to_all(half, across, 0, 0)
     x1, x2 = exchange(m1, m2, GX)
     m1, m2 = call(side_kernel, (rows, rows), (rows, rows))(x1, x2, ylow, yhigh)
     cut = (depth, 1, short * 128)
     (part,) = call(across_kernel, (cut,), ((short * depth, 128),), "va", 12)(got, x2)
     got = lax.all_to_all(part, along, 0, 0)
-    (part,) = call(along_kernel, (cut,), (), "v", 12)(got)
+    y1, y2 = exchange(m1, m2, GY)
+    (part,) = call(along_kernel, (cut,), (), "vaa", 12)(got, y1, y2)
     got = lax.all_to_all(part, along, 0, 0)
     (half,) = call(spread_kernel, (half.shape,), ((short * depth, 128),), "v", 12)(got)
     mine = lax.all_to_all(half, across, 0, 0).reshape(HALF, 128)
-    y1, y2 = exchange(m1, m2, GY)
-    new_velocity, velocity_grad, done = call(
-        end_kernel, (field, field, (8, 128)), ((4, 16, 128),), None, 12
+    new_velocity, velocity_grad = call(
+        end_kernel, (field, field), ((4, 16, 128),), None, 12
     )(nv, vg, factor, x1, x2, y1, y2)
-    mine = in_order(mine, done)
     other = lax.ppermute(mine, "core", swap)
     blocks = 128 * lax.axis_size(GX) * lax.axis_size(GY)
     scale = float(blocks) ** -0.5
     weight_in_grad, bias_in_grad, weight_out_grad, bias_out_grad = call(
-        lambda *refs: weights_kernel(scale, *refs), ((648, 512), (1, 512), (512, 384), (1, 384))
+        lambda *refs: weights_kernel(scale, *refs), ((648, 512), (512,), (512, 384), (384,))
     )(mine, other)
     return (
         new_velocity,
         velocity_grad,
         weight_in_grad,
-        bias_in_grad[0],
+        bias_in_grad,
         weight_out_grad,
-        bias_out_grad[0],
+        bias_out_grad,
     )
 
 

time: 147 us -> 146 us (level)
  waiting for transfers between devices: 25.1 us -> 15 us
  blocking collectives: 35.4 us -> 41.2 us
  starting transfers between devices: 69 us -> 74.2 us
  other arithmetic: 1.7 us -> 0 us
    all_to_all x0 -> x1, blocking collectives: none -> 18 us  [on_device(): mine = lax.all_to_all(half, across, 0, 0).reshape(HALF, 128)]
    all_to_all x2 -> x1, blocking collectives: 35.4 us -> 23.2 us  [on_device(): got = lax.all_to_all(part, along, 0, 0)]
    ppermute x8, waiting for transfers between devices: 20.4 us -> 12.6 us  [exchange(): return (lax.ppermute(first, axes, inner), lax.ppermute(second, axes, outer))]
    ppermute x1, starting transfers between devices: 3.72 us -> 6.56 us  [on_device(): other = lax.ppermute(mine, 'core', swap)]
    all_to_all x1, starting transfers between devices: 6.56 us -> 9.27 us  [on_device(): got = lax.all_to_all(part, along, 0, 0)]
    ppermute x1, waiting for transfers between devices: 2.36 us -> 0.77 us  [on_device(): got = lax.ppermute(send, 'core', swap)]
    pallas_call x5 -> x6, Pallas kernels: 5.74 us -> 6.98 us  [the longest x1 1.9 us: on_device(): call(main_kernel, ((HALF, 128), (HALF, 128), (36, 24, 128), hidden_type,...]
    unnamed x16 -> x18, local copies, waits for them, and re-layouts: 5.67 us -> 5.68 us
  transfers between devices with their start and end apart: 12 -> 12, of which waited for: 6 -> 6; matrix products, arithmetic and copies ran while one was open for 0% -> 0% of each run, Pallas kernels for 1% -> 2%
where the time goes in v5:
time: 146 us; the launch traced here: 145 us
  starting transfers between devices  74.2 us (51%)
  blocking collectives  41.2 us (28%)
  waiting for transfers between devices  15 us (10%)
  Pallas kernels  8.36 us (6%)
  local copies, waits for them, and re-layouts  5.68 us (4%)
    ppermute x8, starting transfers between devices, exchange(): return (lax.ppermute(first, axes, inner), lax.ppermute(second, axes, outer))  50.1 us
    all_to_all x1, blocking collectives, on_device(): got = lax.all_to_all(part, along, 0, 0)  23.2 us
    all_to_all x1, blocking collectives, on_device(): mine = lax.all_to_all(half, across, 0, 0).reshape(HALF, 128)  18 us
    ppermute x8, waiting for transfers between devices, exchange(): return (lax.ppermute(first, axes, inner), lax.ppermute(second, axes, outer))  12.6 us
    all_to_all x1, starting transfers between devices, on_device(): got = lax.all_to_all(part, along, 0, 0)  9.27 us
    ppermute x1, starting transfers between devices, on_device(): other = lax.ppermute(mine, 'core', swap)  6.56 us
    unnamed x18, local copies, waits for them, and re-layouts  5.68 us
    ppermute x1, starting transfers between devices, on_device(): got = lax.ppermute(send, 'core', swap)  4.56 us
  transfers between devices with their start and end apart: 12, of which 6 were waited for; matrix products, arithmetic and copies ran while one was open for 0% of the time, Pallas kernels for 2%

profile of v5, /device:TPU:1, one launch (start us, length us, event | category | flops | bytes accessed | tf_op | source)
XLA Modules:
  0.0 145.3 jit_solution(8644816527217661371)
XLA Ops:
  0.6 0.0 copy-start
  0.6 0.9 copy-done
  1.5 0.8 copy-done.5
  2.3 0.8 copy-done.6
  3.1 0.0 copy-start.1
  3.1 0.0 copy-start.7
  3.1 8.9 %collective-permute-start = (f32[24,128]{1,0:T(8,128)S(1)}, f32[24,128]{1,0:T(8,128)S(1)}, u32[]{:S(2)}, u32[]{:S(2)}) collective-permute-start(f32[24,128]{1,0:T(8,128)S(1)} %get-tuple-element.35), channel_id=1, source_target_pairs={{0,1},{1,0},{2,3},{3,2},{4,5},{5,4},{6,7},{7,6},{8,9},{9,8},{10,11... | collective-permute-start | bytes 36872 | tf_op jit(solution)/shard_map/ppermute | solution.py:429
  12.1 1.9 %collective-permute-start.1 = (f32[24,128]{1,0:T(8,128)S(1)}, f32[24,128]{1,0:T(8,128)S(1)}, u32[]{:S(2)}, u32[]{:S(2)}) collective-permute-start(f32[24,128]{1,0:T(8,128)S(1)} %get-tuple-element.36), channel_id=1, source_target_pairs={{0,7},{1,2},{2,1},{3,4},{4,3},{5,6},{6,5},{7,0},{8,15},{9,10},{10,... | collective-permute-start | bytes 36872 | tf_op jit(solution)/shard_map/ppermute | solution.py:429
  14.0 0.0 collective-permute-done.r1_ref
  14.0 3.1 %collective-permute-done.1.r2_ref = f32[24,128]{1,0:T(8,128)S(1)} collective-permute-done((f32[24,128]{1,0:T(8,128)S(1)}, f32[24,128]{1,0:T(8,128)S(1)}, u32[]{:S(2)}, u32[]{:S(2)}) %collective-permute-start.1) | collective-permute-done | bytes 12320 | tf_op jit(solution)/shard_map/ppermute | solution.py:429
  17.1 11.7 %collective-permute-start.3 = (f32[6,24,128]{2,1,0:T(8,128)S(1)}, f32[6,24,128]{2,1,0:T(8,128)S(1)}, u32[]{:S(2)}, u32[]{:S(2)}) collective-permute-start(f32[6,24,128]{2,1,0:T(8,128)S(1)} %get-tuple-element.38), channel_id=1, source_target_pairs={{0,504},{8,16},{16,8},{24,32},{32,24},{40,48},{48,40},{56,64},{64,... | collective-permute-start | bytes 221192 | tf_op jit(solution)/shard_map/ppermute | solution.py:429
  28.8 1.9 %collective-permute-start.2 = (f32[6,24,128]{2,1,0:T(8,128)S(1)}, f32[6,24,128]{2,1,0:T(8,128)S(1)}, u32[]{:S(2)}, u32[]{:S(2)}) collective-permute-start(f32[6,24,128]{2,1,0:T(8,128)S(1)} %get-tuple-element.37.after), channel_id=1, source_target_pairs={{0,8},{8,0},{16,24},{24,16},{32,40},{40,32},{48,56},{56,48},{64,72... | collective-permute-start | bytes 221192 | tf_op jit(solution)/shard_map/ppermute | solution.py:429
  30.8 0.0 copy-start.2
  30.8 1.1 copy-done.2
  31.9 1.1 copy-done.3
  33.0 1.0 copy-done.4
  34.0 0.5 shard_map.129
  34.5 0.0 copy-start.8
  34.5 0.0 collective-permute-done.3.x2_ref
  34.5 0.0 collective-permute-done.2.x1_ref
  34.5 0.0 copy-done.1
  34.5 0.0 copy-done.7
  34.5 1.9 %shard_map.130 = (f32[2176,128]{1,0:T(8,128)S(1)}, f32[2176,128]{1,0:T(8,128)S(1)}, f32[36,24,128]{2,1,0:T(8,128)S(1)}, bf16[128,512]{1,0:T(8,128)(2,1)S(1)}, bf16[128,512]{1,0:T(8,128)(2,1)S(1)}) custom-call(f32[3,4,16,128]{3,2,1,0:T(8,128)S(1)} %copy-done.1, f32[3,4,16,128]{3,2,1,0:T(8,128)S(1)} %get-tuple-element.34.direct_ref, ...), custom_call_target="tpu_custom_call" | custom-call | tf_op jit(solution)/shard_map/pallas_call | solution.py:457
  36.5 4.6 %collective-permute-start.8 = (f32[2176,128]{1,0:T(8,128)S(1)}, f32[2176,128]{1,0:T(8,128)S(1)}, u32[]{:S(2)}, u32[]{:S(2)}) collective-permute-start(f32[2176,128]{1,0:T(8,128)S(1)} %get-tuple-element.57), channel_id=1, source_target_pairs={{0,1},{1,0},{2,3},{3,2},{4,5},{5,4},{6,7},{7,6},{8,9},{9,8},{10,11... | collective-permute-start | bytes 3342344 | tf_op jit(solution)/shard_map/ppermute | solution.py:467
  41.0 1.6 %shard_map.131 = (f32[3,4,16,128]{3,2,1,0:T(8,128)S(1)}, f32[3,4,16,128]{3,2,1,0:T(8,128)S(1)}, f32[6,24,128]{2,1,0:T(8,128)S(1)}, f32[6,24,128]{2,1,0:T(8,128)S...) custom-call(f32[3,4,16,128]{3,2,1,0:T(8,128)S(1)} %get-tuple-element.34.direct_ref, ...), custom_call_target="tpu_custom_call" | custom-call | tf_op jit(solution)/shard_map/pallas_call | solution.py:468
  42.6 0.8 collective-permute-done.8.second_ref
  43.4 1.1 shard_map.134
  44.5 3.7 %all-to-all-start = ((f32[16,136,128]{2,1,0:T(8,128)}), f32[16,136,128]{2,1,0:T(8,128)S(1)}, u32[]{:S(2)}, u32[]{:S(2)}) async-start(f32[16,136,128]{2,1,0:T(8,128)} %bitcast.1), calls=%async_computation | async-start | bytes 2228224 | tf_op jit(solution)/shard_map/all_to_all | solution.py:485
  48.2 13.6 %collective-permute-start.5 = (f32[6,24,128]{2,1,0:T(8,128)S(1)}, f32[6,24,128]{2,1,0:T(8,128)S(1)}, u32[]{:S(2)}, u32[]{:S(2)}) collective-permute-start(f32[6,24,128]{2,1,0:T(8,128)S(1)} %get-tuple-element.49), channel_id=1, source_target_pairs={{0,504},{8,16},{16,8},{24,32},{32,24},{40,48},{48,40},{56,64},{64,... | collective-permute-start | bytes 221192 | tf_op jit(solution)/shard_map/ppermute | solution.py:429
  61.8 6.2 %collective-permute-done.5.x2_ref.rest_0_ = f32[6,24,128]{2,1,0:T(8,128)S(1)} collective-permute-done((f32[6,24,128]{2,1,0:T(8,128)S(1)}, f32[6,24,128]{2,1,0:T(8,128)S(1)}, u32[]{:S(2)}, u32[]{:S(2)}) %collective-permute-start.5) | collective-permute-done | bytes 73760 | tf_op jit(solution)/shard_map/ppermute | solution.py:429
  68.0 0.0 all-to-all-done.got_ref
  68.0 0.7 shard_map.135
  68.7 9.3 %all-to-all-start.1 = ((f32[16,1,1152]{2,1,0:T(1,128)}), f32[16,1,1152]{2,1,0:T(1,128)S(1)}, u32[]{:S(2)}, u32[]{:S(2)}) async-start(f32[16,1,1152]{2,1,0:T(1,128)} %shard_map.135), calls=%async_computation.1 | async-start | bytes 147456 | tf_op jit(solution)/shard_map/all_to_all | solution.py:490
  78.0 3.3 %collective-permute-start.4 = (f32[6,24,128]{2,1,0:T(8,128)S(1)}, f32[6,24,128]{2,1,0:T(8,128)S(1)}, u32[]{:S(2)}, u32[]{:S(2)}) collective-permute-start(f32[6,24,128]{2,1,0:T(8,128)S(1)} %get-tuple-element.48), channel_id=1, source_target_pairs={{0,8},{8,0},{16,24},{24,16},{32,40},{40,32},{48,56},{56,48},{64,72... | collective-permute-start | bytes 221192 | tf_op jit(solution)/shard_map/ppermute | solution.py:429
  81.3 1.8 %collective-permute-done.4.x1_ref = f32[6,24,128]{2,1,0:T(8,128)S(1)} collective-permute-done((f32[6,24,128]{2,1,0:T(8,128)S(1)}, f32[6,24,128]{2,1,0:T(8,128)S(1)}, u32[]{:S(2)}, u32[]{:S(2)}) %collective-permute-start.4) | collective-permute-done | bytes 73760 | tf_op jit(solution)/shard_map/ppermute | solution.py:429
  83.1 5.3 %collective-permute-start.6 = (f32[24,128]{1,0:T(8,128)S(1)}, f32[24,128]{1,0:T(8,128)S(1)}, u32[]{:S(2)}, u32[]{:S(2)}) collective-permute-start(f32[24,128]{1,0:T(8,128)S(1)} %get-tuple-element.52), channel_id=1, source_target_pairs={{0,1},{1,0},{2,3},{3,2},{4,5},{5,4},{6,7},{7,6},{8,9},{9,8},{10,11... | collective-permute-start | bytes 36872 | tf_op jit(solution)/shard_map/ppermute | solution.py:429
  88.5 3.4 %collective-permute-start.7 = (f32[24,128]{1,0:T(8,128)S(1)}, f32[24,128]{1,0:T(8,128)S(1)}, u32[]{:S(2)}, u32[]{:S(2)}) collective-permute-start(f32[24,128]{1,0:T(8,128)S(1)} %get-tuple-element.53), channel_id=1, source_target_pairs={{0,7},{1,2},{2,1},{3,4},{4,3},{5,6},{6,5},{7,0},{8,15},{9,10},{10,... | collective-permute-start | bytes 36872 | tf_op jit(solution)/shard_map/ppermute | solution.py:429
  91.9 0.0 collective-permute-done.6.y1_ref.rest_0_
  91.9 1.6 %collective-permute-done.7.y2_ref.rest_1_ = f32[24,128]{1,0:T(8,128)S(1)} collective-permute-done((f32[24,128]{1,0:T(8,128)S(1)}, f32[24,128]{1,0:T(8,128)S(1)}, u32[]{:S(2)}, u32[]{:S(2)}) %collective-permute-start.7) | collective-permute-done | bytes 12320 | tf_op jit(solution)/shard_map/ppermute | solution.py:429
  93.5 0.0 all-to-all-done.1.got_ref
  93.5 0.1 shard_map.136
  93.5 23.2 %all_to_all.20.got_ref = f32[16,1,1152]{2,1,0:T(1,128)S(1)} all-to-all(f32[16,1,1152]{2,1,0:T(1,128)S(1)} %shard_map.136), channel_id=1, replica_groups=mesh['zh'=4,'x'=4,'y'=4,'zl'=4,'core'=2] {'zh','zl'}, dimensions={0} | all-to-all | bytes 147456 | tf_op jit(solution)/shard_map/all_to_all | solution.py:493
  116.8 0.1 shard_map.137
  116.9 18.0 %all_to_all.21 = f32[16,136,128]{2,1,0:T(8,128)S(1)} all-to-all(f32[16,136,128]{2,1,0:T(8,128)S(1)} %shard_map.137), channel_id=1, replica_groups=mesh['zh'=4,'x'=4,'y'=4,'zl'=4,'core'=2] {'x','y'}, dimensions={0} | all-to-all | bytes 2228224 | tf_op jit(solution)/shard_map/all_to_all | solution.py:495
  134.9 6.6 %collective-permute-start.9 = (f32[2176,128]{1,0:T(8,128)S(1)}, f32[2176,128]{1,0:T(8,128)S(1)}, u32[]{:S(2)}, u32[]{:S(2)}) collective-permute-start(f32[2176,128]{1,0:T(8,128)S(1)} %bitcast.3), channel_id=1, source_target_pairs={{0,1},{1,0},{2,3},{3,2},{4,5},{5,4},{6,7},{7,6},{8,9},{9,8},{10,11... | collective-permute-start | bytes 3342344 | tf_op jit(solution)/shard_map/ppermute | solution.py:499
  141.4 0.8 shard_map.133
  142.2 1.6 %collective-permute-done.9.refs_1_ = f32[2176,128]{1,0:T(8,128)S(1)} collective-permute-done((f32[2176,128]{1,0:T(8,128)S(1)}, f32[2176,128]{1,0:T(8,128)S(1)}, u32[]{:S(2)}, u32[]{:S(2)}) %collective-permute-start.9) | collective-permute-done | bytes 1114144 | tf_op jit(solution)/shard_map/ppermute | solution.py:499
  143.8 1.6 %shard_map.138 = (f32[648,512]{1,0:T(8,128)}, f32[512]{0:T(512)}, f32[512,384]{1,0:T(8,128)}, f32[384]{0:T(512)}) custom-call(f32[2176,128]{1,0:T(8,128)S(1)} %bitcast.4, f32[2176,128]{1,0:T(8,128)S(1)} %collective-permute-done.9.refs_1_), custom_call_target="tpu_custom_call" | custom-call | tf_op jit(solution)/shard_map/pallas_call | solution.py:502
  (9 shorter events, 0.1 us)
Async XLA Ops:
  0.6 0.9 copy-start
  1.5 0.8 copy-start.5
  2.3 0.8 copy-start.6
  3.1 31.4 %copy-start.1 = (f32[3,4,16,128]{3,2,1,0:T(8,128)S(1)}, f32[3,4,16,128]{3,2,1,0:T(8,128)}, u32[]{:S(2)}) copy-start(f32[3,4,16,128]{3,2,1,0:T(8,128)} %v_ref.5) | copy-start | bytes 294916
  3.1 31.4 %copy-start.7 = (f32[512]{0:T(512)S(1)}, f32[512]{0:T(512)}, u32[]{:S(2)}) copy-start(f32[512]{0:T(512)} %param.11) | copy-start | bytes 6148
  3.1 10.9 %collective-permute-start = (f32[24,128]{1,0:T(8,128)S(1)}, f32[24,128]{1,0:T(8,128)S(1)}, u32[]{:S(2)}, u32[]{:S(2)}) collective-permute-start(f32[24,128]{1,0:T(8,128)S(1)} %get-tuple-element.35), channel_id=1, source_target_pairs={{0,1},{1,0},{2,3},{3,2},{4,5},{5,4},{6,7},{7,6},{8,9},{9,8},{10,11... | collective-permute-start | bytes 36872 | tf_op jit(solution)/shard_map/ppermute | solution.py:429
  12.1 5.0 %collective-permute-start.1 = (f32[24,128]{1,0:T(8,128)S(1)}, f32[24,128]{1,0:T(8,128)S(1)}, u32[]{:S(2)}, u32[]{:S(2)}) collective-permute-start(f32[24,128]{1,0:T(8,128)S(1)} %get-tuple-element.36), channel_id=1, source_target_pairs={{0,7},{1,2},{2,1},{3,4},{4,3},{5,6},{6,5},{7,0},{8,15},{9,10},{10,... | collective-permute-start | bytes 36872 | tf_op jit(solution)/shard_map/ppermute | solution.py:429
  17.1 17.4 %collective-permute-start.3 = (f32[6,24,128]{2,1,0:T(8,128)S(1)}, f32[6,24,128]{2,1,0:T(8,128)S(1)}, u32[]{:S(2)}, u32[]{:S(2)}) collective-permute-start(f32[6,24,128]{2,1,0:T(8,128)S(1)} %get-tuple-element.38), channel_id=1, source_target_pairs={{0,504},{8,16},{16,8},{24,32},{32,24},{40,48},{48,40},{56,64},{64,... | collective-permute-start | bytes 221192 | tf_op jit(solution)/shard_map/ppermute | solution.py:429
  28.8 5.7 %collective-permute-start.2 = (f32[6,24,128]{2,1,0:T(8,128)S(1)}, f32[6,24,128]{2,1,0:T(8,128)S(1)}, u32[]{:S(2)}, u32[]{:S(2)}) collective-permute-start(f32[6,24,128]{2,1,0:T(8,128)S(1)} %get-tuple-element.37.after), channel_id=1, source_target_pairs={{0,8},{8,0},{16,24},{24,16},{32,40},{40,32},{48,56},{56,48},{64,72... | collective-permute-start | bytes 221192 | tf_op jit(solution)/shard_map/ppermute | solution.py:429
  30.8 1.1 copy-start.2
  31.9 1.1 copy-start.3
  33.0 1.0 copy-start.4
  34.5 6.5 %copy-start.8 = (f32[384]{0:T(512)S(1)}, f32[384]{0:T(512)}, u32[]{:S(2)}) copy-start(f32[384]{0:T(512)} %param.13) | copy-start | bytes 4612
  36.5 6.9 %collective-permute-start.8 = (f32[2176,128]{1,0:T(8,128)S(1)}, f32[2176,128]{1,0:T(8,128)S(1)}, u32[]{:S(2)}, u32[]{:S(2)}) collective-permute-start(f32[2176,128]{1,0:T(8,128)S(1)} %get-tuple-element.57), channel_id=1, source_target_pairs={{0,1},{1,0},{2,3},{3,2},{4,5},{5,4},{6,7},{7,6},{8,9},{9,8},{10,11... | collective-permute-start | bytes 3342344 | tf_op jit(solution)/shard_map/ppermute | solution.py:467
  44.5 23.5 %all-to-all-start = ((f32[16,136,128]{2,1,0:T(8,128)}), f32[16,136,128]{2,1,0:T(8,128)S(1)}, u32[]{:S(2)}, u32[]{:S(2)}) async-start(f32[16,136,128]{2,1,0:T(8,128)} %bitcast.1), calls=%async_computation | async-start | bytes 2228224 | tf_op jit(solution)/shard_map/all_to_all | solution.py:485
  48.2 19.8 %collective-permute-start.5 = (f32[6,24,128]{2,1,0:T(8,128)S(1)}, f32[6,24,128]{2,1,0:T(8,128)S(1)}, u32[]{:S(2)}, u32[]{:S(2)}) collective-permute-start(f32[6,24,128]{2,1,0:T(8,128)S(1)} %get-tuple-element.49), channel_id=1, source_target_pairs={{0,504},{8,16},{16,8},{24,32},{32,24},{40,48},{48,40},{56,64},{64,... | collective-permute-start | bytes 221192 | tf_op jit(solution)/shard_map/ppermute | solution.py:429
  68.7 24.8 %all-to-all-start.1 = ((f32[16,1,1152]{2,1,0:T(1,128)}), f32[16,1,1152]{2,1,0:T(1,128)S(1)}, u32[]{:S(2)}, u32[]{:S(2)}) async-start(f32[16,1,1152]{2,1,0:T(1,128)} %shard_map.135), calls=%async_computation.1 | async-start | bytes 147456 | tf_op jit(solution)/shard_map/all_to_all | solution.py:490
  78.0 5.1 %collective-permute-start.4 = (f32[6,24,128]{2,1,0:T(8,128)S(1)}, f32[6,24,128]{2,1,0:T(8,128)S(1)}, u32[]{:S(2)}, u32[]{:S(2)}) collective-permute-start(f32[6,24,128]{2,1,0:T(8,128)S(1)} %get-tuple-element.48), channel_id=1, source_target_pairs={{0,8},{8,0},{16,24},{24,16},{32,40},{40,32},{48,56},{56,48},{64,72... | collective-permute-start | bytes 221192 | tf_op jit(solution)/shard_map/ppermute | solution.py:429
  83.1 8.8 %collective-permute-start.6 = (f32[24,128]{1,0:T(8,128)S(1)}, f32[24,128]{1,0:T(8,128)S(1)}, u32[]{:S(2)}, u32[]{:S(2)}) collective-permute-start(f32[24,128]{1,0:T(8,128)S(1)} %get-tuple-element.52), channel_id=1, source_target_pairs={{0,1},{1,0},{2,3},{3,2},{4,5},{5,4},{6,7},{7,6},{8,9},{9,8},{10,11... | collective-permute-start | bytes 36872 | tf_op jit(solution)/shard_map/ppermute | solution.py:429
  88.5 5.0 %collective-permute-start.7 = (f32[24,128]{1,0:T(8,128)S(1)}, f32[24,128]{1,0:T(8,128)S(1)}, u32[]{:S(2)}, u32[]{:S(2)}) collective-permute-start(f32[24,128]{1,0:T(8,128)S(1)} %get-tuple-element.53), channel_id=1, source_target_pairs={{0,7},{1,2},{2,1},{3,4},{4,3},{5,6},{6,5},{7,0},{8,15},{9,10},{10,... | collective-permute-start | bytes 36872 | tf_op jit(solution)/shard_map/ppermute | solution.py:429
  134.9 8.9 %collective-permute-start.9 = (f32[2176,128]{1,0:T(8,128)S(1)}, f32[2176,128]{1,0:T(8,128)S(1)}, u32[]{:S(2)}, u32[]{:S(2)}) collective-permute-start(f32[2176,128]{1,0:T(8,128)S(1)} %bitcast.3), channel_id=1, source_target_pairs={{0,1},{1,0},{2,3},{3,2},{4,5},{5,4},{6,7},{7,6},{8,9},{9,8},{10,11... | collective-permute-start | bytes 3342344 | tf_op jit(solution)/shard_map/ppermute | solution.py:499

commit v6 on v5

--- a/solution.py
+++ b/solution.py
@@ -480,10 +480,10 @@
         16,
     )(direct, ext, hidden, pre_low, weight_in, weight_out, bias_out[None], selection)
 
-    (half,) = call(add_kernel, (keep.shape,), (), "vva", 16)(keep, got, ylow)
+    x1, x2 = exchange(m1, m2, GX)
+    (half,) = call(add_kernel, (keep.shape,), (), "vva", 16)(keep, got, x1)
     half = half.reshape(parts, count, 128)
     got = lax.all_to_all(half, across, 0, 0)
-    x1, x2 = exchange(m1, m2, GX)
     m1, m2 = call(side_kernel, (rows, rows), (rows, rows))(x1, x2, ylow, yhigh)
     cut = (depth, 1, short * 128)
     (part,) = call(across_kernel, (cut,), ((short * depth, 128),), "va", 12)(got, x2)

time: 146 us -> 145 us (level)
  waiting for transfers between devices: 15 us -> 16.9 us
  blocking collectives: 41.2 us -> 39.4 us
    all_to_all x1, blocking collectives: 23.2 us -> 21.3 us  [on_device(): got = lax.all_to_all(part, along, 0, 0)]
    all_to_all x1, waiting for transfers between devices: 0.01 us -> 1.62 us  [on_device(): got = lax.all_to_all(part, along, 0, 0)]
where the time goes in v6:
time: 145 us; the launch traced here: 144 us
  starting transfers between devices  72.9 us (50%)
  blocking collectives  39.4 us (27%)
  waiting for transfers between devices  16.9 us (12%)
  Pallas kernels  8.38 us (6%)
  local copies, waits for them, and re-layouts  5.68 us (4%)
    ppermute x8, starting transfers between devices, exchange(): return (lax.ppermute(first, axes, inner), lax.ppermute(second, axes, outer))  49.4 us
    all_to_all x1, blocking collectives, on_device(): got = lax.all_to_all(part, along, 0, 0)  21.3 us
    all_to_all x1, blocking collectives, on_device(): mine = lax.all_to_all(half, across, 0, 0).reshape(HALF, 128)  18.1 us
    ppermute x8, waiting for transfers between devices, exchange(): return (lax.ppermute(first, axes, inner), lax.ppermute(second, axes, outer))  13.7 us
    all_to_all x1, starting transfers between devices, on_device(): got = lax.all_to_all(part, along, 0, 0)  8.73 us
    ppermute x1, starting transfers between devices, on_device(): other = lax.ppermute(mine, 'core', swap)  6.56 us
    unnamed x18, local copies, waits for them, and re-layouts  5.68 us
    ppermute x1, starting transfers between devices, on_device(): got = lax.ppermute(send, 'core', swap)  4.56 us
  transfers between devices with their start and end apart: 12, of which 6 were waited for; matrix products, arithmetic and copies ran while one was open for 0% of the time, Pallas kernels for 2%

profile of v6, /device:TPU:1, one launch (start us, length us, event | category | flops | bytes accessed | tf_op | source)
XLA Modules:
  0.0 144.1 jit_solution(3790992758074468049)
XLA Ops:
  0.6 0.0 copy-start
  0.6 0.9 copy-done
  1.5 0.8 copy-done.5
  2.3 0.8 copy-done.6
  3.1 0.0 copy-start.1
  3.1 0.0 copy-start.7
  3.1 8.9 %collective-permute-start = (f32[24,128]{1,0:T(8,128)S(1)}, f32[24,128]{1,0:T(8,128)S(1)}, u32[]{:S(2)}, u32[]{:S(2)}) collective-permute-start(f32[24,128]{1,0:T(8,128)S(1)} %get-tuple-element.35), channel_id=1, source_target_pairs={{0,1},{1,0},{2,3},{3,2},{4,5},{5,4},{6,7},{7,6},{8,9},{9,8},{10,11... | collective-permute-start | bytes 36872 | tf_op jit(solution)/shard_map/ppermute | solution.py:429
  12.1 1.9 %collective-permute-start.1 = (f32[24,128]{1,0:T(8,128)S(1)}, f32[24,128]{1,0:T(8,128)S(1)}, u32[]{:S(2)}, u32[]{:S(2)}) collective-permute-start(f32[24,128]{1,0:T(8,128)S(1)} %get-tuple-element.36), channel_id=1, source_target_pairs={{0,7},{1,2},{2,1},{3,4},{4,3},{5,6},{6,5},{7,0},{8,15},{9,10},{10,... | collective-permute-start | bytes 36872 | tf_op jit(solution)/shard_map/ppermute | solution.py:429
  14.0 0.0 collective-permute-done.r1_ref
  14.0 3.1 %collective-permute-done.1.r2_ref = f32[24,128]{1,0:T(8,128)S(1)} collective-permute-done((f32[24,128]{1,0:T(8,128)S(1)}, f32[24,128]{1,0:T(8,128)S(1)}, u32[]{:S(2)}, u32[]{:S(2)}) %collective-permute-start.1) | collective-permute-done | bytes 12320 | tf_op jit(solution)/shard_map/ppermute | solution.py:429
  17.1 11.7 %collective-permute-start.3 = (f32[6,24,128]{2,1,0:T(8,128)S(1)}, f32[6,24,128]{2,1,0:T(8,128)S(1)}, u32[]{:S(2)}, u32[]{:S(2)}) collective-permute-start(f32[6,24,128]{2,1,0:T(8,128)S(1)} %get-tuple-element.38), channel_id=1, source_target_pairs={{0,504},{8,16},{16,8},{24,32},{32,24},{40,48},{48,40},{56,64},{64,... | collective-permute-start | bytes 221192 | tf_op jit(solution)/shard_map/ppermute | solution.py:429
  28.8 1.9 %collective-permute-start.2 = (f32[6,24,128]{2,1,0:T(8,128)S(1)}, f32[6,24,128]{2,1,0:T(8,128)S(1)}, u32[]{:S(2)}, u32[]{:S(2)}) collective-permute-start(f32[6,24,128]{2,1,0:T(8,128)S(1)} %get-tuple-element.37.after), channel_id=1, source_target_pairs={{0,8},{8,0},{16,24},{24,16},{32,40},{40,32},{48,56},{56,48},{64,72... | collective-permute-start | bytes 221192 | tf_op jit(solution)/shard_map/ppermute | solution.py:429
  30.8 0.0 copy-start.2
  30.8 1.1 copy-done.2
  31.9 1.1 copy-done.3
  33.0 1.0 copy-done.4
  34.0 0.5 shard_map.129
  34.5 0.0 copy-start.8
  34.5 0.0 collective-permute-done.3.x2_ref
  34.5 0.0 collective-permute-done.2.x1_ref
  34.5 0.0 copy-done.1
  34.5 0.0 copy-done.7
  34.5 1.9 %shard_map.130 = (f32[2176,128]{1,0:T(8,128)S(1)}, f32[2176,128]{1,0:T(8,128)S(1)}, f32[36,24,128]{2,1,0:T(8,128)S(1)}, bf16[128,512]{1,0:T(8,128)(2,1)S(1)}, bf16[128,512]{1,0:T(8,128)(2,1)S(1)}) custom-call(f32[3,4,16,128]{3,2,1,0:T(8,128)S(1)} %copy-done.1, f32[3,4,16,128]{3,2,1,0:T(8,128)S(1)} %get-tuple-element.34.direct_ref, ...), custom_call_target="tpu_custom_call" | custom-call | tf_op jit(solution)/shard_map/pallas_call | solution.py:457
  36.5 4.6 %collective-permute-start.8 = (f32[2176,128]{1,0:T(8,128)S(1)}, f32[2176,128]{1,0:T(8,128)S(1)}, u32[]{:S(2)}, u32[]{:S(2)}) collective-permute-start(f32[2176,128]{1,0:T(8,128)S(1)} %get-tuple-element.57), channel_id=1, source_target_pairs={{0,1},{1,0},{2,3},{3,2},{4,5},{5,4},{6,7},{7,6},{8,9},{9,8},{10,11... | collective-permute-start | bytes 3342344 | tf_op jit(solution)/shard_map/ppermute | solution.py:467
  41.0 1.6 %shard_map.131 = (f32[3,4,16,128]{3,2,1,0:T(8,128)S(1)}, f32[3,4,16,128]{3,2,1,0:T(8,128)S(1)}, f32[6,24,128]{2,1,0:T(8,128)S(1)}, f32[6,24,128]{2,1,0:T(8,128)S...) custom-call(f32[3,4,16,128]{3,2,1,0:T(8,128)S(1)} %get-tuple-element.34.direct_ref, ...), custom_call_target="tpu_custom_call" | custom-call | tf_op jit(solution)/shard_map/pallas_call | solution.py:468
  42.6 3.1 %collective-permute-start.4 = (f32[6,24,128]{2,1,0:T(8,128)S(1)}, f32[6,24,128]{2,1,0:T(8,128)S(1)}, u32[]{:S(2)}, u32[]{:S(2)}) collective-permute-start(f32[6,24,128]{2,1,0:T(8,128)S(1)} %get-tuple-element.48), channel_id=1, source_target_pairs={{0,8},{8,0},{16,24},{24,16},{32,40},{40,32},{48,56},{56,48},{64,72... | collective-permute-start | bytes 221192 | tf_op jit(solution)/shard_map/ppermute | solution.py:429
  45.7 2.7 %collective-permute-done.4.x1_ref.after = f32[6,24,128]{2,1,0:T(8,128)S(1)} collective-permute-done((f32[6,24,128]{2,1,0:T(8,128)S(1)}, f32[6,24,128]{2,1,0:T(8,128)S(1)}, u32[]{:S(2)}, u32[]{:S(2)}) %collective-permute-start.4) | collective-permute-done | bytes 73760 | tf_op jit(solution)/shard_map/ppermute | solution.py:429
  48.4 0.0 collective-permute-done.8.second_ref
  48.4 1.2 shard_map.134
  49.5 3.7 %all-to-all-start = ((f32[16,136,128]{2,1,0:T(8,128)}), f32[16,136,128]{2,1,0:T(8,128)S(1)}, u32[]{:S(2)}, u32[]{:S(2)}) async-start(f32[16,136,128]{2,1,0:T(8,128)} %bitcast.1), calls=%async_computation | async-start | bytes 2228224 | tf_op jit(solution)/shard_map/all_to_all | solution.py:486
  53.2 13.6 %collective-permute-start.5 = (f32[6,24,128]{2,1,0:T(8,128)S(1)}, f32[6,24,128]{2,1,0:T(8,128)S(1)}, u32[]{:S(2)}, u32[]{:S(2)}) collective-permute-start(f32[6,24,128]{2,1,0:T(8,128)S(1)} %get-tuple-element.49), channel_id=1, source_target_pairs={{0,504},{8,16},{16,8},{24,32},{32,24},{40,48},{48,40},{56,64},{64,... | collective-permute-start | bytes 221192 | tf_op jit(solution)/shard_map/ppermute | solution.py:429
  66.8 6.0 %collective-permute-done.5.x2_ref.rest_0_ = f32[6,24,128]{2,1,0:T(8,128)S(1)} collective-permute-done((f32[6,24,128]{2,1,0:T(8,128)S(1)}, f32[6,24,128]{2,1,0:T(8,128)S(1)}, u32[]{:S(2)}, u32[]{:S(2)}) %collective-permute-start.5) | collective-permute-done | bytes 73760 | tf_op jit(solution)/shard_map/ppermute | solution.py:429
  72.9 0.0 all-to-all-done.got_ref
  72.9 0.7 shard_map.135
  73.6 8.7 %all-to-all-start.1 = ((f32[16,1,1152]{2,1,0:T(1,128)}), f32[16,1,1152]{2,1,0:T(1,128)S(1)}, u32[]{:S(2)}, u32[]{:S(2)}) async-start(f32[16,1,1152]{2,1,0:T(1,128)} %shard_map.135), calls=%async_computation.1 | async-start | bytes 147456 | tf_op jit(solution)/shard_map/all_to_all | solution.py:490
  82.4 4.8 %collective-permute-start.6 = (f32[24,128]{1,0:T(8,128)S(1)}, f32[24,128]{1,0:T(8,128)S(1)}, u32[]{:S(2)}, u32[]{:S(2)}) collective-permute-start(f32[24,128]{1,0:T(8,128)S(1)} %get-tuple-element.52), channel_id=1, source_target_pairs={{0,1},{1,0},{2,3},{3,2},{4,5},{5,4},{6,7},{7,6},{8,9},{9,8},{10,11... | collective-permute-start | bytes 36872 | tf_op jit(solution)/shard_map/ppermute | solution.py:429
  87.2 3.4 %collective-permute-start.7 = (f32[24,128]{1,0:T(8,128)S(1)}, f32[24,128]{1,0:T(8,128)S(1)}, u32[]{:S(2)}, u32[]{:S(2)}) collective-permute-start(f32[24,128]{1,0:T(8,128)S(1)} %get-tuple-element.53), channel_id=1, source_target_pairs={{0,7},{1,2},{2,1},{3,4},{4,3},{5,6},{6,5},{7,0},{8,15},{9,10},{10,... | collective-permute-start | bytes 36872 | tf_op jit(solution)/shard_map/ppermute | solution.py:429
  90.6 0.0 collective-permute-done.6.y1_ref.rest_0_
  90.6 1.9 %collective-permute-done.7.y2_ref.rest_1_ = f32[24,128]{1,0:T(8,128)S(1)} collective-permute-done((f32[24,128]{1,0:T(8,128)S(1)}, f32[24,128]{1,0:T(8,128)S(1)}, u32[]{:S(2)}, u32[]{:S(2)}) %collective-permute-start.7) | collective-permute-done | bytes 12320 | tf_op jit(solution)/shard_map/ppermute | solution.py:429
  92.5 1.6 %all-to-all-done.1.got_ref = f32[16,1,1152]{2,1,0:T(1,128)S(1)} async-done(((f32[16,1,1152]{2,1,0:T(1,128)}), f32[16,1,1152]{2,1,0:T(1,128)S(1)}, u32[]{:S(2)}, u32[]{:S(2)}) %all-to-all-start.1) | async-done | bytes 73760 | tf_op jit(solution)/shard_map/all_to_all | solution.py:490
  94.1 0.1 shard_map.136
  94.2 21.3 %all_to_all.20.got_ref = f32[16,1,1152]{2,1,0:T(1,128)S(1)} all-to-all(f32[16,1,1152]{2,1,0:T(1,128)S(1)} %shard_map.136), channel_id=1, replica_groups=mesh['zh'=4,'x'=4,'y'=4,'zl'=4,'core'=2] {'zh','zl'}, dimensions={0} | all-to-all | bytes 147456 | tf_op jit(solution)/shard_map/all_to_all | solution.py:493
  115.5 0.1 shard_map.137
  115.6 18.1 %all_to_all.21 = f32[16,136,128]{2,1,0:T(8,128)S(1)} all-to-all(f32[16,136,128]{2,1,0:T(8,128)S(1)} %shard_map.137), channel_id=1, replica_groups=mesh['zh'=4,'x'=4,'y'=4,'zl'=4,'core'=2] {'x','y'}, dimensions={0} | all-to-all | bytes 2228224 | tf_op jit(solution)/shard_map/all_to_all | solution.py:495
  133.7 6.6 %collective-permute-start.9 = (f32[2176,128]{1,0:T(8,128)S(1)}, f32[2176,128]{1,0:T(8,128)S(1)}, u32[]{:S(2)}, u32[]{:S(2)}) collective-permute-start(f32[2176,128]{1,0:T(8,128)S(1)} %bitcast.3), channel_id=1, source_target_pairs={{0,1},{1,0},{2,3},{3,2},{4,5},{5,4},{6,7},{7,6},{8,9},{9,8},{10,11... | collective-permute-start | bytes 3342344 | tf_op jit(solution)/shard_map/ppermute | solution.py:499
  140.2 0.8 shard_map.133
  141.0 1.6 %collective-permute-done.9.refs_1_ = f32[2176,128]{1,0:T(8,128)S(1)} collective-permute-done((f32[2176,128]{1,0:T(8,128)S(1)}, f32[2176,128]{1,0:T(8,128)S(1)}, u32[]{:S(2)}, u32[]{:S(2)}) %collective-permute-start.9) | collective-permute-done | bytes 1114144 | tf_op jit(solution)/shard_map/ppermute | solution.py:499
  142.6 1.6 %shard_map.138 = (f32[648,512]{1,0:T(8,128)}, f32[512]{0:T(512)}, f32[512,384]{1,0:T(8,128)}, f32[384]{0:T(512)}) custom-call(f32[2176,128]{1,0:T(8,128)S(1)} %bitcast.4, f32[2176,128]{1,0:T(8,128)S(1)} %collective-permute-done.9.refs_1_), custom_call_target="tpu_custom_call" | custom-call | tf_op jit(solution)/shard_map/pallas_call | solution.py:502
  (9 shorter events, 0.1 us)
Async XLA Ops:
  0.6 0.9 copy-start
  1.5 0.8 copy-start.5
  2.3 0.8 copy-start.6
  3.1 31.4 %copy-start.1 = (f32[3,4,16,128]{3,2,1,0:T(8,128)S(1)}, f32[3,4,16,128]{3,2,1,0:T(8,128)}, u32[]{:S(2)}) copy-start(f32[3,4,16,128]{3,2,1,0:T(8,128)} %v_ref.5) | copy-start | bytes 294916
  3.1 31.4 %copy-start.7 = (f32[512]{0:T(512)S(1)}, f32[512]{0:T(512)}, u32[]{:S(2)}) copy-start(f32[512]{0:T(512)} %param.11) | copy-start | bytes 6148
  3.1 10.9 %collective-permute-start = (f32[24,128]{1,0:T(8,128)S(1)}, f32[24,128]{1,0:T(8,128)S(1)}, u32[]{:S(2)}, u32[]{:S(2)}) collective-permute-start(f32[24,128]{1,0:T(8,128)S(1)} %get-tuple-element.35), channel_id=1, source_target_pairs={{0,1},{1,0},{2,3},{3,2},{4,5},{5,4},{6,7},{7,6},{8,9},{9,8},{10,11... | collective-permute-start | bytes 36872 | tf_op jit(solution)/shard_map/ppermute | solution.py:429
  12.1 5.0 %collective-permute-start.1 = (f32[24,128]{1,0:T(8,128)S(1)}, f32[24,128]{1,0:T(8,128)S(1)}, u32[]{:S(2)}, u32[]{:S(2)}) collective-permute-start(f32[24,128]{1,0:T(8,128)S(1)} %get-tuple-element.36), channel_id=1, source_target_pairs={{0,7},{1,2},{2,1},{3,4},{4,3},{5,6},{6,5},{7,0},{8,15},{9,10},{10,... | collective-permute-start | bytes 36872 | tf_op jit(solution)/shard_map/ppermute | solution.py:429
  17.1 17.4 %collective-permute-start.3 = (f32[6,24,128]{2,1,0:T(8,128)S(1)}, f32[6,24,128]{2,1,0:T(8,128)S(1)}, u32[]{:S(2)}, u32[]{:S(2)}) collective-permute-start(f32[6,24,128]{2,1,0:T(8,128)S(1)} %get-tuple-element.38), channel_id=1, source_target_pairs={{0,504},{8,16},{16,8},{24,32},{32,24},{40,48},{48,40},{56,64},{64,... | collective-permute-start | bytes 221192 | tf_op jit(solution)/shard_map/ppermute | solution.py:429
  28.8 5.7 %collective-permute-start.2 = (f32[6,24,128]{2,1,0:T(8,128)S(1)}, f32[6,24,128]{2,1,0:T(8,128)S(1)}, u32[]{:S(2)}, u32[]{:S(2)}) collective-permute-start(f32[6,24,128]{2,1,0:T(8,128)S(1)} %get-tuple-element.37.after), channel_id=1, source_target_pairs={{0,8},{8,0},{16,24},{24,16},{32,40},{40,32},{48,56},{56,48},{64,72... | collective-permute-start | bytes 221192 | tf_op jit(solution)/shard_map/ppermute | solution.py:429
  30.8 1.1 copy-start.2
  31.9 1.1 copy-start.3
  33.0 1.0 copy-start.4
  34.5 6.5 %copy-start.8 = (f32[384]{0:T(512)S(1)}, f32[384]{0:T(512)}, u32[]{:S(2)}) copy-start(f32[384]{0:T(512)} %param.13) | copy-start | bytes 4612
  36.5 11.9 %collective-permute-start.8 = (f32[2176,128]{1,0:T(8,128)S(1)}, f32[2176,128]{1,0:T(8,128)S(1)}, u32[]{:S(2)}, u32[]{:S(2)}) collective-permute-start(f32[2176,128]{1,0:T(8,128)S(1)} %get-tuple-element.57), channel_id=1, source_target_pairs={{0,1},{1,0},{2,3},{3,2},{4,5},{5,4},{6,7},{7,6},{8,9},{9,8},{10,11... | collective-permute-start | bytes 3342344 | tf_op jit(solution)/shard_map/ppermute | solution.py:467
  42.6 5.8 %collective-permute-start.4 = (f32[6,24,128]{2,1,0:T(8,128)S(1)}, f32[6,24,128]{2,1,0:T(8,128)S(1)}, u32[]{:S(2)}, u32[]{:S(2)}) collective-permute-start(f32[6,24,128]{2,1,0:T(8,128)S(1)} %get-tuple-element.48), channel_id=1, source_target_pairs={{0,8},{8,0},{16,24},{24,16},{32,40},{40,32},{48,56},{56,48},{64,72... | collective-permute-start | bytes 221192 | tf_op jit(solution)/shard_map/ppermute | solution.py:429
  49.5 23.3 %all-to-all-start = ((f32[16,136,128]{2,1,0:T(8,128)}), f32[16,136,128]{2,1,0:T(8,128)S(1)}, u32[]{:S(2)}, u32[]{:S(2)}) async-start(f32[16,136,128]{2,1,0:T(8,128)} %bitcast.1), calls=%async_computation | async-start | bytes 2228224 | tf_op jit(solution)/shard_map/all_to_all | solution.py:486
  53.2 19.6 %collective-permute-start.5 = (f32[6,24,128]{2,1,0:T(8,128)S(1)}, f32[6,24,128]{2,1,0:T(8,128)S(1)}, u32[]{:S(2)}, u32[]{:S(2)}) collective-permute-start(f32[6,24,128]{2,1,0:T(8,128)S(1)} %get-tuple-element.49), channel_id=1, source_target_pairs={{0,504},{8,16},{16,8},{24,32},{32,24},{40,48},{48,40},{56,64},{64,... | collective-permute-start | bytes 221192 | tf_op jit(solution)/shard_map/ppermute | solution.py:429
  73.6 20.5 %all-to-all-start.1 = ((f32[16,1,1152]{2,1,0:T(1,128)}), f32[16,1,1152]{2,1,0:T(1,128)S(1)}, u32[]{:S(2)}, u32[]{:S(2)}) async-start(f32[16,1,1152]{2,1,0:T(1,128)} %shard_map.135), calls=%async_computation.1 | async-start | bytes 147456 | tf_op jit(solution)/shard_map/all_to_all | solution.py:490
  82.4 8.2 %collective-permute-start.6 = (f32[24,128]{1,0:T(8,128)S(1)}, f32[24,128]{1,0:T(8,128)S(1)}, u32[]{:S(2)}, u32[]{:S(2)}) collective-permute-start(f32[24,128]{1,0:T(8,128)S(1)} %get-tuple-element.52), channel_id=1, source_target_pairs={{0,1},{1,0},{2,3},{3,2},{4,5},{5,4},{6,7},{7,6},{8,9},{9,8},{10,11... | collective-permute-start | bytes 36872 | tf_op jit(solution)/shard_map/ppermute | solution.py:429
  87.2 5.3 %collective-permute-start.7 = (f32[24,128]{1,0:T(8,128)S(1)}, f32[24,128]{1,0:T(8,128)S(1)}, u32[]{:S(2)}, u32[]{:S(2)}) collective-permute-start(f32[24,128]{1,0:T(8,128)S(1)} %get-tuple-element.53), channel_id=1, source_target_pairs={{0,7},{1,2},{2,1},{3,4},{4,3},{5,6},{6,5},{7,0},{8,15},{9,10},{10,... | collective-permute-start | bytes 36872 | tf_op jit(solution)/shard_map/ppermute | solution.py:429
  133.7 8.9 %collective-permute-start.9 = (f32[2176,128]{1,0:T(8,128)S(1)}, f32[2176,128]{1,0:T(8,128)S(1)}, u32[]{:S(2)}, u32[]{:S(2)}) collective-permute-start(f32[2176,128]{1,0:T(8,128)S(1)} %bitcast.3), channel_id=1, source_target_pairs={{0,1},{1,0},{2,3},{3,2},{4,5},{5,4},{6,7},{7,6},{8,9},{9,8},{10,11... | collective-permute-start | bytes 3342344 | tf_op jit(solution)/shard_map/ppermute | solution.py:499

commit v7 on v5

--- a/solution.py
+++ b/solution.py
@@ -1,3 +1,5 @@
+import functools
+
 import jax
 import jax.numpy as jnp
 import numpy as np
@@ -330,7 +332,7 @@
         grad_ref[i] = part[...]
 
 
-def weights_kernel(scale, mine_ref, other_ref, win_ref, bin_ref, wout_ref, bout_ref):
+def weights_kernel(mine_ref, other_ref, win_ref, bin_ref, wout_ref, bout_ref):
     core = lax.axis_index("core")
 
     def put(out, lanes, start, count, first, second):
@@ -341,20 +343,20 @@
                 (first, spot, HALF - spot) if spot < HALF else (second, spot - HALF, count)
             )
             size = min(count - done, room)
-            out[done : done + size, lanes * 128 : lanes * 128 + 128] = (
-                source[spot : spot + size, :] * scale
-            )
+            out[done : done + size, lanes * 128 : lanes * 128 + 128] = source[
+                spot : spot + size, :
+            ]
             done += size
 
     def write(first, second):
         for q in range(4):
             put(win_ref, q, q * WIN_ROWS, WIN_ROWS, first, second)
             row = second[BIAS_BASE + q - HALF, :]
-            bin_ref[q * 128 : q * 128 + 128] = row * scale
+            bin_ref[q * 128 : q * 128 + 128] = row
         for q in range(3):
             put(wout_ref, q, WOUT_BASE + q * 512, 512, first, second)
             row = second[BIAS_BASE + 4 + q - HALF, :]
-            bout_ref[q * 128 : q * 128 + 128] = row * scale
+            bout_ref[q * 128 : q * 128 + 128] = row
 
     @pl.when(core == 0)
     def _():
@@ -381,9 +383,9 @@
             out_ref[i, 0:1, j * 128 : j * 128 + 128] = part[i * short + j : i * short + j + 1, :]
 
 
-def along_kernel(got_ref, *rest):
+def along_kernel(scale, got_ref, *rest):
     out_ref = rest[-1]
-    total = jnp.sum(got_ref[...], axis=0, keepdims=True)
+    total = jnp.sum(got_ref[...], axis=0, keepdims=True) * scale
     out_ref[...] = jnp.broadcast_to(total, out_ref.shape)
 
 
@@ -480,16 +482,20 @@
         16,
     )(direct, ext, hidden, pre_low, weight_in, weight_out, bias_out[None], selection)
 
+    inner, outer = pairs(GX)
+    x2 = lax.ppermute(m2, GX, outer)
+    x1 = lax.ppermute(m1, GX, inner)
     (half,) = call(add_kernel, (keep.shape,), (), "vva", 16)(keep, got, ylow)
     half = half.reshape(parts, count, 128)
     got = lax.all_to_all(half, across, 0, 0)
-    x1, x2 = exchange(m1, m2, GX)
     m1, m2 = call(side_kernel, (rows, rows), (rows, rows))(x1, x2, ylow, yhigh)
     cut = (depth, 1, short * 128)
-    (part,) = call(across_kernel, (cut,), ((short * depth, 128),), "va", 12)(got, x2)
+    (part,) = call(across_kernel, (cut,), ((short * depth, 128),), "vaa", 12)(got, x2, x1)
     got = lax.all_to_all(part, along, 0, 0)
     y1, y2 = exchange(m1, m2, GY)
-    (part,) = call(along_kernel, (cut,), (), "vaa", 12)(got, y1, y2)
+    blocks = 128 * lax.axis_size(GX) * lax.axis_size(GY)
+    scaled = functools.partial(along_kernel, float(blocks) ** -0.5)
+    (part,) = call(scaled, (cut,), (), "vaa", 12)(got, y1, y2)
     got = lax.all_to_all(part, along, 0, 0)
     (half,) = call(spread_kernel, (half.shape,), ((short * depth, 128),), "v", 12)(got)
     mine = lax.all_to_all(half, across, 0, 0).reshape(HALF, 128)
@@ -497,10 +503,8 @@
         end_kernel, (field, field), ((4, 16, 128),), None, 12
     )(nv, vg, factor, x1, x2, y1, y2)
     other = lax.ppermute(mine, "core", swap)
-    blocks = 128 * lax.axis_size(GX) * lax.axis_size(GY)
-    scale = float(blocks) ** -0.5
     weight_in_grad, bias_in_grad, weight_out_grad, bias_out_grad = call(
-        lambda *refs: weights_kernel(scale, *refs), ((648, 512), (512,), (512, 384), (384,))
+        weights_kernel, ((648, 512), (512,), (512, 384), (384,))
     )(mine, other)
     return (
         new_velocity,

time: 146 us -> 142 us (0.973)
  waiting for transfers between devices: 15 us -> 11.3 us
    ppermute x8 -> x6, starting transfers between devices: 50.1 us -> 32.6 us  [exchange(): return (lax.ppermute(first, axes, inner), lax.ppermute(second, axes, outer))]
    ppermute x0 -> x2, starting transfers between devices: none -> 16 us  [the longest x1 12.9 us: on_device(): x2 = lax.ppermute(m2, GX, outer)]
    ppermute x8 -> x6, waiting for transfers between devices: 12.6 us -> 4.94 us  [exchange(): return (lax.ppermute(first, axes, inner), lax.ppermute(second, axes, outer))]
    all_to_all x1, blocking collectives: 18 us -> 20.3 us  [on_device(): mine = lax.all_to_all(half, across, 0, 0).reshape(HALF, 128)]
    ppermute x0 -> x2, waiting for transfers between devices: none -> 2.26 us  [the longest x1 2.26 us: on_device(): x2 = lax.ppermute(m2, GX, outer)]
    all_to_all x1, blocking collectives: 23.2 us -> 21.2 us  [on_device(): got = lax.all_to_all(part, along, 0, 0)]
    all_to_all x1, waiting for transfers between devices: 0.01 us -> 1.72 us  [on_device(): got = lax.all_to_all(part, along, 0, 0)]
where the time goes in v7:
time: 142 us
  starting transfers between devices  73.8 us (52%)
  blocking collectives  41.5 us (29%)
  waiting for transfers between devices  11.3 us (8%)
  Pallas kernels  8.36 us (6%)
  local copies, waits for them, and re-layouts  5.68 us (4%)
    ppermute x6, starting transfers between devices, exchange(): return (lax.ppermute(first, axes, inner), lax.ppermute(second, axes, outer))  32.6 us
    all_to_all x1, blocking collectives, on_device(): got = lax.all_to_all(part, along, 0, 0)  21.2 us
    all_to_all x1, blocking collectives, on_device(): mine = lax.all_to_all(half, across, 0, 0).reshape(HALF, 128)  20.3 us
    ppermute x1, starting transfers between devices, on_device(): x2 = lax.ppermute(m2, GX, outer)  12.9 us
    all_to_all x1, starting transfers between devices, on_device(): got = lax.all_to_all(part, along, 0, 0)  10.4 us
    ppermute x1, starting transfers between devices, on_device(): other = lax.ppermute(mine, 'core', swap)  6.56 us
    unnamed x18, local copies, waits for them, and re-layouts  5.68 us
    ppermute x6, waiting for transfers between devices, exchange(): return (lax.ppermute(first, axes, inner), lax.ppermute(second, axes, outer))  4.94 us
  transfers between devices with their start and end apart: 12, of which 6 were waited for; matrix products, arithmetic and copies ran while one was open for 0% of the time, Pallas kernels for 2%

profile of v7, /device:TPU:1, one launch (start us, length us, event | category | flops | bytes accessed | tf_op | source)
XLA Modules:
  0.0 141.6 jit_solution(13396689513159574412)
XLA Ops:
  0.6 0.0 copy-start
  0.6 0.9 copy-done
  1.5 0.8 copy-done.5
  2.3 0.8 copy-done.6
  3.1 0.0 copy-start.1
  3.1 0.0 copy-start.7
  3.1 8.9 %collective-permute-start = (f32[24,128]{1,0:T(8,128)S(1)}, f32[24,128]{1,0:T(8,128)S(1)}, u32[]{:S(2)}, u32[]{:S(2)}) collective-permute-start(f32[24,128]{1,0:T(8,128)S(1)} %get-tuple-element.35), channel_id=1, source_target_pairs={{0,1},{1,0},{2,3},{3,2},{4,5},{5,4},{6,7},{7,6},{8,9},{9,8},{10,11... | collective-permute-start | bytes 36872 | tf_op jit(solution)/shard_map/ppermute | solution.py:431
  12.1 1.9 %collective-permute-start.1 = (f32[24,128]{1,0:T(8,128)S(1)}, f32[24,128]{1,0:T(8,128)S(1)}, u32[]{:S(2)}, u32[]{:S(2)}) collective-permute-start(f32[24,128]{1,0:T(8,128)S(1)} %get-tuple-element.36), channel_id=1, source_target_pairs={{0,7},{1,2},{2,1},{3,4},{4,3},{5,6},{6,5},{7,0},{8,15},{9,10},{10,... | collective-permute-start | bytes 36872 | tf_op jit(solution)/shard_map/ppermute | solution.py:431
  14.0 0.0 collective-permute-done.r1_ref
  14.0 3.1 %collective-permute-done.1.r2_ref = f32[24,128]{1,0:T(8,128)S(1)} collective-permute-done((f32[24,128]{1,0:T(8,128)S(1)}, f32[24,128]{1,0:T(8,128)S(1)}, u32[]{:S(2)}, u32[]{:S(2)}) %collective-permute-start.1) | collective-permute-done | bytes 12320 | tf_op jit(solution)/shard_map/ppermute | solution.py:431
  17.1 11.7 %collective-permute-start.3 = (f32[6,24,128]{2,1,0:T(8,128)S(1)}, f32[6,24,128]{2,1,0:T(8,128)S(1)}, u32[]{:S(2)}, u32[]{:S(2)}) collective-permute-start(f32[6,24,128]{2,1,0:T(8,128)S(1)} %get-tuple-element.38), channel_id=1, source_target_pairs={{0,504},{8,16},{16,8},{24,32},{32,24},{40,48},{48,40},{56,64},{64,... | collective-permute-start | bytes 221192 | tf_op jit(solution)/shard_map/ppermute | solution.py:431
  28.8 1.9 %collective-permute-start.2 = (f32[6,24,128]{2,1,0:T(8,128)S(1)}, f32[6,24,128]{2,1,0:T(8,128)S(1)}, u32[]{:S(2)}, u32[]{:S(2)}) collective-permute-start(f32[6,24,128]{2,1,0:T(8,128)S(1)} %get-tuple-element.37.after), channel_id=1, source_target_pairs={{0,8},{8,0},{16,24},{24,16},{32,40},{40,32},{48,56},{56,48},{64,72... | collective-permute-start | bytes 221192 | tf_op jit(solution)/shard_map/ppermute | solution.py:431
  30.8 0.0 copy-start.2
  30.8 1.1 copy-done.2
  31.9 1.1 copy-done.3
  33.0 1.0 copy-done.4
  34.0 0.5 shard_map.129
  34.5 0.0 copy-start.8
  34.5 0.0 collective-permute-done.3.x2_ref
  34.5 0.0 collective-permute-done.2.x1_ref
  34.5 0.0 copy-done.1
  34.5 0.0 copy-done.7
  34.5 1.9 %shard_map.130 = (f32[2176,128]{1,0:T(8,128)S(1)}, f32[2176,128]{1,0:T(8,128)S(1)}, f32[36,24,128]{2,1,0:T(8,128)S(1)}, bf16[128,512]{1,0:T(8,128)(2,1)S(1)}, bf16[128,512]{1,0:T(8,128)(2,1)S(1)}) custom-call(f32[3,4,16,128]{3,2,1,0:T(8,128)S(1)} %copy-done.1, f32[3,4,16,128]{3,2,1,0:T(8,128)S(1)} %get-tuple-element.34.direct_ref, ...), custom_call_target="tpu_custom_call" | custom-call | tf_op jit(solution)/shard_map/pallas_call | solution.py:459
  36.5 4.6 %collective-permute-start.8 = (f32[2176,128]{1,0:T(8,128)S(1)}, f32[2176,128]{1,0:T(8,128)S(1)}, u32[]{:S(2)}, u32[]{:S(2)}) collective-permute-start(f32[2176,128]{1,0:T(8,128)S(1)} %get-tuple-element.57), channel_id=1, source_target_pairs={{0,1},{1,0},{2,3},{3,2},{4,5},{5,4},{6,7},{7,6},{8,9},{9,8},{10,11... | collective-permute-start | bytes 3342344 | tf_op jit(solution)/shard_map/ppermute | solution.py:469
  41.0 1.6 %shard_map.131 = (f32[3,4,16,128]{3,2,1,0:T(8,128)S(1)}, f32[3,4,16,128]{3,2,1,0:T(8,128)S(1)}, f32[6,24,128]{2,1,0:T(8,128)S(1)}, f32[6,24,128]{2,1,0:T(8,128)S...) custom-call(f32[3,4,16,128]{3,2,1,0:T(8,128)S(1)} %get-tuple-element.34.direct_ref, ...), custom_call_target="tpu_custom_call" | custom-call | tf_op jit(solution)/shard_map/pallas_call | solution.py:470
  42.6 0.8 collective-permute-done.8.second_ref
  43.4 1.1 shard_map.134
  44.5 3.7 %all-to-all-start = ((f32[16,136,128]{2,1,0:T(8,128)}), f32[16,136,128]{2,1,0:T(8,128)S(1)}, u32[]{:S(2)}, u32[]{:S(2)}) async-start(f32[16,136,128]{2,1,0:T(8,128)} %bitcast.1), calls=%async_computation | async-start | bytes 2228224 | tf_op jit(solution)/shard_map/all_to_all | solution.py:490
  48.2 3.1 %collective-permute-start.4 = (f32[6,24,128]{2,1,0:T(8,128)S(1)}, f32[6,24,128]{2,1,0:T(8,128)S(1)}, u32[]{:S(2)}, u32[]{:S(2)}) collective-permute-start(f32[6,24,128]{2,1,0:T(8,128)S(1)} %get-tuple-element.48), channel_id=1, source_target_pairs={{0,8},{8,0},{16,24},{24,16},{32,40},{40,32},{48,56},{56,48},{64,72... | collective-permute-start | bytes 221192 | tf_op jit(solution)/shard_map/ppermute | solution.py:487
  51.4 12.9 %collective-permute-start.5 = (f32[6,24,128]{2,1,0:T(8,128)S(1)}, f32[6,24,128]{2,1,0:T(8,128)S(1)}, u32[]{:S(2)}, u32[]{:S(2)}) collective-permute-start(f32[6,24,128]{2,1,0:T(8,128)S(1)} %get-tuple-element.49), channel_id=1, source_target_pairs={{0,504},{8,16},{16,8},{24,32},{32,24},{40,48},{48,40},{56,64},{64,... | collective-permute-start | bytes 221192 | tf_op jit(solution)/shard_map/ppermute | solution.py:486
  64.3 0.0 collective-permute-done.4.x1_ref.rest_1_
  64.3 2.3 %collective-permute-done.5.x2_ref.rest_0_ = f32[6,24,128]{2,1,0:T(8,128)S(1)} collective-permute-done((f32[6,24,128]{2,1,0:T(8,128)S(1)}, f32[6,24,128]{2,1,0:T(8,128)S(1)}, u32[]{:S(2)}, u32[]{:S(2)}) %collective-permute-start.5) | collective-permute-done | bytes 73760 | tf_op jit(solution)/shard_map/ppermute | solution.py:486
  66.5 0.0 all-to-all-done.got_ref
  66.5 0.7 shard_map.135
  67.3 10.4 %all-to-all-start.1 = ((f32[16,1,1152]{2,1,0:T(1,128)}), f32[16,1,1152]{2,1,0:T(1,128)S(1)}, u32[]{:S(2)}, u32[]{:S(2)}) async-start(f32[16,1,1152]{2,1,0:T(1,128)} %shard_map.135), calls=%async_computation.1 | async-start | bytes 147456 | tf_op jit(solution)/shard_map/all_to_all | solution.py:494
  77.8 4.6 %collective-permute-start.6 = (f32[24,128]{1,0:T(8,128)S(1)}, f32[24,128]{1,0:T(8,128)S(1)}, u32[]{:S(2)}, u32[]{:S(2)}) collective-permute-start(f32[24,128]{1,0:T(8,128)S(1)} %get-tuple-element.52), channel_id=1, source_target_pairs={{0,1},{1,0},{2,3},{3,2},{4,5},{5,4},{6,7},{7,6},{8,9},{9,8},{10,11... | collective-permute-start | bytes 36872 | tf_op jit(solution)/shard_map/ppermute | solution.py:431
  82.4 3.4 %collective-permute-start.7 = (f32[24,128]{1,0:T(8,128)S(1)}, f32[24,128]{1,0:T(8,128)S(1)}, u32[]{:S(2)}, u32[]{:S(2)}) collective-permute-start(f32[24,128]{1,0:T(8,128)S(1)} %get-tuple-element.53), channel_id=1, source_target_pairs={{0,7},{1,2},{2,1},{3,4},{4,3},{5,6},{6,5},{7,0},{8,15},{9,10},{10,... | collective-permute-start | bytes 36872 | tf_op jit(solution)/shard_map/ppermute | solution.py:431
  85.8 0.0 collective-permute-done.6.y1_ref.rest_0_
  85.9 1.9 %collective-permute-done.7.y2_ref.rest_1_ = f32[24,128]{1,0:T(8,128)S(1)} collective-permute-done((f32[24,128]{1,0:T(8,128)S(1)}, f32[24,128]{1,0:T(8,128)S(1)}, u32[]{:S(2)}, u32[]{:S(2)}) %collective-permute-start.7) | collective-permute-done | bytes 12320 | tf_op jit(solution)/shard_map/ppermute | solution.py:431
  87.7 1.7 %all-to-all-done.1.got_ref = f32[16,1,1152]{2,1,0:T(1,128)S(1)} async-done(((f32[16,1,1152]{2,1,0:T(1,128)}), f32[16,1,1152]{2,1,0:T(1,128)S(1)}, u32[]{:S(2)}, u32[]{:S(2)}) %all-to-all-start.1) | async-done | bytes 73760 | tf_op jit(solution)/shard_map/all_to_all | solution.py:494
  89.4 0.1 shard_map.136
  89.5 21.2 %all_to_all.20.got_ref = f32[16,1,1152]{2,1,0:T(1,128)S(1)} all-to-all(f32[16,1,1152]{2,1,0:T(1,128)S(1)} %shard_map.136), channel_id=1, replica_groups=mesh['zh'=4,'x'=4,'y'=4,'zl'=4,'core'=2] {'zh','zl'}, dimensions={0} | all-to-all | bytes 147456 | tf_op jit(solution)/shard_map/all_to_all | solution.py:499
  110.7 0.1 shard_map.137
  110.8 20.3 %all_to_all.21 = f32[16,136,128]{2,1,0:T(8,128)S(1)} all-to-all(f32[16,136,128]{2,1,0:T(8,128)S(1)} %shard_map.137), channel_id=1, replica_groups=mesh['zh'=4,'x'=4,'y'=4,'zl'=4,'core'=2] {'x','y'}, dimensions={0} | all-to-all | bytes 2228224 | tf_op jit(solution)/shard_map/all_to_all | solution.py:501
  131.1 6.6 %collective-permute-start.9 = (f32[2176,128]{1,0:T(8,128)S(1)}, f32[2176,128]{1,0:T(8,128)S(1)}, u32[]{:S(2)}, u32[]{:S(2)}) collective-permute-start(f32[2176,128]{1,0:T(8,128)S(1)} %bitcast.3), channel_id=1, source_target_pairs={{0,1},{1,0},{2,3},{3,2},{4,5},{5,4},{6,7},{7,6},{8,9},{9,8},{10,11... | collective-permute-start | bytes 3342344 | tf_op jit(solution)/shard_map/ppermute | solution.py:505
  137.7 0.8 shard_map.133
  138.4 1.6 %collective-permute-done.9.other_ref = f32[2176,128]{1,0:T(8,128)S(1)} collective-permute-done((f32[2176,128]{1,0:T(8,128)S(1)}, f32[2176,128]{1,0:T(8,128)S(1)}, u32[]{:S(2)}, u32[]{:S(2)}) %collective-permute-start.9) | collective-permute-done | bytes 1114144 | tf_op jit(solution)/shard_map/ppermute | solution.py:505
  140.0 1.6 %shard_map.138 = (f32[648,512]{1,0:T(8,128)}, f32[512]{0:T(512)}, f32[512,384]{1,0:T(8,128)}, f32[384]{0:T(512)}) custom-call(f32[2176,128]{1,0:T(8,128)S(1)} %bitcast.4, f32[2176,128]{1,0:T(8,128)S(1)} %collective-permute-done.9.other_ref), custom_call_target="tpu_custom_call" | custom-call | tf_op jit(solution)/shard_map/pallas_call | solution.py:506
  (9 shorter events, 0.1 us)
Async XLA Ops:
  0.6 0.9 copy-start
  1.5 0.8 copy-start.5
  2.3 0.8 copy-start.6
  3.1 31.4 %copy-start.1 = (f32[3,4,16,128]{3,2,1,0:T(8,128)S(1)}, f32[3,4,16,128]{3,2,1,0:T(8,128)}, u32[]{:S(2)}) copy-start(f32[3,4,16,128]{3,2,1,0:T(8,128)} %v_ref.5) | copy-start | bytes 294916
  3.1 31.4 %copy-start.7 = (f32[512]{0:T(512)S(1)}, f32[512]{0:T(512)}, u32[]{:S(2)}) copy-start(f32[512]{0:T(512)} %param.11) | copy-start | bytes 6148
  3.1 10.9 %collective-permute-start = (f32[24,128]{1,0:T(8,128)S(1)}, f32[24,128]{1,0:T(8,128)S(1)}, u32[]{:S(2)}, u32[]{:S(2)}) collective-permute-start(f32[24,128]{1,0:T(8,128)S(1)} %get-tuple-element.35), channel_id=1, source_target_pairs={{0,1},{1,0},{2,3},{3,2},{4,5},{5,4},{6,7},{7,6},{8,9},{9,8},{10,11... | collective-permute-start | bytes 36872 | tf_op jit(solution)/shard_map/ppermute | solution.py:431
  12.1 5.0 %collective-permute-start.1 = (f32[24,128]{1,0:T(8,128)S(1)}, f32[24,128]{1,0:T(8,128)S(1)}, u32[]{:S(2)}, u32[]{:S(2)}) collective-permute-start(f32[24,128]{1,0:T(8,128)S(1)} %get-tuple-element.36), channel_id=1, source_target_pairs={{0,7},{1,2},{2,1},{3,4},{4,3},{5,6},{6,5},{7,0},{8,15},{9,10},{10,... | collective-permute-start | bytes 36872 | tf_op jit(solution)/shard_map/ppermute | solution.py:431
  17.1 17.4 %collective-permute-start.3 = (f32[6,24,128]{2,1,0:T(8,128)S(1)}, f32[6,24,128]{2,1,0:T(8,128)S(1)}, u32[]{:S(2)}, u32[]{:S(2)}) collective-permute-start(f32[6,24,128]{2,1,0:T(8,128)S(1)} %get-tuple-element.38), channel_id=1, source_target_pairs={{0,504},{8,16},{16,8},{24,32},{32,24},{40,48},{48,40},{56,64},{64,... | collective-permute-start | bytes 221192 | tf_op jit(solution)/shard_map/ppermute | solution.py:431
  28.8 5.7 %collective-permute-start.2 = (f32[6,24,128]{2,1,0:T(8,128)S(1)}, f32[6,24,128]{2,1,0:T(8,128)S(1)}, u32[]{:S(2)}, u32[]{:S(2)}) collective-permute-start(f32[6,24,128]{2,1,0:T(8,128)S(1)} %get-tuple-element.37.after), channel_id=1, source_target_pairs={{0,8},{8,0},{16,24},{24,16},{32,40},{40,32},{48,56},{56,48},{64,72... | collective-permute-start | bytes 221192 | tf_op jit(solution)/shard_map/ppermute | solution.py:431
  30.8 1.1 copy-start.2
  31.9 1.1 copy-start.3
  33.0 1.0 copy-start.4
  34.5 6.5 %copy-start.8 = (f32[384]{0:T(512)S(1)}, f32[384]{0:T(512)}, u32[]{:S(2)}) copy-start(f32[384]{0:T(512)} %param.13) | copy-start | bytes 4612
  36.5 6.9 %collective-permute-start.8 = (f32[2176,128]{1,0:T(8,128)S(1)}, f32[2176,128]{1,0:T(8,128)S(1)}, u32[]{:S(2)}, u32[]{:S(2)}) collective-permute-start(f32[2176,128]{1,0:T(8,128)S(1)} %get-tuple-element.57), channel_id=1, source_target_pairs={{0,1},{1,0},{2,3},{3,2},{4,5},{5,4},{6,7},{7,6},{8,9},{9,8},{10,11... | collective-permute-start | bytes 3342344 | tf_op jit(solution)/shard_map/ppermute | solution.py:469
  44.5 22.0 %all-to-all-start = ((f32[16,136,128]{2,1,0:T(8,128)}), f32[16,136,128]{2,1,0:T(8,128)S(1)}, u32[]{:S(2)}, u32[]{:S(2)}) async-start(f32[16,136,128]{2,1,0:T(8,128)} %bitcast.1), calls=%async_computation | async-start | bytes 2228224 | tf_op jit(solution)/shard_map/all_to_all | solution.py:490
  48.2 16.1 %collective-permute-start.4 = (f32[6,24,128]{2,1,0:T(8,128)S(1)}, f32[6,24,128]{2,1,0:T(8,128)S(1)}, u32[]{:S(2)}, u32[]{:S(2)}) collective-permute-start(f32[6,24,128]{2,1,0:T(8,128)S(1)} %get-tuple-element.48), channel_id=1, source_target_pairs={{0,8},{8,0},{16,24},{24,16},{32,40},{40,32},{48,56},{56,48},{64,72... | collective-permute-start | bytes 221192 | tf_op jit(solution)/shard_map/ppermute | solution.py:487
  51.4 15.2 %collective-permute-start.5 = (f32[6,24,128]{2,1,0:T(8,128)S(1)}, f32[6,24,128]{2,1,0:T(8,128)S(1)}, u32[]{:S(2)}, u32[]{:S(2)}) collective-permute-start(f32[6,24,128]{2,1,0:T(8,128)S(1)} %get-tuple-element.49), channel_id=1, source_target_pairs={{0,504},{8,16},{16,8},{24,32},{32,24},{40,48},{48,40},{56,64},{64,... | collective-permute-start | bytes 221192 | tf_op jit(solution)/shard_map/ppermute | solution.py:486
  67.3 22.2 %all-to-all-start.1 = ((f32[16,1,1152]{2,1,0:T(1,128)}), f32[16,1,1152]{2,1,0:T(1,128)S(1)}, u32[]{:S(2)}, u32[]{:S(2)}) async-start(f32[16,1,1152]{2,1,0:T(1,128)} %shard_map.135), calls=%async_computation.1 | async-start | bytes 147456 | tf_op jit(solution)/shard_map/all_to_all | solution.py:494
  77.8 8.1 %collective-permute-start.6 = (f32[24,128]{1,0:T(8,128)S(1)}, f32[24,128]{1,0:T(8,128)S(1)}, u32[]{:S(2)}, u32[]{:S(2)}) collective-permute-start(f32[24,128]{1,0:T(8,128)S(1)} %get-tuple-element.52), channel_id=1, source_target_pairs={{0,1},{1,0},{2,3},{3,2},{4,5},{5,4},{6,7},{7,6},{8,9},{9,8},{10,11... | collective-permute-start | bytes 36872 | tf_op jit(solution)/shard_map/ppermute | solution.py:431
  82.4 5.3 %collective-permute-start.7 = (f32[24,128]{1,0:T(8,128)S(1)}, f32[24,128]{1,0:T(8,128)S(1)}, u32[]{:S(2)}, u32[]{:S(2)}) collective-permute-start(f32[24,128]{1,0:T(8,128)S(1)} %get-tuple-element.53), channel_id=1, source_target_pairs={{0,7},{1,2},{2,1},{3,4},{4,3},{5,6},{6,5},{7,0},{8,15},{9,10},{10,... | collective-permute-start | bytes 36872 | tf_op jit(solution)/shard_map/ppermute | solution.py:431
  131.1 8.9 %collective-permute-start.9 = (f32[2176,128]{1,0:T(8,128)S(1)}, f32[2176,128]{1,0:T(8,128)S(1)}, u32[]{:S(2)}, u32[]{:S(2)}) collective-permute-start(f32[2176,128]{1,0:T(8,128)S(1)} %bitcast.3), channel_id=1, source_target_pairs={{0,1},{1,0},{2,3},{3,2},{4,5},{5,4},{6,7},{7,6},{8,9},{9,8},{10,11... | collective-permute-start | bytes 3342344 | tf_op jit(solution)/shard_map/ppermute | solution.py:505

commit v8 on v7

--- a/solution.py
+++ b/solution.py
@@ -371,6 +371,10 @@
     out_ref[...] = first_ref[...] + second_ref[...]
 
 
+def arrived_kernel(got_ref, out_ref):
+    out_ref[...] = got_ref[0, 0:8, :]
+
+
 def across_kernel(got_ref, *rest):
     out_ref, part = rest[-2:]
     count = got_ref.shape[1]
@@ -485,12 +489,13 @@
     inner, outer = pairs(GX)
     x2 = lax.ppermute(m2, GX, outer)
     x1 = lax.ppermute(m1, GX, inner)
+    (arrived,) = call(arrived_kernel, ((8, 128),), (), "v", 12)(x2)
     (half,) = call(add_kernel, (keep.shape,), (), "vva", 16)(keep, got, ylow)
     half = half.reshape(parts, count, 128)
     got = lax.all_to_all(half, across, 0, 0)
     m1, m2 = call(side_kernel, (rows, rows), (rows, rows))(x1, x2, ylow, yhigh)
     cut = (depth, 1, short * 128)
-    (part,) = call(across_kernel, (cut,), ((short * depth, 128),), "vaa", 12)(got, x2, x1)
+    (part,) = call(across_kernel, (cut,), ((short * depth, 128),), "vaa", 12)(got, arrived, x1)
     got = lax.all_to_all(part, along, 0, 0)
     y1, y2 = exchange(m1, m2, GY)
     blocks = 128 * lax.axis_size(GX) * lax.axis_size(GY)

time: 142 us -> 140 us (0.986)
  blocking collectives: 41.5 us -> 38.7 us
  waiting for transfers between devices: 11.3 us -> 13.8 us
  starting transfers between devices: 73.8 us -> 71.7 us
    all_to_all x1, blocking collectives: 20.3 us -> 18 us  [on_device(): mine = lax.all_to_all(half, across, 0, 0).reshape(HALF, 128)]
    ppermute x1, waiting for transfers between devices: 2.26 us -> 4.28 us  [on_device(): x2 = lax.ppermute(m2, GX, outer)]
where the time goes in v8:
time: 140 us; the launch traced here: 139 us
  starting transfers between devices  71.7 us (51%)
  blocking collectives  38.7 us (28%)
  waiting for transfers between devices  13.8 us (10%)
  Pallas kernels  8.36 us (6%)
  local copies, waits for them, and re-layouts  5.68 us (4%)
    ppermute x6, starting transfers between devices, exchange(): return (lax.ppermute(first, axes, inner), lax.ppermute(second, axes, outer))  32.1 us
    all_to_all x1, blocking collectives, on_device(): got = lax.all_to_all(part, along, 0, 0)  20.7 us
    all_to_all x1, blocking collectives, on_device(): mine = lax.all_to_all(half, across, 0, 0).reshape(HALF, 128)  18 us
    ppermute x1, starting transfers between devices, on_device(): x2 = lax.ppermute(m2, GX, outer)  13.6 us
    all_to_all x1, starting transfers between devices, on_device(): got = lax.all_to_all(part, along, 0, 0)  9.27 us
    ppermute x1, starting transfers between devices, on_device(): other = lax.ppermute(mine, 'core', swap)  6.56 us
    unnamed x18, local copies, waits for them, and re-layouts  5.68 us
    ppermute x6, waiting for transfers between devices, exchange(): return (lax.ppermute(first, axes, inner), lax.ppermute(second, axes, outer))  5.09 us
  transfers between devices with their start and end apart: 12, of which 6 were waited for; matrix products, arithmetic and copies ran while one was open for 0% of the time, Pallas kernels for 2%

profile of v8, /device:TPU:1, one launch (start us, length us, event | category | flops | bytes accessed | tf_op | source)
XLA Modules:
  0.0 139.1 jit_solution(7977139032369196170)
XLA Ops:
  0.6 0.0 copy-start
  0.6 0.9 copy-done
  1.5 0.8 copy-done.5
  2.3 0.8 copy-done.6
  3.1 0.0 copy-start.1
  3.1 0.0 copy-start.7
  3.1 8.9 %collective-permute-start = (f32[24,128]{1,0:T(8,128)S(1)}, f32[24,128]{1,0:T(8,128)S(1)}, u32[]{:S(2)}, u32[]{:S(2)}) collective-permute-start(f32[24,128]{1,0:T(8,128)S(1)} %get-tuple-element.35), channel_id=1, source_target_pairs={{0,1},{1,0},{2,3},{3,2},{4,5},{5,4},{6,7},{7,6},{8,9},{9,8},{10,11... | collective-permute-start | bytes 36872 | tf_op jit(solution)/shard_map/ppermute | solution.py:435
  12.1 1.9 %collective-permute-start.1 = (f32[24,128]{1,0:T(8,128)S(1)}, f32[24,128]{1,0:T(8,128)S(1)}, u32[]{:S(2)}, u32[]{:S(2)}) collective-permute-start(f32[24,128]{1,0:T(8,128)S(1)} %get-tuple-element.36), channel_id=1, source_target_pairs={{0,7},{1,2},{2,1},{3,4},{4,3},{5,6},{6,5},{7,0},{8,15},{9,10},{10,... | collective-permute-start | bytes 36872 | tf_op jit(solution)/shard_map/ppermute | solution.py:435
  14.0 0.0 collective-permute-done.r1_ref
  14.0 3.1 %collective-permute-done.1.r2_ref = f32[24,128]{1,0:T(8,128)S(1)} collective-permute-done((f32[24,128]{1,0:T(8,128)S(1)}, f32[24,128]{1,0:T(8,128)S(1)}, u32[]{:S(2)}, u32[]{:S(2)}) %collective-permute-start.1) | collective-permute-done | bytes 12320 | tf_op jit(solution)/shard_map/ppermute | solution.py:435
  17.1 11.7 %collective-permute-start.3 = (f32[6,24,128]{2,1,0:T(8,128)S(1)}, f32[6,24,128]{2,1,0:T(8,128)S(1)}, u32[]{:S(2)}, u32[]{:S(2)}) collective-permute-start(f32[6,24,128]{2,1,0:T(8,128)S(1)} %get-tuple-element.38), channel_id=1, source_target_pairs={{0,504},{8,16},{16,8},{24,32},{32,24},{40,48},{48,40},{56,64},{64,... | collective-permute-start | bytes 221192 | tf_op jit(solution)/shard_map/ppermute | solution.py:435
  28.8 1.9 %collective-permute-start.2 = (f32[6,24,128]{2,1,0:T(8,128)S(1)}, f32[6,24,128]{2,1,0:T(8,128)S(1)}, u32[]{:S(2)}, u32[]{:S(2)}) collective-permute-start(f32[6,24,128]{2,1,0:T(8,128)S(1)} %get-tuple-element.37.after), channel_id=1, source_target_pairs={{0,8},{8,0},{16,24},{24,16},{32,40},{40,32},{48,56},{56,48},{64,72... | collective-permute-start | bytes 221192 | tf_op jit(solution)/shard_map/ppermute | solution.py:435
  30.8 0.0 copy-start.2
  30.8 1.1 copy-done.2
  31.9 1.1 copy-done.3
  33.0 1.0 copy-done.4
  34.0 0.5 shard_map.129
  34.5 0.0 copy-start.8
  34.5 0.0 collective-permute-done.3.x2_ref
  34.5 0.0 collective-permute-done.2.x1_ref
  34.5 0.0 copy-done.1
  34.5 0.0 copy-done.7
  34.5 1.9 %shard_map.130 = (f32[2176,128]{1,0:T(8,128)S(1)}, f32[2176,128]{1,0:T(8,128)S(1)}, f32[36,24,128]{2,1,0:T(8,128)S(1)}, bf16[128,512]{1,0:T(8,128)(2,1)S(1)}, bf16[128,512]{1,0:T(8,128)(2,1)S(1)}) custom-call(f32[3,4,16,128]{3,2,1,0:T(8,128)S(1)} %copy-done.1, f32[3,4,16,128]{3,2,1,0:T(8,128)S(1)} %get-tuple-element.34.direct_ref, ...), custom_call_target="tpu_custom_call" | custom-call | tf_op jit(solution)/shard_map/pallas_call | solution.py:463
  36.5 4.6 %collective-permute-start.8 = (f32[2176,128]{1,0:T(8,128)S(1)}, f32[2176,128]{1,0:T(8,128)S(1)}, u32[]{:S(2)}, u32[]{:S(2)}) collective-permute-start(f32[2176,128]{1,0:T(8,128)S(1)} %get-tuple-element.57), channel_id=1, source_target_pairs={{0,1},{1,0},{2,3},{3,2},{4,5},{5,4},{6,7},{7,6},{8,9},{9,8},{10,11... | collective-permute-start | bytes 3342344 | tf_op jit(solution)/shard_map/ppermute | solution.py:473
  41.0 1.6 %shard_map.131 = (f32[3,4,16,128]{3,2,1,0:T(8,128)S(1)}, f32[3,4,16,128]{3,2,1,0:T(8,128)S(1)}, f32[6,24,128]{2,1,0:T(8,128)S(1)}, f32[6,24,128]{2,1,0:T(8,128)S...) custom-call(f32[3,4,16,128]{3,2,1,0:T(8,128)S(1)} %get-tuple-element.34.direct_ref, ...), custom_call_target="tpu_custom_call" | custom-call | tf_op jit(solution)/shard_map/pallas_call | solution.py:474
  42.6 0.8 collective-permute-done.8.second_ref
  43.4 1.1 shard_map.134
  44.5 3.7 %all-to-all-start = ((f32[16,136,128]{2,1,0:T(8,128)}), f32[16,136,128]{2,1,0:T(8,128)S(1)}, u32[]{:S(2)}, u32[]{:S(2)}) async-start(f32[16,136,128]{2,1,0:T(8,128)} %bitcast.1), calls=%async_computation | async-start | bytes 2228224 | tf_op jit(solution)/shard_map/all_to_all | solution.py:495
  48.2 13.6 %collective-permute-start.5 = (f32[6,24,128]{2,1,0:T(8,128)S(1)}, f32[6,24,128]{2,1,0:T(8,128)S(1)}, u32[]{:S(2)}, u32[]{:S(2)}) collective-permute-start(f32[6,24,128]{2,1,0:T(8,128)S(1)} %get-tuple-element.49), channel_id=1, source_target_pairs={{0,504},{8,16},{16,8},{24,32},{32,24},{40,48},{48,40},{56,64},{64,... | collective-permute-start | bytes 221192 | tf_op jit(solution)/shard_map/ppermute | solution.py:490
  61.8 1.9 %collective-permute-start.4 = (f32[6,24,128]{2,1,0:T(8,128)S(1)}, f32[6,24,128]{2,1,0:T(8,128)S(1)}, u32[]{:S(2)}, u32[]{:S(2)}) collective-permute-start(f32[6,24,128]{2,1,0:T(8,128)S(1)} %get-tuple-element.48), channel_id=1, source_target_pairs={{0,8},{8,0},{16,24},{24,16},{32,40},{40,32},{48,56},{56,48},{64,72... | collective-permute-start | bytes 221192 | tf_op jit(solution)/shard_map/ppermute | solution.py:491
  63.7 4.3 %collective-permute-done.5.x2_ref.got_ref = f32[6,24,128]{2,1,0:T(8,128)S(1)} collective-permute-done((f32[6,24,128]{2,1,0:T(8,128)S(1)}, f32[6,24,128]{2,1,0:T(8,128)S(1)}, u32[]{:S(2)}, u32[]{:S(2)}) %collective-permute-start.5) | collective-permute-done | bytes 73760 | tf_op jit(solution)/shard_map/ppermute | solution.py:490
  68.0 0.0 collective-permute-done.4.x1_ref.rest_1_
  68.0 0.0 all-to-all-done.got_ref
  68.0 0.7 shard_map.136
  68.7 9.3 %all-to-all-start.1 = ((f32[16,1,1152]{2,1,0:T(1,128)}), f32[16,1,1152]{2,1,0:T(1,128)S(1)}, u32[]{:S(2)}, u32[]{:S(2)}) async-start(f32[16,1,1152]{2,1,0:T(1,128)} %shard_map.136), calls=%async_computation.1 | async-start | bytes 147456 | tf_op jit(solution)/shard_map/all_to_all | solution.py:499
  78.0 4.2 %collective-permute-start.6 = (f32[24,128]{1,0:T(8,128)S(1)}, f32[24,128]{1,0:T(8,128)S(1)}, u32[]{:S(2)}, u32[]{:S(2)}) collective-permute-start(f32[24,128]{1,0:T(8,128)S(1)} %get-tuple-element.52), channel_id=1, source_target_pairs={{0,1},{1,0},{2,3},{3,2},{4,5},{5,4},{6,7},{7,6},{8,9},{9,8},{10,11... | collective-permute-start | bytes 36872 | tf_op jit(solution)/shard_map/ppermute | solution.py:435
  82.2 3.4 %collective-permute-start.7 = (f32[24,128]{1,0:T(8,128)S(1)}, f32[24,128]{1,0:T(8,128)S(1)}, u32[]{:S(2)}, u32[]{:S(2)}) collective-permute-start(f32[24,128]{1,0:T(8,128)S(1)} %get-tuple-element.53), channel_id=1, source_target_pairs={{0,7},{1,2},{2,1},{3,4},{4,3},{5,6},{6,5},{7,0},{8,15},{9,10},{10,... | collective-permute-start | bytes 36872 | tf_op jit(solution)/shard_map/ppermute | solution.py:435
  85.7 0.0 collective-permute-done.6.y1_ref.rest_0_
  85.7 2.0 %collective-permute-done.7.y2_ref.rest_1_ = f32[24,128]{1,0:T(8,128)S(1)} collective-permute-done((f32[24,128]{1,0:T(8,128)S(1)}, f32[24,128]{1,0:T(8,128)S(1)}, u32[]{:S(2)}, u32[]{:S(2)}) %collective-permute-start.7) | collective-permute-done | bytes 12320 | tf_op jit(solution)/shard_map/ppermute | solution.py:435
  87.7 2.1 %all-to-all-done.1.got_ref = f32[16,1,1152]{2,1,0:T(1,128)S(1)} async-done(((f32[16,1,1152]{2,1,0:T(1,128)}), f32[16,1,1152]{2,1,0:T(1,128)S(1)}, u32[]{:S(2)}, u32[]{:S(2)}) %all-to-all-start.1) | async-done | bytes 73760 | tf_op jit(solution)/shard_map/all_to_all | solution.py:499
  89.8 0.1 shard_map.137
  89.9 20.7 %all_to_all.20.got_ref = f32[16,1,1152]{2,1,0:T(1,128)S(1)} all-to-all(f32[16,1,1152]{2,1,0:T(1,128)S(1)} %shard_map.137), channel_id=1, replica_groups=mesh['zh'=4,'x'=4,'y'=4,'zl'=4,'core'=2] {'zh','zl'}, dimensions={0} | all-to-all | bytes 147456 | tf_op jit(solution)/shard_map/all_to_all | solution.py:504
  110.5 0.1 shard_map.138
  110.6 18.0 %all_to_all.21 = f32[16,136,128]{2,1,0:T(8,128)S(1)} all-to-all(f32[16,136,128]{2,1,0:T(8,128)S(1)} %shard_map.138), channel_id=1, replica_groups=mesh['zh'=4,'x'=4,'y'=4,'zl'=4,'core'=2] {'x','y'}, dimensions={0} | all-to-all | bytes 2228224 | tf_op jit(solution)/shard_map/all_to_all | solution.py:506
  128.6 6.6 %collective-permute-start.9 = (f32[2176,128]{1,0:T(8,128)S(1)}, f32[2176,128]{1,0:T(8,128)S(1)}, u32[]{:S(2)}, u32[]{:S(2)}) collective-permute-start(f32[2176,128]{1,0:T(8,128)S(1)} %bitcast.3), channel_id=1, source_target_pairs={{0,1},{1,0},{2,3},{3,2},{4,5},{5,4},{6,7},{7,6},{8,9},{9,8},{10,11... | collective-permute-start | bytes 3342344 | tf_op jit(solution)/shard_map/ppermute | solution.py:510
  135.2 0.8 shard_map.133
  136.0 1.6 %collective-permute-done.9.other_ref = f32[2176,128]{1,0:T(8,128)S(1)} collective-permute-done((f32[2176,128]{1,0:T(8,128)S(1)}, f32[2176,128]{1,0:T(8,128)S(1)}, u32[]{:S(2)}, u32[]{:S(2)}) %collective-permute-start.9) | collective-permute-done | bytes 1114144 | tf_op jit(solution)/shard_map/ppermute | solution.py:510
  137.6 1.6 %shard_map.139 = (f32[648,512]{1,0:T(8,128)}, f32[512]{0:T(512)}, f32[512,384]{1,0:T(8,128)}, f32[384]{0:T(512)}) custom-call(f32[2176,128]{1,0:T(8,128)S(1)} %bitcast.4, f32[2176,128]{1,0:T(8,128)S(1)} %collective-permute-done.9.other_ref), custom_call_target="tpu_custom_call" | custom-call | tf_op jit(solution)/shard_map/pallas_call | solution.py:511
  (10 shorter events, 0.1 us)
Async XLA Ops:
  0.6 0.9 copy-start
  1.5 0.8 copy-start.5
  2.3 0.8 copy-start.6
  3.1 31.4 %copy-start.1 = (f32[3,4,16,128]{3,2,1,0:T(8,128)S(1)}, f32[3,4,16,128]{3,2,1,0:T(8,128)}, u32[]{:S(2)}) copy-start(f32[3,4,16,128]{3,2,1,0:T(8,128)} %v_ref.5) | copy-start | bytes 294916
  3.1 31.4 %copy-start.7 = (f32[512]{0:T(512)S(1)}, f32[512]{0:T(512)}, u32[]{:S(2)}) copy-start(f32[512]{0:T(512)} %param.11) | copy-start | bytes 6148
  3.1 10.9 %collective-permute-start = (f32[24,128]{1,0:T(8,128)S(1)}, f32[24,128]{1,0:T(8,128)S(1)}, u32[]{:S(2)}, u32[]{:S(2)}) collective-permute-start(f32[24,128]{1,0:T(8,128)S(1)} %get-tuple-element.35), channel_id=1, source_target_pairs={{0,1},{1,0},{2,3},{3,2},{4,5},{5,4},{6,7},{7,6},{8,9},{9,8},{10,11... | collective-permute-start | bytes 36872 | tf_op jit(solution)/shard_map/ppermute | solution.py:435
  12.1 5.0 %collective-permute-start.1 = (f32[24,128]{1,0:T(8,128)S(1)}, f32[24,128]{1,0:T(8,128)S(1)}, u32[]{:S(2)}, u32[]{:S(2)}) collective-permute-start(f32[24,128]{1,0:T(8,128)S(1)} %get-tuple-element.36), channel_id=1, source_target_pairs={{0,7},{1,2},{2,1},{3,4},{4,3},{5,6},{6,5},{7,0},{8,15},{9,10},{10,... | collective-permute-start | bytes 36872 | tf_op jit(solution)/shard_map/ppermute | solution.py:435
  17.1 17.4 %collective-permute-start.3 = (f32[6,24,128]{2,1,0:T(8,128)S(1)}, f32[6,24,128]{2,1,0:T(8,128)S(1)}, u32[]{:S(2)}, u32[]{:S(2)}) collective-permute-start(f32[6,24,128]{2,1,0:T(8,128)S(1)} %get-tuple-element.38), channel_id=1, source_target_pairs={{0,504},{8,16},{16,8},{24,32},{32,24},{40,48},{48,40},{56,64},{64,... | collective-permute-start | bytes 221192 | tf_op jit(solution)/shard_map/ppermute | solution.py:435
  28.8 5.7 %collective-permute-start.2 = (f32[6,24,128]{2,1,0:T(8,128)S(1)}, f32[6,24,128]{2,1,0:T(8,128)S(1)}, u32[]{:S(2)}, u32[]{:S(2)}) collective-permute-start(f32[6,24,128]{2,1,0:T(8,128)S(1)} %get-tuple-element.37.after), channel_id=1, source_target_pairs={{0,8},{8,0},{16,24},{24,16},{32,40},{40,32},{48,56},{56,48},{64,72... | collective-permute-start | bytes 221192 | tf_op jit(solution)/shard_map/ppermute | solution.py:435
  30.8 1.1 copy-start.2
  31.9 1.1 copy-start.3
  33.0 1.0 copy-start.4
  34.5 6.5 %copy-start.8 = (f32[384]{0:T(512)S(1)}, f32[384]{0:T(512)}, u32[]{:S(2)}) copy-start(f32[384]{0:T(512)} %param.13) | copy-start | bytes 4612
  36.5 6.9 %collective-permute-start.8 = (f32[2176,128]{1,0:T(8,128)S(1)}, f32[2176,128]{1,0:T(8,128)S(1)}, u32[]{:S(2)}, u32[]{:S(2)}) collective-permute-start(f32[2176,128]{1,0:T(8,128)S(1)} %get-tuple-element.57), channel_id=1, source_target_pairs={{0,1},{1,0},{2,3},{3,2},{4,5},{5,4},{6,7},{7,6},{8,9},{9,8},{10,11... | collective-permute-start | bytes 3342344 | tf_op jit(solution)/shard_map/ppermute | solution.py:473
  44.5 23.5 %all-to-all-start = ((f32[16,136,128]{2,1,0:T(8,128)}), f32[16,136,128]{2,1,0:T(8,128)S(1)}, u32[]{:S(2)}, u32[]{:S(2)}) async-start(f32[16,136,128]{2,1,0:T(8,128)} %bitcast.1), calls=%async_computation | async-start | bytes 2228224 | tf_op jit(solution)/shard_map/all_to_all | solution.py:495
  48.2 19.8 %collective-permute-start.5 = (f32[6,24,128]{2,1,0:T(8,128)S(1)}, f32[6,24,128]{2,1,0:T(8,128)S(1)}, u32[]{:S(2)}, u32[]{:S(2)}) collective-permute-start(f32[6,24,128]{2,1,0:T(8,128)S(1)} %get-tuple-element.49), channel_id=1, source_target_pairs={{0,504},{8,16},{16,8},{24,32},{32,24},{40,48},{48,40},{56,64},{64,... | collective-permute-start | bytes 221192 | tf_op jit(solution)/shard_map/ppermute | solution.py:490
  61.8 6.2 %collective-permute-start.4 = (f32[6,24,128]{2,1,0:T(8,128)S(1)}, f32[6,24,128]{2,1,0:T(8,128)S(1)}, u32[]{:S(2)}, u32[]{:S(2)}) collective-permute-start(f32[6,24,128]{2,1,0:T(8,128)S(1)} %get-tuple-element.48), channel_id=1, source_target_pairs={{0,8},{8,0},{16,24},{24,16},{32,40},{40,32},{48,56},{56,48},{64,72... | collective-permute-start | bytes 221192 | tf_op jit(solution)/shard_map/ppermute | solution.py:491
  68.7 21.1 %all-to-all-start.1 = ((f32[16,1,1152]{2,1,0:T(1,128)}), f32[16,1,1152]{2,1,0:T(1,128)S(1)}, u32[]{:S(2)}, u32[]{:S(2)}) async-start(f32[16,1,1152]{2,1,0:T(1,128)} %shard_map.136), calls=%async_computation.1 | async-start | bytes 147456 | tf_op jit(solution)/shard_map/all_to_all | solution.py:499
  78.0 7.6 %collective-permute-start.6 = (f32[24,128]{1,0:T(8,128)S(1)}, f32[24,128]{1,0:T(8,128)S(1)}, u32[]{:S(2)}, u32[]{:S(2)}) collective-permute-start(f32[24,128]{1,0:T(8,128)S(1)} %get-tuple-element.52), channel_id=1, source_target_pairs={{0,1},{1,0},{2,3},{3,2},{4,5},{5,4},{6,7},{7,6},{8,9},{9,8},{10,11... | collective-permute-start | bytes 36872 | tf_op jit(solution)/shard_map/ppermute | solution.py:435
  82.2 5.5 %collective-permute-start.7 = (f32[24,128]{1,0:T(8,128)S(1)}, f32[24,128]{1,0:T(8,128)S(1)}, u32[]{:S(2)}, u32[]{:S(2)}) collective-permute-start(f32[24,128]{1,0:T(8,128)S(1)} %get-tuple-element.53), channel_id=1, source_target_pairs={{0,7},{1,2},{2,1},{3,4},{4,3},{5,6},{6,5},{7,0},{8,15},{9,10},{10,... | collective-permute-start | bytes 36872 | tf_op jit(solution)/shard_map/ppermute | solution.py:435
  128.6 8.9 %collective-permute-start.9 = (f32[2176,128]{1,0:T(8,128)S(1)}, f32[2176,128]{1,0:T(8,128)S(1)}, u32[]{:S(2)}, u32[]{:S(2)}) collective-permute-start(f32[2176,128]{1,0:T(8,128)S(1)} %bitcast.3), channel_id=1, source_target_pairs={{0,1},{1,0},{2,3},{3,2},{4,5},{5,4},{6,7},{7,6},{8,9},{9,8},{10,11... | collective-permute-start | bytes 3342344 | tf_op jit(solution)/shard_map/ppermute | solution.py:510

commit v9 on v8

--- a/solution.py
+++ b/solution.py
@@ -372,7 +372,7 @@
 
 
 def arrived_kernel(got_ref, out_ref):
-    out_ref[...] = got_ref[0, 0:8, :]
+    out_ref[...] = got_ref[0:8] if len(got_ref.shape) == 2 else got_ref[0, 0:8, :]
 
 
 def across_kernel(got_ref, *rest):
@@ -498,9 +498,10 @@
     (part,) = call(across_kernel, (cut,), ((short * depth, 128),), "vaa", 12)(got, arrived, x1)
     got = lax.all_to_all(part, along, 0, 0)
     y1, y2 = exchange(m1, m2, GY)
+    (arrived,) = call(arrived_kernel, ((8, 128),), (), "v", 12)(y2)
     blocks = 128 * lax.axis_size(GX) * lax.axis_size(GY)
     scaled = functools.partial(along_kernel, float(blocks) ** -0.5)
-    (part,) = call(scaled, (cut,), (), "vaa", 12)(got, y1, y2)
+    (part,) = call(scaled, (cut,), (), "vaa", 12)(got, arrived, y1)
     got = lax.all_to_all(part, along, 0, 0)
     (half,) = call(spread_kernel, (half.shape,), ((short * depth, 128),), "v", 12)(got)
     mine = lax.all_to_all(half, across, 0, 0).reshape(HALF, 128)

time: 140 us -> 138 us (0.986)
  blocking collectives: 38.7 us -> 37 us
    all_to_all x1, blocking collectives: 20.7 us -> 18.9 us  [on_device(): got = lax.all_to_all(part, along, 0, 0)]
where the time goes in v9:
time: 138 us; the launch traced here: 137 us
  starting transfers between devices  71.6 us (52%)
  blocking collectives  37 us (27%)
  waiting for transfers between devices  13.8 us (10%)
  Pallas kernels  8.37 us (6%)
  local copies, waits for them, and re-layouts  5.68 us (4%)
    ppermute x6, starting transfers between devices, exchange(): return (lax.ppermute(first, axes, inner), lax.ppermute(second, axes, outer))  32.1 us
    all_to_all x1, blocking collectives, on_device(): got = lax.all_to_all(part, along, 0, 0)  18.9 us
    all_to_all x1, blocking collectives, on_device(): mine = lax.all_to_all(half, across, 0, 0).reshape(HALF, 128)  18.1 us
    ppermute x1, starting transfers between devices, on_device(): x2 = lax.ppermute(m2, GX, outer)  13.6 us
    all_to_all x1, starting transfers between devices, on_device(): got = lax.all_to_all(part, along, 0, 0)  9.27 us
    ppermute x1, starting transfers between devices, on_device(): other = lax.ppermute(mine, 'core', swap)  6.46 us
    unnamed x18, local copies, waits for them, and re-layouts  5.68 us
    ppermute x1, starting transfers between devices, on_device(): got = lax.ppermute(send, 'core', swap)  4.56 us
  transfers between devices with their start and end apart: 12, of which 6 were waited for; matrix products, arithmetic and copies ran while one was open for 0% of the time, Pallas kernels for 2%

profile of v9, /device:TPU:1, one launch (start us, length us, event | category | flops | bytes accessed | tf_op | source)
XLA Modules:
  0.0 137.3 jit_solution(5954066991032166101)
XLA Ops:
  0.6 0.0 copy-start
  0.6 0.9 copy-done
  1.5 0.8 copy-done.5
  2.3 0.8 copy-done.6
  3.1 0.0 copy-start.1
  3.1 0.0 copy-start.7
  3.1 8.9 %collective-permute-start = (f32[24,128]{1,0:T(8,128)S(1)}, f32[24,128]{1,0:T(8,128)S(1)}, u32[]{:S(2)}, u32[]{:S(2)}) collective-permute-start(f32[24,128]{1,0:T(8,128)S(1)} %get-tuple-element.35), channel_id=1, source_target_pairs={{0,1},{1,0},{2,3},{3,2},{4,5},{5,4},{6,7},{7,6},{8,9},{9,8},{10,11... | collective-permute-start | bytes 36872 | tf_op jit(solution)/shard_map/ppermute | solution.py:435
  12.1 1.9 %collective-permute-start.1 = (f32[24,128]{1,0:T(8,128)S(1)}, f32[24,128]{1,0:T(8,128)S(1)}, u32[]{:S(2)}, u32[]{:S(2)}) collective-permute-start(f32[24,128]{1,0:T(8,128)S(1)} %get-tuple-element.36), channel_id=1, source_target_pairs={{0,7},{1,2},{2,1},{3,4},{4,3},{5,6},{6,5},{7,0},{8,15},{9,10},{10,... | collective-permute-start | bytes 36872 | tf_op jit(solution)/shard_map/ppermute | solution.py:435
  14.0 0.0 collective-permute-done.r1_ref
  14.0 3.1 %collective-permute-done.1.r2_ref = f32[24,128]{1,0:T(8,128)S(1)} collective-permute-done((f32[24,128]{1,0:T(8,128)S(1)}, f32[24,128]{1,0:T(8,128)S(1)}, u32[]{:S(2)}, u32[]{:S(2)}) %collective-permute-start.1) | collective-permute-done | bytes 12320 | tf_op jit(solution)/shard_map/ppermute | solution.py:435
  17.1 11.7 %collective-permute-start.3 = (f32[6,24,128]{2,1,0:T(8,128)S(1)}, f32[6,24,128]{2,1,0:T(8,128)S(1)}, u32[]{:S(2)}, u32[]{:S(2)}) collective-permute-start(f32[6,24,128]{2,1,0:T(8,128)S(1)} %get-tuple-element.38), channel_id=1, source_target_pairs={{0,504},{8,16},{16,8},{24,32},{32,24},{40,48},{48,40},{56,64},{64,... | collective-permute-start | bytes 221192 | tf_op jit(solution)/shard_map/ppermute | solution.py:435
  28.8 1.9 %collective-permute-start.2 = (f32[6,24,128]{2,1,0:T(8,128)S(1)}, f32[6,24,128]{2,1,0:T(8,128)S(1)}, u32[]{:S(2)}, u32[]{:S(2)}) collective-permute-start(f32[6,24,128]{2,1,0:T(8,128)S(1)} %get-tuple-element.37.after), channel_id=1, source_target_pairs={{0,8},{8,0},{16,24},{24,16},{32,40},{40,32},{48,56},{56,48},{64,72... | collective-permute-start | bytes 221192 | tf_op jit(solution)/shard_map/ppermute | solution.py:435
  30.8 0.0 copy-start.2
  30.8 1.1 copy-done.2
  31.9 1.1 copy-done.3
  33.0 1.0 copy-done.4
  34.0 0.5 shard_map.129
  34.5 0.0 copy-start.8
  34.5 0.0 collective-permute-done.3.x2_ref
  34.5 0.0 collective-permute-done.2.x1_ref
  34.5 0.0 copy-done.1
  34.5 0.0 copy-done.7
  34.5 1.9 %shard_map.130 = (f32[2176,128]{1,0:T(8,128)S(1)}, f32[2176,128]{1,0:T(8,128)S(1)}, f32[36,24,128]{2,1,0:T(8,128)S(1)}, bf16[128,512]{1,0:T(8,128)(2,1)S(1)}, bf16[128,512]{1,0:T(8,128)(2,1)S(1)}) custom-call(f32[3,4,16,128]{3,2,1,0:T(8,128)S(1)} %copy-done.1, f32[3,4,16,128]{3,2,1,0:T(8,128)S(1)} %get-tuple-element.34.direct_ref, ...), custom_call_target="tpu_custom_call" | custom-call | tf_op jit(solution)/shard_map/pallas_call | solution.py:463
  36.5 4.6 %collective-permute-start.8 = (f32[2176,128]{1,0:T(8,128)S(1)}, f32[2176,128]{1,0:T(8,128)S(1)}, u32[]{:S(2)}, u32[]{:S(2)}) collective-permute-start(f32[2176,128]{1,0:T(8,128)S(1)} %get-tuple-element.57), channel_id=1, source_target_pairs={{0,1},{1,0},{2,3},{3,2},{4,5},{5,4},{6,7},{7,6},{8,9},{9,8},{10,11... | collective-permute-start | bytes 3342344 | tf_op jit(solution)/shard_map/ppermute | solution.py:473
  41.0 1.6 %shard_map.131 = (f32[3,4,16,128]{3,2,1,0:T(8,128)S(1)}, f32[3,4,16,128]{3,2,1,0:T(8,128)S(1)}, f32[6,24,128]{2,1,0:T(8,128)S(1)}, f32[6,24,128]{2,1,0:T(8,128)S...) custom-call(f32[3,4,16,128]{3,2,1,0:T(8,128)S(1)} %get-tuple-element.34.direct_ref, ...), custom_call_target="tpu_custom_call" | custom-call | tf_op jit(solution)/shard_map/pallas_call | solution.py:474
  42.6 0.8 collective-permute-done.8.second_ref
  43.4 1.1 shard_map.134
  44.5 3.7 %all-to-all-start = ((f32[16,136,128]{2,1,0:T(8,128)}), f32[16,136,128]{2,1,0:T(8,128)S(1)}, u32[]{:S(2)}, u32[]{:S(2)}) async-start(f32[16,136,128]{2,1,0:T(8,128)} %bitcast.1), calls=%async_computation | async-start | bytes 2228224 | tf_op jit(solution)/shard_map/all_to_all | solution.py:495
  48.2 13.6 %collective-permute-start.5 = (f32[6,24,128]{2,1,0:T(8,128)S(1)}, f32[6,24,128]{2,1,0:T(8,128)S(1)}, u32[]{:S(2)}, u32[]{:S(2)}) collective-permute-start(f32[6,24,128]{2,1,0:T(8,128)S(1)} %get-tuple-element.49), channel_id=1, source_target_pairs={{0,504},{8,16},{16,8},{24,32},{32,24},{40,48},{48,40},{56,64},{64,... | collective-permute-start | bytes 221192 | tf_op jit(solution)/shard_map/ppermute | solution.py:490
  61.8 1.9 %collective-permute-start.4 = (f32[6,24,128]{2,1,0:T(8,128)S(1)}, f32[6,24,128]{2,1,0:T(8,128)S(1)}, u32[]{:S(2)}, u32[]{:S(2)}) collective-permute-start(f32[6,24,128]{2,1,0:T(8,128)S(1)} %get-tuple-element.48), channel_id=1, source_target_pairs={{0,8},{8,0},{16,24},{24,16},{32,40},{40,32},{48,56},{56,48},{64,72... | collective-permute-start | bytes 221192 | tf_op jit(solution)/shard_map/ppermute | solution.py:491
  63.7 4.3 %collective-permute-done.5.x2_ref.got_ref = f32[6,24,128]{2,1,0:T(8,128)S(1)} collective-permute-done((f32[6,24,128]{2,1,0:T(8,128)S(1)}, f32[6,24,128]{2,1,0:T(8,128)S(1)}, u32[]{:S(2)}, u32[]{:S(2)}) %collective-permute-start.5) | collective-permute-done | bytes 73760 | tf_op jit(solution)/shard_map/ppermute | solution.py:490
  68.0 0.0 collective-permute-done.4.x1_ref.rest_1_
  68.0 0.0 all-to-all-done.got_ref
  68.0 0.7 shard_map.136
  68.7 9.3 %all-to-all-start.1 = ((f32[16,1,1152]{2,1,0:T(1,128)}), f32[16,1,1152]{2,1,0:T(1,128)S(1)}, u32[]{:S(2)}, u32[]{:S(2)}) async-start(f32[16,1,1152]{2,1,0:T(1,128)} %shard_map.136), calls=%async_computation.1 | async-start | bytes 147456 | tf_op jit(solution)/shard_map/all_to_all | solution.py:499
  78.0 5.7 %collective-permute-start.7 = (f32[24,128]{1,0:T(8,128)S(1)}, f32[24,128]{1,0:T(8,128)S(1)}, u32[]{:S(2)}, u32[]{:S(2)}) collective-permute-start(f32[24,128]{1,0:T(8,128)S(1)} %get-tuple-element.53), channel_id=1, source_target_pairs={{0,7},{1,2},{2,1},{3,4},{4,3},{5,6},{6,5},{7,0},{8,15},{9,10},{10,... | collective-permute-start | bytes 36872 | tf_op jit(solution)/shard_map/ppermute | solution.py:435
  83.8 1.9 %collective-permute-start.6 = (f32[24,128]{1,0:T(8,128)S(1)}, f32[24,128]{1,0:T(8,128)S(1)}, u32[]{:S(2)}, u32[]{:S(2)}) collective-permute-start(f32[24,128]{1,0:T(8,128)S(1)} %get-tuple-element.52), channel_id=1, source_target_pairs={{0,1},{1,0},{2,3},{3,2},{4,5},{5,4},{6,7},{7,6},{8,9},{9,8},{10,11... | collective-permute-start | bytes 36872 | tf_op jit(solution)/shard_map/ppermute | solution.py:435
  85.7 0.0 collective-permute-done.7.y2_ref.got_ref
  85.7 1.1 collective-permute-done.6.y1_ref.rest_1_
  86.8 3.0 %all-to-all-done.1.got_ref = f32[16,1,1152]{2,1,0:T(1,128)S(1)} async-done(((f32[16,1,1152]{2,1,0:T(1,128)}), f32[16,1,1152]{2,1,0:T(1,128)S(1)}, u32[]{:S(2)}, u32[]{:S(2)}) %all-to-all-start.1) | async-done | bytes 73760 | tf_op jit(solution)/shard_map/all_to_all | solution.py:499
  89.8 0.1 shard_map.138
  89.9 18.9 %all_to_all.20.got_ref = f32[16,1,1152]{2,1,0:T(1,128)S(1)} all-to-all(f32[16,1,1152]{2,1,0:T(1,128)S(1)} %shard_map.138), channel_id=1, replica_groups=mesh['zh'=4,'x'=4,'y'=4,'zl'=4,'core'=2] {'zh','zl'}, dimensions={0} | all-to-all | bytes 147456 | tf_op jit(solution)/shard_map/all_to_all | solution.py:505
  108.8 0.1 shard_map.139
  108.9 18.1 %all_to_all.21 = f32[16,136,128]{2,1,0:T(8,128)S(1)} all-to-all(f32[16,136,128]{2,1,0:T(8,128)S(1)} %shard_map.139), channel_id=1, replica_groups=mesh['zh'=4,'x'=4,'y'=4,'zl'=4,'core'=2] {'x','y'}, dimensions={0} | all-to-all | bytes 2228224 | tf_op jit(solution)/shard_map/all_to_all | solution.py:507
  127.0 6.5 %collective-permute-start.9 = (f32[2176,128]{1,0:T(8,128)S(1)}, f32[2176,128]{1,0:T(8,128)S(1)}, u32[]{:S(2)}, u32[]{:S(2)}) collective-permute-start(f32[2176,128]{1,0:T(8,128)S(1)} %bitcast.3), channel_id=1, source_target_pairs={{0,1},{1,0},{2,3},{3,2},{4,5},{5,4},{6,7},{7,6},{8,9},{9,8},{10,11... | collective-permute-start | bytes 3342344 | tf_op jit(solution)/shard_map/ppermute | solution.py:511
  133.4 0.8 shard_map.133
  134.2 1.6 %collective-permute-done.9.other_ref = f32[2176,128]{1,0:T(8,128)S(1)} collective-permute-done((f32[2176,128]{1,0:T(8,128)S(1)}, f32[2176,128]{1,0:T(8,128)S(1)}, u32[]{:S(2)}, u32[]{:S(2)}) %collective-permute-start.9) | collective-permute-done | bytes 1114144 | tf_op jit(solution)/shard_map/ppermute | solution.py:511
  135.8 1.6 %shard_map.140 = (f32[648,512]{1,0:T(8,128)}, f32[512]{0:T(512)}, f32[512,384]{1,0:T(8,128)}, f32[384]{0:T(512)}) custom-call(f32[2176,128]{1,0:T(8,128)S(1)} %bitcast.4, f32[2176,128]{1,0:T(8,128)S(1)} %collective-permute-done.9.other_ref), custom_call_target="tpu_custom_call" | custom-call | tf_op jit(solution)/shard_map/pallas_call | solution.py:512
  (11 shorter events, 0.1 us)
Async XLA Ops:
  0.6 0.9 copy-start
  1.5 0.8 copy-start.5
  2.3 0.8 copy-start.6
  3.1 31.4 %copy-start.1 = (f32[3,4,16,128]{3,2,1,0:T(8,128)S(1)}, f32[3,4,16,128]{3,2,1,0:T(8,128)}, u32[]{:S(2)}) copy-start(f32[3,4,16,128]{3,2,1,0:T(8,128)} %v_ref.5) | copy-start | bytes 294916
  3.1 31.4 %copy-start.7 = (f32[512]{0:T(512)S(1)}, f32[512]{0:T(512)}, u32[]{:S(2)}) copy-start(f32[512]{0:T(512)} %param.11) | copy-start | bytes 6148
  3.1 10.9 %collective-permute-start = (f32[24,128]{1,0:T(8,128)S(1)}, f32[24,128]{1,0:T(8,128)S(1)}, u32[]{:S(2)}, u32[]{:S(2)}) collective-permute-start(f32[24,128]{1,0:T(8,128)S(1)} %get-tuple-element.35), channel_id=1, source_target_pairs={{0,1},{1,0},{2,3},{3,2},{4,5},{5,4},{6,7},{7,6},{8,9},{9,8},{10,11... | collective-permute-start | bytes 36872 | tf_op jit(solution)/shard_map/ppermute | solution.py:435
  12.1 5.0 %collective-permute-start.1 = (f32[24,128]{1,0:T(8,128)S(1)}, f32[24,128]{1,0:T(8,128)S(1)}, u32[]{:S(2)}, u32[]{:S(2)}) collective-permute-start(f32[24,128]{1,0:T(8,128)S(1)} %get-tuple-element.36), channel_id=1, source_target_pairs={{0,7},{1,2},{2,1},{3,4},{4,3},{5,6},{6,5},{7,0},{8,15},{9,10},{10,... | collective-permute-start | bytes 36872 | tf_op jit(solution)/shard_map/ppermute | solution.py:435
  17.1 17.4 %collective-permute-start.3 = (f32[6,24,128]{2,1,0:T(8,128)S(1)}, f32[6,24,128]{2,1,0:T(8,128)S(1)}, u32[]{:S(2)}, u32[]{:S(2)}) collective-permute-start(f32[6,24,128]{2,1,0:T(8,128)S(1)} %get-tuple-element.38), channel_id=1, source_target_pairs={{0,504},{8,16},{16,8},{24,32},{32,24},{40,48},{48,40},{56,64},{64,... | collective-permute-start | bytes 221192 | tf_op jit(solution)/shard_map/ppermute | solution.py:435
  28.8 5.7 %collective-permute-start.2 = (f32[6,24,128]{2,1,0:T(8,128)S(1)}, f32[6,24,128]{2,1,0:T(8,128)S(1)}, u32[]{:S(2)}, u32[]{:S(2)}) collective-permute-start(f32[6,24,128]{2,1,0:T(8,128)S(1)} %get-tuple-element.37.after), channel_id=1, source_target_pairs={{0,8},{8,0},{16,24},{24,16},{32,40},{40,32},{48,56},{56,48},{64,72... | collective-permute-start | bytes 221192 | tf_op jit(solution)/shard_map/ppermute | solution.py:435
  30.8 1.1 copy-start.2
  31.9 1.1 copy-start.3
  33.0 1.0 copy-start.4
  34.5 6.5 %copy-start.8 = (f32[384]{0:T(512)S(1)}, f32[384]{0:T(512)}, u32[]{:S(2)}) copy-start(f32[384]{0:T(512)} %param.13) | copy-start | bytes 4612
  36.5 6.9 %collective-permute-start.8 = (f32[2176,128]{1,0:T(8,128)S(1)}, f32[2176,128]{1,0:T(8,128)S(1)}, u32[]{:S(2)}, u32[]{:S(2)}) collective-permute-start(f32[2176,128]{1,0:T(8,128)S(1)} %get-tuple-element.57), channel_id=1, source_target_pairs={{0,1},{1,0},{2,3},{3,2},{4,5},{5,4},{6,7},{7,6},{8,9},{9,8},{10,11... | collective-permute-start | bytes 3342344 | tf_op jit(solution)/shard_map/ppermute | solution.py:473
  44.5 23.5 %all-to-all-start = ((f32[16,136,128]{2,1,0:T(8,128)}), f32[16,136,128]{2,1,0:T(8,128)S(1)}, u32[]{:S(2)}, u32[]{:S(2)}) async-start(f32[16,136,128]{2,1,0:T(8,128)} %bitcast.1), calls=%async_computation | async-start | bytes 2228224 | tf_op jit(solution)/shard_map/all_to_all | solution.py:495
  48.2 19.8 %collective-permute-start.5 = (f32[6,24,128]{2,1,0:T(8,128)S(1)}, f32[6,24,128]{2,1,0:T(8,128)S(1)}, u32[]{:S(2)}, u32[]{:S(2)}) collective-permute-start(f32[6,24,128]{2,1,0:T(8,128)S(1)} %get-tuple-element.49), channel_id=1, source_target_pairs={{0,504},{8,16},{16,8},{24,32},{32,24},{40,48},{48,40},{56,64},{64,... | collective-permute-start | bytes 221192 | tf_op jit(solution)/shard_map/ppermute | solution.py:490
  61.8 6.2 %collective-permute-start.4 = (f32[6,24,128]{2,1,0:T(8,128)S(1)}, f32[6,24,128]{2,1,0:T(8,128)S(1)}, u32[]{:S(2)}, u32[]{:S(2)}) collective-permute-start(f32[6,24,128]{2,1,0:T(8,128)S(1)} %get-tuple-element.48), channel_id=1, source_target_pairs={{0,8},{8,0},{16,24},{24,16},{32,40},{40,32},{48,56},{56,48},{64,72... | collective-permute-start | bytes 221192 | tf_op jit(solution)/shard_map/ppermute | solution.py:491
  68.7 21.1 %all-to-all-start.1 = ((f32[16,1,1152]{2,1,0:T(1,128)}), f32[16,1,1152]{2,1,0:T(1,128)S(1)}, u32[]{:S(2)}, u32[]{:S(2)}) async-start(f32[16,1,1152]{2,1,0:T(1,128)} %shard_map.136), calls=%async_computation.1 | async-start | bytes 147456 | tf_op jit(solution)/shard_map/all_to_all | solution.py:499
  78.0 7.6 %collective-permute-start.7 = (f32[24,128]{1,0:T(8,128)S(1)}, f32[24,128]{1,0:T(8,128)S(1)}, u32[]{:S(2)}, u32[]{:S(2)}) collective-permute-start(f32[24,128]{1,0:T(8,128)S(1)} %get-tuple-element.53), channel_id=1, source_target_pairs={{0,7},{1,2},{2,1},{3,4},{4,3},{5,6},{6,5},{7,0},{8,15},{9,10},{10,... | collective-permute-start | bytes 36872 | tf_op jit(solution)/shard_map/ppermute | solution.py:435
  83.8 3.1 %collective-permute-start.6 = (f32[24,128]{1,0:T(8,128)S(1)}, f32[24,128]{1,0:T(8,128)S(1)}, u32[]{:S(2)}, u32[]{:S(2)}) collective-permute-start(f32[24,128]{1,0:T(8,128)S(1)} %get-tuple-element.52), channel_id=1, source_target_pairs={{0,1},{1,0},{2,3},{3,2},{4,5},{5,4},{6,7},{7,6},{8,9},{9,8},{10,11... | collective-permute-start | bytes 36872 | tf_op jit(solution)/shard_map/ppermute | solution.py:435
  127.0 8.8 %collective-permute-start.9 = (f32[2176,128]{1,0:T(8,128)S(1)}, f32[2176,128]{1,0:T(8,128)S(1)}, u32[]{:S(2)}, u32[]{:S(2)}) collective-permute-start(f32[2176,128]{1,0:T(8,128)S(1)} %bitcast.3), channel_id=1, source_target_pairs={{0,1},{1,0},{2,3},{3,2},{4,5},{5,4},{6,7},{7,6},{8,9},{9,8},{10,11... | collective-permute-start | bytes 3342344 | tf_op jit(solution)/shard_map/ppermute | solution.py:511
